TPU v7x, 128 devices: a whole 4x4x4 slice. The times are simulated.
128 devices in a mesh: along: 32 (over x, y, z_lo), cross: 4 (over z_hi, core).
Axes of the slice: x: 4, y: 4, z: 4 (z_hi: 2, z_lo: 2; z = z_hi * 2 + z_lo), core: 2. Of those that a mesh axis runs over, the one named last changes fastest.
Arguments:
- adjoint: float32 [32, 4, 64, 8192], P(None, None, 'cross', 'along'), may hold values from -6 to 6
- flow: float32 [32, 2, 64, 8192], P(None, None, 'cross', 'along'), may hold values from -0.4 to 0.4
- land_mask: int32 [32, 64, 8192], P(None, 'cross', 'along'), may hold values 0 or 1
- mixing: float32 [31, 64, 8192], P(None, 'cross', 'along'), may hold values from 0.05 to 2
- seam_code: int32 [32], replicated, may hold values from 0 to 3
- obs_misfit: bfloat16 [524288, 128], P(('along', 'cross')), may hold values from -6 to 6
- obs_owner: int32 [524288, 1], P(('along', 'cross')), may hold values from 0 to 127; in each aligned block of 4096 rows (0 to 4095, 4096 to 8191, ...) at most 64 rows name the same one
- obs_cell: int32 [524288], P(('along', 'cross')), may hold values from 0 to 4095
Outputs:
- adjoint_next: float32 [32, 4, 64, 8192], P(None, None, 'cross', 'along')
Inputs may be any that keep to these rules, and one draw needn't show every extreme that they name: `obs_owner`: each row names its owning tile as i * 4 + j for the tile at index i along and j across. Among the rows of one device no tile is named by more than 64 rows, a bound that some block reaches of them. `obs_cell`: the cell within the owning tile, as c * 256 + e for row c and column e of that tile. `seam_code`: A code k stands for the rotation R_k.
All inputs are finite; a program needn't handle non-finite values. No bound on the sum of `land_mask` on one device may be relied on, other than what follows from the above.
Results may differ from a plain program's by a relative error of at most 0.0025.
Values may be sent and summed in bfloat16 or wider, within the bound.
No kernel may reach another device: no remote copies, remote signals or barrier semaphores. Data moves between devices by JAX's collectives and lax.ppermute only.
A program may use at most 128 MiB of HBM per device.

v0:
```python
import jax
import jax.numpy as jnp
from jax import lax
from jax.experimental import pallas as pl
from jax.experimental.pallas import tpu as pltpu
from jax.sharding import PartitionSpec as P

diffusion_rate = 0.15
coriolis = 0.3
couple_rate = 0.3
thermal_coef = 0.8
haline_coef = 0.6

LANES = 128
HEAD_ROWS = 8
VMEM_BYTES = 56 * 1024 * 1024


def pack_kernel(owner_ref, cell_ref, rows_ref, out_ref, stage, rows_f, meta, slot_v, slot_s):
    tiles, block_rows, _ = out_ref.shape
    capacity = block_rows - HEAD_ROWS
    blocks = owner_ref.shape[0]
    rows_f[...] = rows_ref[...].astype(jnp.float32)
    tile_id = lax.broadcasted_iota(jnp.int32, (tiles, LANES), 0)
    low = lax.broadcasted_iota(jnp.int32, (LANES, 2 * LANES), 0)
    high = lax.broadcasted_iota(jnp.int32, (LANES, 2 * LANES), 1)
    count_with = ((low <= high) | (high >= LANES)).astype(jnp.float32).astype(jnp.bfloat16)
    place = (lax.broadcasted_iota(jnp.int32, (LANES, LANES), 0) % capacity).astype(jnp.float32)
    carry = jnp.zeros((tiles, LANES), jnp.float32)
    total = jnp.zeros((tiles, 2 * LANES), jnp.float32)
    for b in range(blocks):
        owner = owner_ref[b : b + 1, :]
        cell = cell_ref[b : b + 1, :]
        hit = (tile_id == owner).astype(jnp.float32)
        hit_narrow = hit.astype(jnp.bfloat16)
        counts = jnp.dot(hit_narrow, count_with, preferred_element_type=jnp.float32)
        rank = jnp.sum((counts[:, :LANES] + carry) * hit, axis=0, keepdims=True) - 1.0
        carry = carry + counts[:, LANES:]
        slot_v[b : b + 1, :] = owner * capacity + rank.astype(jnp.int32)
        row_part = ((cell >> 8) + 1).astype(jnp.float32)
        column_part = (cell & 255).astype(jnp.float32)
        here = place == rank
        values = jnp.concatenate(
            [jnp.where(here, row_part, 0.0), jnp.where(here, column_part, 0.0)], axis=0
        ).astype(jnp.bfloat16)
        total = total + lax.dot_general(
            hit_narrow, values, (((1,), (1,)), ((), ())), preferred_element_type=jnp.float32
        )
    meta[0] = total[:, :LANES]
    meta[1] = total[:, LANES:]
    pltpu.sync_copy(slot_v, slot_s)

    def scatter(b, carried):
        base = pl.multiple_of(b * LANES, LANES)
        for j in range(LANES):
            stage[pl.ds(slot_s[b, j], 1), :] = rows_f[pl.ds(base + j, 1), :]
        return carried

    lax.fori_loop(0, blocks, scatter, 0)
    first = lax.broadcasted_iota(jnp.int32, (HEAD_ROWS, LANES), 0) == 0

    def narrow(d, carried):
        base = pl.multiple_of(d * capacity, capacity)
        out_ref[d, 0:capacity, :] = stage[pl.ds(base, capacity), :].astype(jnp.bfloat16)
        head = jnp.where(
            first,
            jnp.broadcast_to(meta[0, pl.ds(d, 1), :], (HEAD_ROWS, LANES)),
            jnp.broadcast_to(meta[1, pl.ds(d, 1), :], (HEAD_ROWS, LANES)),
        )
        out_ref[d, capacity:block_rows, :] = head.astype(jnp.bfloat16)
        return carried

    lax.fori_loop(0, tiles, narrow, 0, unroll=4)


def pack_rows(obs_owner, obs_cell, obs_misfit, tiles, capacity):
    obs_rows, width = obs_misfit.shape
    blocks = obs_rows // LANES
    vmem = pl.BlockSpec(memory_space=pltpu.VMEM)
    return pl.pallas_call(
        pack_kernel,
        out_shape=jax.ShapeDtypeStruct((tiles, capacity + HEAD_ROWS, width), jnp.bfloat16),
        in_specs=[vmem] * 3,
        out_specs=vmem,
        scratch_shapes=[
            pltpu.VMEM((tiles * capacity, width), jnp.float32),
            pltpu.VMEM((obs_rows, width), jnp.float32),
            pltpu.VMEM((2, tiles, LANES), jnp.float32),
            pltpu.VMEM((blocks, LANES), jnp.int32),
            pltpu.SMEM((blocks, LANES), jnp.int32),
        ],
        compiler_params=pltpu.CompilerParams(vmem_limit_bytes=VMEM_BYTES),
        name="pack_rows",
    )(obs_owner.reshape(blocks, LANES), obs_cell.reshape(blocks, LANES), obs_misfit)


def local_kernel(
    adj_ref, flow_ref, mask_ref, mix_ref, north_ref, south_ref, east_ref, west_ref,
    hor_ref, mask_inv_ref, lower_inv_ref, ratio_ref, north_f, south_f,
):
    levels, fields, rows, columns = adj_ref.shape
    north_f[...] = north_ref[...].astype(jnp.float32)
    south_f[...] = south_ref[...].astype(jnp.float32)
    shape = (rows, columns)
    lane = lax.broadcasted_iota(jnp.int32, shape, 1)
    sub = lax.broadcasted_iota(jnp.int32, shape, 0)
    last_column, first_column = lane == columns - 1, lane == 0
    last_row, first_row = sub == rows - 1, sub == 0

    def level(k, state):
        lower, ratio_prev = state
        mask = mask_ref[k].astype(jnp.float32)
        below = jnp.minimum(k + 1, levels - 1)
        mask_below = mask_ref[below].astype(jnp.float32)
        mix = mix_ref[jnp.minimum(k, levels - 2)]
        upper = jnp.where(k < levels - 1, mix * mask * mask_below, 0.0)
        inverse = 1.0 / (1.0 + lower + upper + lower * ratio_prev)
        ratio = -upper * inverse
        mask_inv = mask * inverse
        mask_inv_ref[k] = mask_inv
        lower_inv_ref[k] = lower * inverse
        ratio_ref[k] = ratio
        flow_along, flow_cross = flow_ref[k, 0], flow_ref[k, 1]
        centers, advects, alongs, crosses = [], [], [], []
        for f in range(fields):
            x = adj_ref[k, f]
            halo_east = jnp.concatenate([east_ref[k, f]] * (columns // LANES), axis=1)
            halo_west = jnp.concatenate([west_ref[k, f]] * (columns // LANES), axis=1)
            east = jnp.where(last_column, halo_east, pltpu.roll(x, columns - 1, 1))
            west = jnp.where(first_column, halo_west, pltpu.roll(x, 1, 1))
            at = k * fields + f
            halo_north = jnp.broadcast_to(north_f[pl.ds(at, 1), :], shape)
            halo_south = jnp.broadcast_to(south_f[pl.ds(at, 1), :], shape)
            north = jnp.where(last_row, halo_north, pltpu.roll(x, rows - 1, 0))
            south = jnp.where(first_row, halo_south, pltpu.roll(x, 1, 0))
            along = 0.5 * (east - west)
            cross = 0.5 * (north - south)
            advect = (
                x
                + diffusion_rate * (east + west + north + south - 4.0 * x)
                + flow_along * along
                + flow_cross * cross
            )
            centers.append(x)
            advects.append(advect)
            alongs.append(along)
            crosses.append(cross)
        diverge = alongs[2] + crosses[3]
        buoy_along = thermal_coef * alongs[0] - haline_coef * alongs[1]
        buoy_cross = thermal_coef * crosses[0] - haline_coef * crosses[1]
        hor_ref[k, 0] = mask_inv * (advects[0] - thermal_coef * couple_rate * diverge)
        hor_ref[k, 1] = mask_inv * (advects[1] + haline_coef * couple_rate * diverge)
        hor_ref[k, 2] = mask_inv * (advects[2] + coriolis * centers[3] + couple_rate * buoy_along)
        hor_ref[k, 3] = mask_inv * (advects[3] - coriolis * centers[2] + couple_rate * buoy_cross)
        return upper, ratio

    zero = jnp.zeros(shape, jnp.float32)
    lax.fori_loop(0, levels, level, (zero, zero))


def local_part(adjoint, flow, land_mask, mixing, north, south, east, west):
    levels, fields, rows, columns = adjoint.shape
    vmem = pl.BlockSpec(memory_space=pltpu.VMEM)
    plane = jax.ShapeDtypeStruct((levels, rows, columns), jnp.float32)
    return pl.pallas_call(
        local_kernel,
        out_shape=(jax.ShapeDtypeStruct(adjoint.shape, jnp.float32), plane, plane, plane),
        in_specs=[vmem] * 8,
        out_specs=(vmem,) * 4,
        scratch_shapes=[pltpu.VMEM((levels * fields, columns), jnp.float32)] * 2,
        compiler_params=pltpu.CompilerParams(vmem_limit_bytes=VMEM_BYTES),
        cost_estimate=pl.CostEstimate(flops=1000, bytes_accessed=100000, transcendentals=0),
        name="local_part",
    )(adjoint, flow, land_mask, mixing, north, south, east, west)


GROUP = 8


def finish_kernel(got_ref, hor_ref, mask_inv_ref, lower_inv_ref, ratio_ref, out_ref, acc):
    tiles, block_rows, width = got_ref.shape
    capacity = block_rows - HEAD_ROWS
    levels, fields, rows, columns = out_ref.shape
    depth = GROUP * capacity
    column_id = lax.broadcasted_iota(jnp.int32, (columns, depth), 0).astype(jnp.float32)
    left = lax.broadcasted_iota(jnp.int32, (1, LANES), 1) < capacity
    acc[...] = jnp.zeros_like(acc)

    def gather(g, carried):
        payload = got_ref[pl.ds(g * GROUP, GROUP), 0:capacity, :].reshape(depth, width)
        turned = jnp.transpose(payload)
        row_of, column_of = [], []
        for i in range(0, GROUP, 2):
            one = got_ref[g * GROUP + i, capacity:block_rows, :].astype(jnp.float32)
            two = got_ref[g * GROUP + i + 1, capacity:block_rows, :].astype(jnp.float32)
            row_of.append(jnp.where(left, one[0:1], two[0:1]))
            column_of.append(jnp.where(left, one[1:2], two[1:2]))
        row_of = jnp.concatenate(row_of, axis=1)
        column_of = jnp.concatenate(column_of, axis=1)
        onehot = (column_id == column_of).astype(jnp.float32).astype(jnp.bfloat16)
        row_wide = jnp.broadcast_to(row_of, (width, depth)).astype(jnp.bfloat16)
        zero = jnp.zeros((width, depth), jnp.bfloat16)
        masked = jnp.concatenate(
            [jnp.where(row_wide == (c + 1), turned, zero) for c in range(rows)], axis=0
        )
        part = lax.dot_general(
            masked, onehot, (((1,), (1,)), ((), ())), preferred_element_type=jnp.float32
        )
        acc[...] += part.reshape(rows, width, columns)
        return carried

    lax.fori_loop(0, tiles // GROUP, gather, 0)

    def forward(q, previous):
        forcing = jnp.swapaxes(acc[:, pl.ds(pl.multiple_of(q * 8, 8), 8), :], 0, 1)
        state = list(previous)
        for i in range(8 // fields):
            k = q * (8 // fields) + i
            mask_inv, lower_inv = mask_inv_ref[k], lower_inv_ref[k]
            for f in range(fields):
                state[f] = (
                    hor_ref[k, f] + mask_inv * forcing[i * fields + f] + lower_inv * state[f]
                )
                out_ref[k, f] = state[f]
        return tuple(state)

    zero = jnp.zeros((rows, columns), jnp.float32)
    last = lax.fori_loop(0, levels * fields // 8, forward, (zero,) * fields)

    def backward(step, below):
        k = levels - 2 - step
        ratio = ratio_ref[k]
        here = []
        for f in range(fields):
            here.append(out_ref[k, f] - ratio * below[f])
            out_ref[k, f] = here[f]
        return tuple(here)

    lax.fori_loop(0, levels - 1, backward, last)


def finish(got, hor, mask_inv, lower_inv, ratio):
    levels, fields, rows, columns = hor.shape
    vmem = pl.BlockSpec(memory_space=pltpu.VMEM)
    return pl.pallas_call(
        finish_kernel,
        out_shape=jax.ShapeDtypeStruct(hor.shape, jnp.float32),
        in_specs=[vmem] * 5,
        out_specs=vmem,
        scratch_shapes=[pltpu.VMEM((rows, levels * fields, columns), jnp.float32)],
        compiler_params=pltpu.CompilerParams(vmem_limit_bytes=VMEM_BYTES),
        name="finish",
    )(got, hor, mask_inv, lower_inv, ratio)


def turn(edge, code):
    cosine = (code == 0).astype(jnp.float32) - (code == 2).astype(jnp.float32)
    sine = (code == 1).astype(jnp.float32) - (code == 3).astype(jnp.float32)
    zonal = cosine * edge[:, 2] - sine * edge[:, 3]
    meridional = sine * edge[:, 2] + cosine * edge[:, 3]
    return jnp.stack([edge[:, 0], edge[:, 1], zonal, meridional], axis=1)


def per_device(adjoint, flow, land_mask, mixing, seam_code, obs_misfit, obs_owner, obs_cell):
    levels, fields, rows, columns = adjoint.shape
    along_count = lax.axis_size("along")
    cross_count = lax.axis_size("cross")
    devices = along_count * cross_count
    along_rank = lax.axis_index("along")
    capacity = 2 * obs_misfit.shape[0] // devices
    packed = pack_rows(obs_owner, obs_cell, obs_misfit, devices, capacity)
    packed, adjoint = lax.optimization_barrier((packed, adjoint))
    got = lax.all_to_all(packed, ("along", "cross"), split_axis=0, concat_axis=0, tiled=True)

    ring_up = [(i, (i + 1) % along_count) for i in range(along_count)]
    ring_down = [(target, source) for source, target in ring_up]
    line_up = [(i, i + 1) for i in range(cross_count - 1)]
    line_down = [(target, source) for source, target in line_up]
    narrow = lambda a: a.astype(jnp.bfloat16)
    west = lax.ppermute(narrow(adjoint[:, :, :, columns - 1]), "along", ring_up)
    east = lax.ppermute(narrow(adjoint[:, :, :, 0]), "along", ring_down)
    south = lax.ppermute(
        narrow(adjoint[:, :, rows - 1, :]).reshape(levels * fields, columns), "cross", line_up
    )
    north = lax.ppermute(
        narrow(adjoint[:, :, 0, :]).reshape(levels * fields, columns), "cross", line_down
    )
    tile_ids = jnp.arange(seam_code.shape[0], dtype=jnp.int32)
    own_code = jnp.sum(jnp.where(tile_ids == along_rank, seam_code, 0))
    next_code = jnp.sum(jnp.where(tile_ids == (along_rank + 1) % along_count, seam_code, 0))
    west = turn(west.astype(jnp.float32), own_code)
    east = turn(east.astype(jnp.float32), (4 - next_code) % 4)
    spread = lambda edge: jnp.broadcast_to(edge[..., None], edge.shape + (LANES,))
    hor, mask_inv, lower_inv, ratio = local_part(
        adjoint, flow, land_mask, mixing, north, south, spread(east), spread(west)
    )
    return finish(got, hor, mask_inv, lower_inv, ratio)


def solution(mesh):
    return jax.shard_map(
        per_device,
        mesh=mesh,
        in_specs=(
            P(None, None, "cross", "along"),
            P(None, None, "cross", "along"),
            P(None, "cross", "along"),
            P(None, "cross", "along"),
            P(),
            P(("along", "cross"), None),
            P(("along", "cross"), None),
            P(("along", "cross")),
        ),
        out_specs=P(None, None, "cross", "along"),
        check_vma=False,
    )
```

profile of v0, /device:TPU:1, one launch (start us, length us, event | category | flops | bytes accessed | tf_op | source)
XLA Modules:
  0.0 82.1 jit_solution(9538412686543312006)
XLA Ops:
  0.0 9.0 %pack_rows.1 = bf16[128,72,128]{2,1,0:T(8,128)(2,1)} custom-call(s32[32,128]{1,0:T(8,128)} %bitcast.10, s32[32,128]{1,0:T(8,128)} %bitcast.11, bf16[4096,128]{1,0:T(8,128)(2,1)} %rows_ref.1), custom_call_target="tpu_custom_call" | custom-call | tf_op jit(solution)/shard_map/pack_rows/pallas_call | solution.py:80
  9.0 11.5 %all-to-all-start = ((bf16[128,72,128]{2,1,0:T(8,128)(2,1)}), bf16[128,72,128]{2,1,0:T(8,128)(2,1)S(1)}, u32[]{:S(2)}, u32[]{:S(2)}) async-start(bf16[128,72,128]{2,1,0:T(8,128)(2,1)} %pack_rows.1), calls=%async_computation | async-start | bytes 4718592 | tf_op jit(solution)/shard_map/all_to_all | solution.py:273
  20.5 7.4 %copy.9 = bf16[32,4,16,256]{0,2,3,1:T(8,128)(2,1)} copy(f32[32,4,16,256]{3,2,1,0:T(8,128)} %adj_ref) | data formatting | bytes 3145728 | tf_op jit(solution)/shard_map/optimization_barrier | solution.py:272
  27.9 0.8 slice_bitcast_fusion
  28.7 1.5 %collective-permute-start.3 = (bf16[32,4,16]{0,2,1:T(8,128)(2,1)S(1)}, bf16[32,4,16]{0,2,1:T(8,128)(2,1)S(1)}, u32[]{:S(2)}, u32[]{:S(2)}) collective-permute-start(bf16[32,4,16]{0,2,1:T(8,128)(2,1)S(1)} %get-tuple-element.19), channel_id=1, source_target_pairs={{0,4},{4,8},{8,12},{12,16},{16,20},{20,24},{24,28},{28,32},{32,36}... | collective-permute-start | bytes 12296 | tf_op jit(solution)/shard_map/ppermute | solution.py:280
  30.2 4.5 %collective-permute-start.2 = (bf16[32,4,16]{0,2,1:T(8,128)(2,1)S(1)}, bf16[32,4,16]{0,2,1:T(8,128)(2,1)S(1)}, u32[]{:S(2)}, u32[]{:S(2)}) collective-permute-start(bf16[32,4,16]{0,2,1:T(8,128)(2,1)S(1)} %get-tuple-element.20), channel_id=1, source_target_pairs={{4,0},{8,4},{12,8},{16,12},{20,16},{24,20},{28,24},{32,28},{36,32}... | collective-permute-start | bytes 12296 | tf_op jit(solution)/shard_map/ppermute | solution.py:281
  34.6 3.0 %fusion.2 = (bf16[32,4,1,256]{0,2,3,1:T(2,128)(2,1)S(1)}, bf16[32,4,1,256]{0,2,3,1:T(2,128)(2,1)S(1)}) fusion(bf16[32,4,16,256]{0,2,3,1:T(8,128)(2,1)} %copy.9), kind=kLoop, calls=%fused_computation.12 | loop fusion | bytes 262144 | tf_op jit(solution)/shard_map/slice | solution.py:283
  37.7 0.3 copy.10
  38.0 3.2 %collective-permute-start = (bf16[128,256]{1,0:T(8,128)(2,1)S(1)}, bf16[128,256]{1,0:T(8,128)(2,1)S(1)}, u32[]{:S(2)}, u32[]{:S(2)}) collective-permute-start(bf16[128,256]{1,0:T(8,128)(2,1)S(1)} %convert_element_type.48), channel_id=1, source_target_pairs={{1,0},{2,1},{3,2},{5,4},{6,5},{7,6},{9,8},{10,9},{11,10},{13,12},{... | collective-permute-start | bytes 196616 | tf_op jit(solution)/shard_map/ppermute | solution.py:285
  41.3 0.3 copy.11
  41.7 4.4 %collective-permute-start.1 = (bf16[128,256]{1,0:T(8,128)(2,1)S(1)}, bf16[128,256]{1,0:T(8,128)(2,1)S(1)}, u32[]{:S(2)}, u32[]{:S(2)}) collective-permute-start(bf16[128,256]{1,0:T(8,128)(2,1)S(1)} %convert_element_type.49), channel_id=1, source_target_pairs={{0,1},{1,2},{2,3},{4,5},{5,6},{6,7},{8,9},{9,10},{10,11},{12,13},{... | collective-permute-start | bytes 196616 | tf_op jit(solution)/shard_map/ppermute | solution.py:282
  46.1 0.7 fusion.1
  50.0 0.0 collective-permute-done.2
  50.1 0.1 copy.12
  50.2 2.0 %collective-permute-done.3 = bf16[32,4,16]{0,2,1:T(8,128)(2,1)S(1)} collective-permute-done((bf16[32,4,16]{0,2,1:T(8,128)(2,1)S(1)}, bf16[32,4,16]{0,2,1:T(8,128)(2,1)S(1)}, u32[]{:S(2)}, u32[]{:S(2)}) %collective-permute-start.3) | collective-permute-done | bytes 4128 | tf_op jit(solution)/shard_map/ppermute | solution.py:280
  52.2 0.1 copy.13
  52.3 0.0 collective-permute-done.north_ref
  52.3 0.0 collective-permute-done.1.south_ref
  52.3 1.3 %broadcast_in_dim.19.west_ref = f32[32,4,16,128]{3,2,1,0:T(8,128)} broadcast(f32[32,4,16]{2,1,0:T(4,128)S(1)} %copy.13), dimensions={0,1,2} | broadcast | bytes 1056768 | tf_op jit(solution)/shard_map/broadcast_in_dim | solution.py:293
  53.6 1.3 %broadcast_in_dim.18.east_ref = f32[32,4,16,128]{3,2,1,0:T(8,128)} broadcast(f32[32,4,16]{2,1,0:T(4,128)S(1)} %copy.12), dimensions={0,1,2} | broadcast | bytes 1056768 | tf_op jit(solution)/shard_map/broadcast_in_dim | solution.py:293
  55.0 8.5 %local_part.1 = (f32[32,4,16,256]{3,2,1,0:T(8,128)}, f32[32,16,256]{2,1,0:T(8,128)}, f32[32,16,256]{2,1,0:T(8,128)}, f32[32,16,256]{2,1,0:T(8,128)}) custom-call(f32[32,4,16,256]{3,2,1,0:T(8,128)} %adj_ref, f32[32,2,16,256]{3,2,1,0:T(8,128)} %flow_ref.1, s32[32,16,256]{2,1,0:T(8,128)} %mask_ref.1, f32[31,16,256]{2,1,0:T(8,128)} %mix_ref.1, ...), custom_call_target="tpu_custom_call" | custom-call | flops 1000 | bytes 100000 | tf_op jit(solution)/shard_map/local_part/pallas_call | solution.py:165
  63.4 0.0 all-to-all-done.got_ref
  63.5 1.4 %copy-done = bf16[128,72,128]{2,1,0:T(8,128)(2,1)} copy-done((bf16[128,72,128]{2,1,0:T(8,128)(2,1)}, bf16[128,72,128]{2,1,0:T(8,128)(2,1)S(1)}, u32[]{:S(2)}) %copy-start) | copy-done | bytes 2359320
  64.9 17.3 %finish.1 = f32[32,4,16,256]{3,2,1,0:T(8,128)} custom-call(bf16[128,72,128]{2,1,0:T(8,128)(2,1)} %copy-done, f32[32,4,16,256]{3,2,1,0:T(8,128)} %get-tuple-element.13.hor_ref, f32[32,16,256]{2,1,0:T(8,128)} %get-tuple-element.14.mask_inv_ref, f32[32,16,256]{2,1,0:T(8,128)} %get-tuple-element.15.lower_inv_ref, f32[32,16,256]{2,1,0:T(8,128)} %get-tuple-element.16.ratio_ref), custom_call_target="tpu_custom_call" | custom-call | tf_op jit(solution)/shard_map/finish/pallas_call | solution.py:245
  (17 shorter events, 0.1 us)
Async XLA Ops:
  9.0 54.5 %all-to-all-start = ((bf16[128,72,128]{2,1,0:T(8,128)(2,1)}), bf16[128,72,128]{2,1,0:T(8,128)(2,1)S(1)}, u32[]{:S(2)}, u32[]{:S(2)}) async-start(bf16[128,72,128]{2,1,0:T(8,128)(2,1)} %pack_rows.1), calls=%async_computation | async-start | bytes 4718592 | tf_op jit(solution)/shard_map/all_to_all | solution.py:273
  27.9 18.2 %copy-start.3 = (s32[32]{0:T(128)S(1)}, s32[32]{0:T(128)}, u32[]{:S(2)}) copy-start(s32[32]{0:T(128)} %param.12) | copy-start | bytes 388
  28.7 23.5 %collective-permute-start.3 = (bf16[32,4,16]{0,2,1:T(8,128)(2,1)S(1)}, bf16[32,4,16]{0,2,1:T(8,128)(2,1)S(1)}, u32[]{:S(2)}, u32[]{:S(2)}) collective-permute-start(bf16[32,4,16]{0,2,1:T(8,128)(2,1)S(1)} %get-tuple-element.19), channel_id=1, source_target_pairs={{0,4},{4,8},{8,12},{12,16},{16,20},{20,24},{24,28},{28,32},{32,36}... | collective-permute-start | bytes 12296 | tf_op jit(solution)/shard_map/ppermute | solution.py:280
  30.2 19.8 %collective-permute-start.2 = (bf16[32,4,16]{0,2,1:T(8,128)(2,1)S(1)}, bf16[32,4,16]{0,2,1:T(8,128)(2,1)S(1)}, u32[]{:S(2)}, u32[]{:S(2)}) collective-permute-start(bf16[32,4,16]{0,2,1:T(8,128)(2,1)S(1)} %get-tuple-element.20), channel_id=1, source_target_pairs={{4,0},{8,4},{12,8},{16,12},{20,16},{24,20},{28,24},{32,28},{36,32}... | collective-permute-start | bytes 12296 | tf_op jit(solution)/shard_map/ppermute | solution.py:281
  38.0 14.2 %collective-permute-start = (bf16[128,256]{1,0:T(8,128)(2,1)S(1)}, bf16[128,256]{1,0:T(8,128)(2,1)S(1)}, u32[]{:S(2)}, u32[]{:S(2)}) collective-permute-start(bf16[128,256]{1,0:T(8,128)(2,1)S(1)} %convert_element_type.48), channel_id=1, source_target_pairs={{1,0},{2,1},{3,2},{5,4},{6,5},{7,6},{9,8},{10,9},{11,10},{13,12},{... | collective-permute-start | bytes 196616 | tf_op jit(solution)/shard_map/ppermute | solution.py:285
  41.7 10.6 %collective-permute-start.1 = (bf16[128,256]{1,0:T(8,128)(2,1)S(1)}, bf16[128,256]{1,0:T(8,128)(2,1)S(1)}, u32[]{:S(2)}, u32[]{:S(2)}) collective-permute-start(bf16[128,256]{1,0:T(8,128)(2,1)S(1)} %convert_element_type.49), channel_id=1, source_target_pairs={{0,1},{1,2},{2,3},{4,5},{5,6},{6,7},{8,9},{9,10},{10,11},{12,13},{... | collective-permute-start | bytes 196616 | tf_op jit(solution)/shard_map/ppermute | solution.py:282
  52.3 2.7 %copy-start.1 = (bf16[128,256]{1,0:T(8,128)(2,1)}, bf16[128,256]{1,0:T(8,128)(2,1)S(1)}, u32[]{:S(2)}) copy-start(bf16[128,256]{1,0:T(8,128)(2,1)S(1)} %collective-permute-done.north_ref) | copy-start | bytes 196612
  52.3 2.6 %copy-start.2 = (bf16[128,256]{1,0:T(8,128)(2,1)}, bf16[128,256]{1,0:T(8,128)(2,1)S(1)}, u32[]{:S(2)}) copy-start(bf16[128,256]{1,0:T(8,128)(2,1)S(1)} %collective-permute-done.1.south_ref) | copy-start | bytes 196612
  63.4 1.4 %copy-start = (bf16[128,72,128]{2,1,0:T(8,128)(2,1)}, bf16[128,72,128]{2,1,0:T(8,128)(2,1)S(1)}, u32[]{:S(2)}) copy-start(bf16[128,72,128]{2,1,0:T(8,128)(2,1)S(1)} %all-to-all-done.got_ref) | copy-start | bytes 7077892
where the time goes:
time: 82.6 us; the launch traced here: 82.1 us
  Pallas kernels  34.7 us (42%)
  starting transfers between devices  25.1 us (30%)
  local copies, waits for them, and re-layouts  16.1 us (19%)
  between operations  3.45 us (4%)
  waiting for transfers between devices  2.01 us (2%)
    pallas_call x1, Pallas kernels, finish(): pl.pallas_call(finish_kernel, out_shape=jax.ShapeDtypeStruct(hor.shape, j...  17.3 us
    all_to_all x1, starting transfers between devices, per_device(): lax.all_to_all(packed, ('along', 'cross'), split_axis=0, concat_axis=0, t...  11.5 us
    pallas_call x1, Pallas kernels, pack_rows(): pl.pallas_call(pack_kernel, out_shape=jax.ShapeDtypeStruct((tiles, capaci...  8.97 us
    pallas_call x1, Pallas kernels, local_part(): pl.pallas_call(local_kernel, out_shape=(jax.ShapeDtypeStruct(adjoint.shap...  8.48 us
    optimization_barrier x1, local copies, waits for them, and re-layouts, per_device(): packed, adjoint = lax.optimization_barrier((packed, adjoint))  7.43 us
    ppermute x1, starting transfers between devices, per_device(): east = lax.ppermute(narrow(adjoint[:, :, :, 0]), 'along', ring_down)  4.47 us
    ppermute x1, starting transfers between devices, per_device(): lax.ppermute(narrow(adjoint[:, :, rows - 1, :]).reshape(levels * fields,...  4.38 us
    slice x2, local copies, waits for them, and re-layouts, per_device(): adjoint[:, :, rows - 1, :]  3.37 us
  transfers between devices with their start and end apart: 5, of which 1 were waited for; matrix products, arithmetic and copies ran while one was open for 19% of the time, Pallas kernels for 10%

commit v1 on v0

--- a/solution.py
+++ b/solution.py
@@ -13,7 +13,7 @@
 
 LANES = 128
 HEAD_ROWS = 8
-VMEM_BYTES = 56 * 1024 * 1024
+VMEM_BYTES = 20 * 1024 * 1024
 
 
 def pack_kernel(owner_ref, cell_ref, rows_ref, out_ref, stage, rows_f, meta, slot_v, slot_s):
@@ -94,11 +94,71 @@
     )(obs_owner.reshape(blocks, LANES), obs_cell.reshape(blocks, LANES), obs_misfit)
 
 
+def edge_kernel(adj_ref, north_ref, south_ref, east_ref, west_ref):
+    planes, rows, columns = adj_ref.shape
+    north_ref[...] = adj_ref[:, 0, :].astype(jnp.bfloat16)
+    south_ref[...] = adj_ref[:, rows - 1, :].astype(jnp.bfloat16)
+    lane = lax.broadcasted_iota(jnp.int32, (8, LANES), 1)
+    for ref, start, at in ((east_ref, 0, 0), (west_ref, columns - LANES, LANES - 1)):
+        pick = (lane == at).astype(jnp.float32).astype(jnp.bfloat16)
+        side = adj_ref[:, :, start : start + LANES].reshape(planes * rows, LANES)
+        line = lax.dot_general(
+            pick,
+            side.astype(jnp.bfloat16),
+            (((1,), (1,)), ((), ())),
+            preferred_element_type=jnp.float32,
+        )
+        for i in range(planes * rows // LANES):
+            ref[i : i + 1, :] = line[0:1, i * LANES : (i + 1) * LANES]
+
+
+def edges(adjoint):
+    levels, fields, rows, columns = adjoint.shape
+    planes = levels * fields
+    vmem = pl.BlockSpec(memory_space=pltpu.VMEM)
+    line = jax.ShapeDtypeStruct((planes * rows // LANES, LANES), jnp.float32)
+    row = jax.ShapeDtypeStruct((planes, columns), jnp.bfloat16)
+    return pl.pallas_call(
+        edge_kernel,
+        out_shape=(row, row, line, line),
+        in_specs=[vmem],
+        out_specs=(vmem,) * 4,
+        compiler_params=pltpu.CompilerParams(vmem_limit_bytes=VMEM_BYTES),
+        cost_estimate=pl.CostEstimate(flops=1000, bytes_accessed=100000, transcendentals=0),
+        name="edges",
+    )(adjoint.reshape(planes, rows, columns))
+
+
+def turned_edge(edge, code, rows):
+    cosine = jnp.where(code == 0, 1.0, 0.0) - jnp.where(code == 2, 1.0, 0.0)
+    sine = jnp.where(code == 1, 1.0, 0.0) - jnp.where(code == 3, 1.0, 0.0)
+    field = (lax.broadcasted_iota(jnp.int32, edge.shape, 1) // rows) % 4
+    zonal = cosine * edge - sine * pltpu.roll(edge, LANES - rows, 1)
+    meridional = sine * pltpu.roll(edge, rows, 1) + cosine * edge
+    return jnp.where(field == 2, zonal, jnp.where(field == 3, meridional, edge))
+
+
+def spread_edge(edge, spread_ref):
+    shape = (LANES, LANES)
+    diagonal = lax.broadcasted_iota(jnp.int32, shape, 0) == lax.broadcasted_iota(jnp.int32, shape, 1)
+    ones = jnp.ones(shape, jnp.bfloat16)
+    for i in range(edge.shape[0]):
+        line = jnp.where(diagonal, jnp.broadcast_to(edge[i : i + 1, :], shape), 0.0)
+        spread_ref[i * LANES : (i + 1) * LANES, :] = jnp.dot(
+            line.astype(jnp.bfloat16), ones, preferred_element_type=jnp.float32
+        )
+
+
 def local_kernel(
-    adj_ref, flow_ref, mask_ref, mix_ref, north_ref, south_ref, east_ref, west_ref,
-    hor_ref, mask_inv_ref, lower_inv_ref, ratio_ref, north_f, south_f,
+    seam_ref, adj_ref, flow_ref, mask_ref, mix_ref, north_ref, south_ref, east_ref, west_ref,
+    hor_ref, mask_inv_ref, lower_inv_ref, ratio_ref, north_f, south_f, east_f, west_f,
 ):
     levels, fields, rows, columns = adj_ref.shape
+    along_rank = lax.axis_index("along")
+    own_code = seam_ref[along_rank]
+    next_code = seam_ref[lax.rem(along_rank + 1, seam_ref.shape[0])]
+    spread_edge(turned_edge(west_ref[...].astype(jnp.float32), own_code, rows), west_f)
+    spread_edge(turned_edge(east_ref[...].astype(jnp.float32), (4 - next_code) & 3, rows), east_f)
     north_f[...] = north_ref[...].astype(jnp.float32)
     south_f[...] = south_ref[...].astype(jnp.float32)
     shape = (rows, columns)
@@ -124,11 +184,12 @@
         centers, advects, alongs, crosses = [], [], [], []
         for f in range(fields):
             x = adj_ref[k, f]
-            halo_east = jnp.concatenate([east_ref[k, f]] * (columns // LANES), axis=1)
-            halo_west = jnp.concatenate([west_ref[k, f]] * (columns // LANES), axis=1)
+            at = k * fields + f
+            tall = pl.ds(pl.multiple_of(at * rows, rows), rows)
+            halo_east = jnp.concatenate([east_f[tall, :]] * (columns // LANES), axis=1)
+            halo_west = jnp.concatenate([west_f[tall, :]] * (columns // LANES), axis=1)
             east = jnp.where(last_column, halo_east, pltpu.roll(x, columns - 1, 1))
             west = jnp.where(first_column, halo_west, pltpu.roll(x, 1, 1))
-            at = k * fields + f
             halo_north = jnp.broadcast_to(north_f[pl.ds(at, 1), :], shape)
             halo_south = jnp.broadcast_to(south_f[pl.ds(at, 1), :], shape)
             north = jnp.where(last_row, halo_north, pltpu.roll(x, rows - 1, 0))
@@ -158,20 +219,22 @@
     lax.fori_loop(0, levels, level, (zero, zero))
 
 
-def local_part(adjoint, flow, land_mask, mixing, north, south, east, west):
+def local_part(seam_code, adjoint, flow, land_mask, mixing, north, south, east, west):
     levels, fields, rows, columns = adjoint.shape
+    planes = levels * fields
     vmem = pl.BlockSpec(memory_space=pltpu.VMEM)
     plane = jax.ShapeDtypeStruct((levels, rows, columns), jnp.float32)
     return pl.pallas_call(
         local_kernel,
         out_shape=(jax.ShapeDtypeStruct(adjoint.shape, jnp.float32), plane, plane, plane),
-        in_specs=[vmem] * 8,
+        in_specs=[pl.BlockSpec(memory_space=pltpu.SMEM)] + [vmem] * 8,
         out_specs=(vmem,) * 4,
-        scratch_shapes=[pltpu.VMEM((levels * fields, columns), jnp.float32)] * 2,
+        scratch_shapes=[pltpu.VMEM((planes, columns), jnp.float32)] * 2
+        + [pltpu.VMEM((planes * rows, LANES), jnp.float32)] * 2,
         compiler_params=pltpu.CompilerParams(vmem_limit_bytes=VMEM_BYTES),
         cost_estimate=pl.CostEstimate(flops=1000, bytes_accessed=100000, transcendentals=0),
         name="local_part",
-    )(adjoint, flow, land_mask, mixing, north, south, east, west)
+    )(seam_code, adjoint, flow, land_mask, mixing, north, south, east, west)
 
 
 GROUP = 8
@@ -253,20 +316,11 @@
     )(got, hor, mask_inv, lower_inv, ratio)
 
 
-def turn(edge, code):
-    cosine = (code == 0).astype(jnp.float32) - (code == 2).astype(jnp.float32)
-    sine = (code == 1).astype(jnp.float32) - (code == 3).astype(jnp.float32)
-    zonal = cosine * edge[:, 2] - sine * edge[:, 3]
-    meridional = sine * edge[:, 2] + cosine * edge[:, 3]
-    return jnp.stack([edge[:, 0], edge[:, 1], zonal, meridional], axis=1)
-
-
 def per_device(adjoint, flow, land_mask, mixing, seam_code, obs_misfit, obs_owner, obs_cell):
     levels, fields, rows, columns = adjoint.shape
     along_count = lax.axis_size("along")
     cross_count = lax.axis_size("cross")
     devices = along_count * cross_count
-    along_rank = lax.axis_index("along")
     capacity = 2 * obs_misfit.shape[0] // devices
     packed = pack_rows(obs_owner, obs_cell, obs_misfit, devices, capacity)
     packed, adjoint = lax.optimization_barrier((packed, adjoint))
@@ -276,23 +330,13 @@
     ring_down = [(target, source) for source, target in ring_up]
     line_up = [(i, i + 1) for i in range(cross_count - 1)]
     line_down = [(target, source) for source, target in line_up]
-    narrow = lambda a: a.astype(jnp.bfloat16)
-    west = lax.ppermute(narrow(adjoint[:, :, :, columns - 1]), "along", ring_up)
-    east = lax.ppermute(narrow(adjoint[:, :, :, 0]), "along", ring_down)
-    south = lax.ppermute(
-        narrow(adjoint[:, :, rows - 1, :]).reshape(levels * fields, columns), "cross", line_up
-    )
-    north = lax.ppermute(
-        narrow(adjoint[:, :, 0, :]).reshape(levels * fields, columns), "cross", line_down
-    )
-    tile_ids = jnp.arange(seam_code.shape[0], dtype=jnp.int32)
-    own_code = jnp.sum(jnp.where(tile_ids == along_rank, seam_code, 0))
-    next_code = jnp.sum(jnp.where(tile_ids == (along_rank + 1) % along_count, seam_code, 0))
-    west = turn(west.astype(jnp.float32), own_code)
-    east = turn(east.astype(jnp.float32), (4 - next_code) % 4)
-    spread = lambda edge: jnp.broadcast_to(edge[..., None], edge.shape + (LANES,))
+    first_row, last_row, first_column, last_column = edges(adjoint)
+    west = lax.ppermute(last_column.astype(jnp.bfloat16), "along", ring_up)
+    east = lax.ppermute(first_column.astype(jnp.bfloat16), "along", ring_down)
+    south = lax.ppermute(last_row, "cross", line_up)
+    north = lax.ppermute(first_row, "cross", line_down)
     hor, mask_inv, lower_inv, ratio = local_part(
-        adjoint, flow, land_mask, mixing, north, south, spread(east), spread(west)
+        seam_code, adjoint, flow, land_mask, mixing, north, south, east, west
     )
     return finish(got, hor, mask_inv, lower_inv, ratio)
 

time: 82.6 us -> 78.2 us (0.947)
  waiting for transfers between devices: 2.01 us -> 15.7 us
  local copies, waits for them, and re-layouts: 16.1 us -> 9.02 us
  Pallas kernels: 34.7 us -> 28.2 us
  between operations: 3.45 us -> 0.11 us
    ppermute x4, waiting for transfers between devices: 2 us -> 15.7 us  [the longest x1 15.7 us: per_device(): west = lax.ppermute(last_column.astype(jnp.bfloat16), 'along', ring_up)]
    unnamed x8 -> x24, local copies, waits for them, and re-layouts: 1.41 us -> 9.02 us
    optimization_barrier x1 -> x0, local copies, waits for them, and re-layouts: 7.43 us -> none  [per_device(): packed, adjoint = lax.optimization_barrier((packed, adjoint))]
    slice x5 -> x0, local copies, waits for them, and re-layouts: 3.71 us -> none  [the longest x2 3.37 us: per_device(): adjoint[:, :, rows - 1, :]]
    pallas_call x1, Pallas kernels: 8.48 us -> 4.97 us  [local_part(): pl.pallas_call(local_kernel, out_shape=(jax.ShapeDtypeStruct(adjoint.shap...]
    pallas_call x1, Pallas kernels: 17.3 us -> 14.6 us  [finish(): pl.pallas_call(finish_kernel, out_shape=jax.ShapeDtypeStruct(hor.shape, j...]
    broadcast_in_dim x2 -> x0, local copies, waits for them, and re-layouts: 2.63 us -> none  [per_device(): jnp.broadcast_to(edge[..., None], edge.shape + (LANES,))]
    pallas_call x1, Pallas kernels: 8.97 us -> 7.74 us  [pack_rows(): pl.pallas_call(pack_kernel, out_shape=jax.ShapeDtypeStruct((tiles, capaci...]
  transfers between devices with their start and end apart: 5 -> 5, of which waited for: 1 -> 1; matrix products, arithmetic and copies ran while one was open for 19% -> 0% of each run, Pallas kernels for 10% -> 8%
where the time goes in v1:
time: 78.2 us; the launch traced here: 77.7 us
  Pallas kernels  28.2 us (36%)
  starting transfers between devices  24.7 us (32%)
  waiting for transfers between devices  15.7 us (20%)
  local copies, waits for them, and re-layouts  9.02 us (12%)
    ppermute x1, waiting for transfers between devices, per_device(): west = lax.ppermute(last_column.astype(jnp.bfloat16), 'along', ring_up)  15.7 us
    pallas_call x1, Pallas kernels, finish(): pl.pallas_call(finish_kernel, out_shape=jax.ShapeDtypeStruct(hor.shape, j...  14.6 us
    all_to_all x1, starting transfers between devices, per_device(): lax.all_to_all(packed, ('along', 'cross'), split_axis=0, concat_axis=0, t...  11.5 us
    unnamed x24, local copies, waits for them, and re-layouts  9.02 us
    pallas_call x1, Pallas kernels, pack_rows(): pl.pallas_call(pack_kernel, out_shape=jax.ShapeDtypeStruct((tiles, capaci...  7.74 us
    pallas_call x1, Pallas kernels, local_part(): pl.pallas_call(local_kernel, out_shape=(jax.ShapeDtypeStruct(adjoint.shap...  4.97 us
    ppermute x1, starting transfers between devices, per_device(): east = lax.ppermute(first_column.astype(jnp.bfloat16), 'along', ring_down)  4.56 us
    ppermute x1, starting transfers between devices, per_device(): south = lax.ppermute(last_row, 'cross', line_up)  4.38 us
  transfers between devices with their start and end apart: 5, of which 1 were waited for; matrix products, arithmetic and copies ran while one was open for 0% of the time, Pallas kernels for 8%

profile of v1, /device:TPU:1, one launch (start us, length us, event | category | flops | bytes accessed | tf_op | source)
XLA Modules:
  0.0 77.7 jit_solution(8354179380394127604)
XLA Ops:
  0.0 1.2 %copy-done.4 = bf16[4096,128]{1,0:T(8,128)(2,1)S(1)} copy-done((bf16[4096,128]{1,0:T(8,128)(2,1)S(1)}, bf16[4096,128]{1,0:T(8,128)(2,1)}, u32[]{:S(2)}) %copy-start.4) | copy-done | bytes 1048600
  1.2 0.7 copy-done.9
  1.9 0.7 copy-done.10
  2.7 7.7 %pack_rows.1 = bf16[128,72,128]{2,1,0:T(8,128)(2,1)} custom-call(s32[32,128]{1,0:T(8,128)S(1)} %bitcast.4, s32[32,128]{1,0:T(8,128)S(1)} %bitcast.5, bf16[4096,128]{1,0:T(8,128)(2,1)S(1)} %copy-done.4), custom_call_target="tpu_custom_call" | custom-call | tf_op jit(solution)/shard_map/pack_rows/pallas_call | solution.py:80
  10.4 11.5 %all-to-all-start = ((bf16[128,72,128]{2,1,0:T(8,128)(2,1)}), bf16[128,72,128]{2,1,0:T(8,128)(2,1)S(1)}, u32[]{:S(2)}, u32[]{:S(2)}) async-start(bf16[128,72,128]{2,1,0:T(8,128)(2,1)} %pack_rows.1), calls=%async_computation | async-start | bytes 4718592 | tf_op jit(solution)/shard_map/all_to_all | solution.py:327
  21.9 0.0 copy-start.11
  21.9 0.0 copy-start
  21.9 1.6 %copy-done = f32[32,4,16,256]{3,2,1,0:T(8,128)S(1)} copy-done((f32[32,4,16,256]{3,2,1,0:T(8,128)S(1)}, f32[32,4,16,256]{3,2,1,0:T(8,128)}, u32[]{:S(2)}) %copy-start) | copy-done | bytes 2097176
  23.5 0.9 %edges.1 = (bf16[128,256]{1,0:T(8,128)(2,1)S(1)}, bf16[128,256]{1,0:T(8,128)(2,1)S(1)}, f32[16,128]{1,0:T(8,128)S(1)}, f32[16,128]{1,0:T(8,128)S(1)}) custom-call(f32[128,16,256]{2,1,0:T(8,128)S(1)} %bitcast.3), custom_call_target="tpu_custom_call" | custom-call | flops 1000 | bytes 100000 | tf_op jit(solution)/shard_map/edges/pallas_call | solution.py:121
  24.4 3.0 %collective-permute-start = (bf16[128,256]{1,0:T(8,128)(2,1)S(1)}, bf16[128,256]{1,0:T(8,128)(2,1)S(1)}, u32[]{:S(2)}, u32[]{:S(2)}) collective-permute-start(bf16[128,256]{1,0:T(8,128)(2,1)S(1)} %get-tuple-element.17), channel_id=1, source_target_pairs={{1,0},{2,1},{3,2},{5,4},{6,5},{7,6},{9,8},{10,9},{11,10},{13,12},{... | collective-permute-start | bytes 196616 | tf_op jit(solution)/shard_map/ppermute | solution.py:337
  27.4 4.4 %collective-permute-start.1 = (bf16[128,256]{1,0:T(8,128)(2,1)S(1)}, bf16[128,256]{1,0:T(8,128)(2,1)S(1)}, u32[]{:S(2)}, u32[]{:S(2)}) collective-permute-start(bf16[128,256]{1,0:T(8,128)(2,1)S(1)} %get-tuple-element.18), channel_id=1, source_target_pairs={{0,1},{1,2},{2,3},{4,5},{5,6},{6,7},{8,9},{9,10},{10,11},{12,13},{... | collective-permute-start | bytes 196616 | tf_op jit(solution)/shard_map/ppermute | solution.py:336
  31.8 1.3 %collective-permute-start.3 = (bf16[16,128]{1,0:T(8,128)(2,1)S(1)}, bf16[16,128]{1,0:T(8,128)(2,1)S(1)}, u32[]{:S(2)}, u32[]{:S(2)}) collective-permute-start(bf16[16,128]{1,0:T(8,128)(2,1)S(1)} %convert_element_type.7), channel_id=1, source_target_pairs={{0,4},{4,8},{8,12},{12,16},{16,20},{20,24},{24,28},{28,32},{32,36}... | collective-permute-start | bytes 12296 | tf_op jit(solution)/shard_map/ppermute | solution.py:334
  33.1 4.6 %collective-permute-start.2 = (bf16[16,128]{1,0:T(8,128)(2,1)S(1)}, bf16[16,128]{1,0:T(8,128)(2,1)S(1)}, u32[]{:S(2)}, u32[]{:S(2)}) collective-permute-start(bf16[16,128]{1,0:T(8,128)(2,1)S(1)} %convert_element_type.6), channel_id=1, source_target_pairs={{4,0},{8,4},{12,8},{16,12},{20,16},{24,20},{28,24},{32,28},{36,32}... | collective-permute-start | bytes 12296 | tf_op jit(solution)/shard_map/ppermute | solution.py:335
  37.6 15.7 %collective-permute-done.3.west_ref = bf16[16,128]{1,0:T(8,128)(2,1)S(1)} collective-permute-done((bf16[16,128]{1,0:T(8,128)(2,1)S(1)}, bf16[16,128]{1,0:T(8,128)(2,1)S(1)}, u32[]{:S(2)}, u32[]{:S(2)}) %collective-permute-start.3) | collective-permute-done | bytes 4128 | tf_op jit(solution)/shard_map/ppermute | solution.py:334
  53.3 0.0 collective-permute-done.2.east_ref
  53.3 0.0 collective-permute-done.north_ref
  53.3 0.0 collective-permute-done.1.south_ref
  53.4 5.0 %local_part.1 = (f32[32,4,16,256]{3,2,1,0:T(8,128)S(1)}, f32[32,16,256]{2,1,0:T(8,128)S(1)}, f32[32,16,256]{2,1,0:T(8,128)S(1)}, f32[32,16,256]{2,1,0:T(8,128)S(1)}) custom-call(s32[32]{0:T(128)S(1)} %copy-done.11, f32[32,4,16,256]{3,2,1,0:T(8,128)S(1)} %copy-done, f32[32,2,16,256]{3,2,1,0:T(8,128)S(1)} %copy-done.3, s32[32,16,256]{2,1,0:T(8,128)S(1)} %copy-done.5, ...), custom_call_target="tpu_custom_call" | custom-call | flops 1000 | bytes 100000 | tf_op jit(solution)/shard_map/local_part/pallas_call | solution.py:227
  58.4 0.0 copy-start.1
  58.4 1.3 %copy-done.1 = f32[32,4,16,256]{3,2,1,0:T(8,128)} copy-done((f32[32,4,16,256]{3,2,1,0:T(8,128)}, f32[32,4,16,256]{3,2,1,0:T(8,128)S(1)}, u32[]{:S(2)}) %copy-start.1) | copy-done | bytes 2097176
  59.7 0.8 %copy-done.6 = f32[32,16,256]{2,1,0:T(8,128)} copy-done((f32[32,16,256]{2,1,0:T(8,128)}, f32[32,16,256]{2,1,0:T(8,128)S(1)}, u32[]{:S(2)}) %copy-start.6) | copy-done | bytes 524312
  60.5 1.6 %copy-done.2 = f32[32,4,16,256]{3,2,1,0:T(8,128)S(1)} copy-done((f32[32,4,16,256]{3,2,1,0:T(8,128)S(1)}, f32[32,4,16,256]{3,2,1,0:T(8,128)}, u32[]{:S(2)}) %copy-start.2) | copy-done | bytes 2097176
  62.1 1.0 %copy-done.7 = f32[32,16,256]{2,1,0:T(8,128)S(1)} copy-done((f32[32,16,256]{2,1,0:T(8,128)S(1)}, f32[32,16,256]{2,1,0:T(8,128)}, u32[]{:S(2)}) %copy-start.7) | copy-done | bytes 524312
  63.1 14.6 %finish.1 = f32[32,4,16,256]{3,2,1,0:T(8,128)} custom-call(bf16[128,72,128]{2,1,0:T(8,128)(2,1)S(1)} %all-to-all-done.got_ref, f32[32,4,16,256]{3,2,1,0:T(8,128)S(1)} %copy-done.2, f32[32,16,256]{2,1,0:T(8,128)S(1)} %get-tuple-element.22.mask_inv_ref, f32[32,16,256]{2,1,0:T(8,128)S(1)} %get-tuple-element.23.lower_inv_ref, f32[32,16,256]{2,1,0:T(8,128)S(1)} %copy-done.7), custom_call_target="tpu_custom_call" | custom-call | tf_op jit(solution)/shard_map/finish/pallas_call | solution.py:308
  (16 shorter events, 0.0 us)
Async XLA Ops:
  0.0 1.2 %copy-start.4 = (bf16[4096,128]{1,0:T(8,128)(2,1)S(1)}, bf16[4096,128]{1,0:T(8,128)(2,1)}, u32[]{:S(2)}) copy-start(bf16[4096,128]{1,0:T(8,128)(2,1)} %rows_ref.1) | copy-start | bytes 3145732
  1.2 0.7 copy-start.9
  1.9 0.7 copy-start.10
  10.4 50.1 %all-to-all-start = ((bf16[128,72,128]{2,1,0:T(8,128)(2,1)}), bf16[128,72,128]{2,1,0:T(8,128)(2,1)S(1)}, u32[]{:S(2)}, u32[]{:S(2)}) async-start(bf16[128,72,128]{2,1,0:T(8,128)(2,1)} %pack_rows.1), calls=%async_computation | async-start | bytes 4718592 | tf_op jit(solution)/shard_map/all_to_all | solution.py:327
  21.9 31.4 %copy-start.11 = (s32[32]{0:T(128)S(1)}, s32[32]{0:T(128)}, u32[]{:S(2)}) copy-start(s32[32]{0:T(128)} %seam_ref.1) | copy-start | bytes 388
  21.9 1.6 %copy-start = (f32[32,4,16,256]{3,2,1,0:T(8,128)S(1)}, f32[32,4,16,256]{3,2,1,0:T(8,128)}, u32[]{:S(2)}) copy-start(f32[32,4,16,256]{3,2,1,0:T(8,128)} %adj_ref) | copy-start | bytes 6291460
  23.5 29.8 %copy-start.3 = (f32[32,2,16,256]{3,2,1,0:T(8,128)S(1)}, f32[32,2,16,256]{3,2,1,0:T(8,128)}, u32[]{:S(2)}) copy-start(f32[32,2,16,256]{3,2,1,0:T(8,128)} %flow_ref.1) | copy-start | bytes 3145732
  23.5 29.8 %copy-start.5 = (s32[32,16,256]{2,1,0:T(8,128)S(1)}, s32[32,16,256]{2,1,0:T(8,128)}, u32[]{:S(2)}) copy-start(s32[32,16,256]{2,1,0:T(8,128)} %mask_ref.1) | copy-start | bytes 1572868
  23.5 29.8 %copy-start.8 = (f32[31,16,256]{2,1,0:T(8,128)S(1)}, f32[31,16,256]{2,1,0:T(8,128)}, u32[]{:S(2)}) copy-start(f32[31,16,256]{2,1,0:T(8,128)} %mix_ref.1) | copy-start | bytes 1523716
  24.4 28.9 %collective-permute-start = (bf16[128,256]{1,0:T(8,128)(2,1)S(1)}, bf16[128,256]{1,0:T(8,128)(2,1)S(1)}, u32[]{:S(2)}, u32[]{:S(2)}) collective-permute-start(bf16[128,256]{1,0:T(8,128)(2,1)S(1)} %get-tuple-element.17), channel_id=1, source_target_pairs={{1,0},{2,1},{3,2},{5,4},{6,5},{7,6},{9,8},{10,9},{11,10},{13,12},{... | collective-permute-start | bytes 196616 | tf_op jit(solution)/shard_map/ppermute | solution.py:337
  27.4 25.9 %collective-permute-start.1 = (bf16[128,256]{1,0:T(8,128)(2,1)S(1)}, bf16[128,256]{1,0:T(8,128)(2,1)S(1)}, u32[]{:S(2)}, u32[]{:S(2)}) collective-permute-start(bf16[128,256]{1,0:T(8,128)(2,1)S(1)} %get-tuple-element.18), channel_id=1, source_target_pairs={{0,1},{1,2},{2,3},{4,5},{5,6},{6,7},{8,9},{9,10},{10,11},{12,13},{... | collective-permute-start | bytes 196616 | tf_op jit(solution)/shard_map/ppermute | solution.py:336
  31.8 21.5 %collective-permute-start.3 = (bf16[16,128]{1,0:T(8,128)(2,1)S(1)}, bf16[16,128]{1,0:T(8,128)(2,1)S(1)}, u32[]{:S(2)}, u32[]{:S(2)}) collective-permute-start(bf16[16,128]{1,0:T(8,128)(2,1)S(1)} %convert_element_type.7), channel_id=1, source_target_pairs={{0,4},{4,8},{8,12},{12,16},{16,20},{20,24},{24,28},{28,32},{32,36}... | collective-permute-start | bytes 12296 | tf_op jit(solution)/shard_map/ppermute | solution.py:334
  33.1 20.2 %collective-permute-start.2 = (bf16[16,128]{1,0:T(8,128)(2,1)S(1)}, bf16[16,128]{1,0:T(8,128)(2,1)S(1)}, u32[]{:S(2)}, u32[]{:S(2)}) collective-permute-start(bf16[16,128]{1,0:T(8,128)(2,1)S(1)} %convert_element_type.6), channel_id=1, source_target_pairs={{4,0},{8,4},{12,8},{16,12},{20,16},{24,20},{28,24},{32,28},{36,32}... | collective-permute-start | bytes 12296 | tf_op jit(solution)/shard_map/ppermute | solution.py:335
  58.4 1.3 %copy-start.1 = (f32[32,4,16,256]{3,2,1,0:T(8,128)}, f32[32,4,16,256]{3,2,1,0:T(8,128)S(1)}, u32[]{:S(2)}) copy-start(f32[32,4,16,256]{3,2,1,0:T(8,128)S(1)} %get-tuple-element.21.hor_ref) | copy-start | bytes 6291460
  59.7 0.8 %copy-start.6 = (f32[32,16,256]{2,1,0:T(8,128)}, f32[32,16,256]{2,1,0:T(8,128)S(1)}, u32[]{:S(2)}) copy-start(f32[32,16,256]{2,1,0:T(8,128)S(1)} %get-tuple-element.24.ratio_ref) | copy-start | bytes 1572868
  60.5 1.6 %copy-start.2 = (f32[32,4,16,256]{3,2,1,0:T(8,128)S(1)}, f32[32,4,16,256]{3,2,1,0:T(8,128)}, u32[]{:S(2)}) copy-start(f32[32,4,16,256]{3,2,1,0:T(8,128)} %copy-done.1) | copy-start | bytes 6291460
  62.1 1.0 %copy-start.7 = (f32[32,16,256]{2,1,0:T(8,128)S(1)}, f32[32,16,256]{2,1,0:T(8,128)}, u32[]{:S(2)}) copy-start(f32[32,16,256]{2,1,0:T(8,128)} %copy-done.6) | copy-start | bytes 1572868

commit v2 on v1

--- a/solution.py
+++ b/solution.py
@@ -14,13 +14,24 @@
 LANES = 128
 HEAD_ROWS = 8
 VMEM_BYTES = 20 * 1024 * 1024
-
-
-def pack_kernel(owner_ref, cell_ref, rows_ref, out_ref, stage, rows_f, meta, slot_v, slot_s):
+WIDE_VMEM_BYTES = 61 * 1024 * 1024
+
+
+def pack_kernel(
+    owner_hbm, cell_hbm, rows_hbm, out_ref,
+    owner_ref, cell_ref, rows_ref, stage, rows_f, meta, slot_v, slot_s, sems,
+):
     tiles, block_rows, _ = out_ref.shape
     capacity = block_rows - HEAD_ROWS
     blocks = owner_ref.shape[0]
-    rows_f[...] = rows_ref[...].astype(jnp.float32)
+    owner_copy = pltpu.make_async_copy(owner_hbm, owner_ref, sems.at[0])
+    cell_copy = pltpu.make_async_copy(cell_hbm, cell_ref, sems.at[1])
+    rows_copy = pltpu.make_async_copy(rows_hbm, rows_ref, sems.at[2])
+    owner_copy.start()
+    cell_copy.start()
+    rows_copy.start()
+    owner_copy.wait()
+    cell_copy.wait()
     tile_id = lax.broadcasted_iota(jnp.int32, (tiles, LANES), 0)
     low = lax.broadcasted_iota(jnp.int32, (LANES, 2 * LANES), 0)
     high = lax.broadcasted_iota(jnp.int32, (LANES, 2 * LANES), 1)
@@ -48,7 +59,11 @@
         )
     meta[0] = total[:, :LANES]
     meta[1] = total[:, LANES:]
-    pltpu.sync_copy(slot_v, slot_s)
+    slot_copy = pltpu.make_async_copy(slot_v, slot_s, sems.at[3])
+    slot_copy.start()
+    rows_copy.wait()
+    rows_f[...] = rows_ref[...].astype(jnp.float32)
+    slot_copy.wait()
 
     def scatter(b, carried):
         base = pl.multiple_of(b * LANES, LANES)
@@ -80,16 +95,20 @@
     return pl.pallas_call(
         pack_kernel,
         out_shape=jax.ShapeDtypeStruct((tiles, capacity + HEAD_ROWS, width), jnp.bfloat16),
-        in_specs=[vmem] * 3,
+        in_specs=[pl.BlockSpec(memory_space=pltpu.HBM)] * 3,
         out_specs=vmem,
         scratch_shapes=[
+            pltpu.VMEM((blocks, LANES), jnp.int32),
+            pltpu.VMEM((blocks, LANES), jnp.int32),
+            pltpu.VMEM((obs_rows, width), jnp.bfloat16),
             pltpu.VMEM((tiles * capacity, width), jnp.float32),
             pltpu.VMEM((obs_rows, width), jnp.float32),
             pltpu.VMEM((2, tiles, LANES), jnp.float32),
             pltpu.VMEM((blocks, LANES), jnp.int32),
             pltpu.SMEM((blocks, LANES), jnp.int32),
+            pltpu.SemaphoreType.DMA((4,)),
         ],
-        compiler_params=pltpu.CompilerParams(vmem_limit_bytes=VMEM_BYTES),
+        compiler_params=pltpu.CompilerParams(vmem_limit_bytes=WIDE_VMEM_BYTES),
         name="pack_rows",
     )(obs_owner.reshape(blocks, LANES), obs_cell.reshape(blocks, LANES), obs_misfit)
 
@@ -98,29 +117,28 @@
     planes, rows, columns = adj_ref.shape
     north_ref[...] = adj_ref[:, 0, :].astype(jnp.bfloat16)
     south_ref[...] = adj_ref[:, rows - 1, :].astype(jnp.bfloat16)
-    lane = lax.broadcasted_iota(jnp.int32, (8, LANES), 1)
+    row = lax.broadcasted_iota(jnp.int32, (rows, LANES), 0)
+    lane = lax.broadcasted_iota(jnp.int32, (rows, LANES), 1)
     for ref, start, at in ((east_ref, 0, 0), (west_ref, columns - LANES, LANES - 1)):
-        pick = (lane == at).astype(jnp.float32).astype(jnp.bfloat16)
-        side = adj_ref[:, :, start : start + LANES].reshape(planes * rows, LANES)
-        line = lax.dot_general(
-            pick,
-            side.astype(jnp.bfloat16),
-            (((1,), (1,)), ((), ())),
-            preferred_element_type=jnp.float32,
-        )
-        for i in range(planes * rows // LANES):
-            ref[i : i + 1, :] = line[0:1, i * LANES : (i + 1) * LANES]
+        line = jnp.zeros((rows, planes), jnp.float32)
+        for r in range(rows):
+            pick = ((lane == at) & (row == r)).astype(jnp.float32).astype(jnp.bfloat16)
+            side = adj_ref[:, r, start : start + LANES].astype(jnp.bfloat16)
+            line = line + lax.dot_general(
+                pick, side, (((1,), (1,)), ((), ())), preferred_element_type=jnp.float32
+            )
+        ref[...] = line.astype(jnp.bfloat16)
 
 
 def edges(adjoint):
     levels, fields, rows, columns = adjoint.shape
     planes = levels * fields
     vmem = pl.BlockSpec(memory_space=pltpu.VMEM)
-    line = jax.ShapeDtypeStruct((planes * rows // LANES, LANES), jnp.float32)
+    side = jax.ShapeDtypeStruct((rows, planes), jnp.bfloat16)
     row = jax.ShapeDtypeStruct((planes, columns), jnp.bfloat16)
     return pl.pallas_call(
         edge_kernel,
-        out_shape=(row, row, line, line),
+        out_shape=(row, row, side, side),
         in_specs=[vmem],
         out_specs=(vmem,) * 4,
         compiler_params=pltpu.CompilerParams(vmem_limit_bytes=VMEM_BYTES),
@@ -129,43 +147,42 @@
     )(adjoint.reshape(planes, rows, columns))
 
 
-def turned_edge(edge, code, rows):
-    cosine = jnp.where(code == 0, 1.0, 0.0) - jnp.where(code == 2, 1.0, 0.0)
-    sine = jnp.where(code == 1, 1.0, 0.0) - jnp.where(code == 3, 1.0, 0.0)
-    field = (lax.broadcasted_iota(jnp.int32, edge.shape, 1) // rows) % 4
-    zonal = cosine * edge - sine * pltpu.roll(edge, LANES - rows, 1)
-    meridional = sine * pltpu.roll(edge, rows, 1) + cosine * edge
-    return jnp.where(field == 2, zonal, jnp.where(field == 3, meridional, edge))
-
-
-def spread_edge(edge, spread_ref):
-    shape = (LANES, LANES)
-    diagonal = lax.broadcasted_iota(jnp.int32, shape, 0) == lax.broadcasted_iota(jnp.int32, shape, 1)
-    ones = jnp.ones(shape, jnp.bfloat16)
-    for i in range(edge.shape[0]):
-        line = jnp.where(diagonal, jnp.broadcast_to(edge[i : i + 1, :], shape), 0.0)
-        spread_ref[i * LANES : (i + 1) * LANES, :] = jnp.dot(
-            line.astype(jnp.bfloat16), ones, preferred_element_type=jnp.float32
-        )
-
-
 def local_kernel(
-    seam_ref, adj_ref, flow_ref, mask_ref, mix_ref, north_ref, south_ref, east_ref, west_ref,
-    hor_ref, mask_inv_ref, lower_inv_ref, ratio_ref, north_f, south_f, east_f, west_f,
+    adj_ref, flow_ref, mask_ref, mix_ref,
+    hor_ref, coef_ref, weight_north_ref, weight_south_ref, weight_east_ref, weight_west_ref,
 ):
     levels, fields, rows, columns = adj_ref.shape
-    along_rank = lax.axis_index("along")
-    own_code = seam_ref[along_rank]
-    next_code = seam_ref[lax.rem(along_rank + 1, seam_ref.shape[0])]
-    spread_edge(turned_edge(west_ref[...].astype(jnp.float32), own_code, rows), west_f)
-    spread_edge(turned_edge(east_ref[...].astype(jnp.float32), (4 - next_code) & 3, rows), east_f)
-    north_f[...] = north_ref[...].astype(jnp.float32)
-    south_f[...] = south_ref[...].astype(jnp.float32)
+    planes = levels * fields
     shape = (rows, columns)
     lane = lax.broadcasted_iota(jnp.int32, shape, 1)
     sub = lax.broadcasted_iota(jnp.int32, shape, 0)
     last_column, first_column = lane == columns - 1, lane == 0
     last_row, first_row = sub == rows - 1, sub == 0
+
+    row = lax.broadcasted_iota(jnp.int32, (rows, LANES), 0)
+    short_lane = lax.broadcasted_iota(jnp.int32, (rows, LANES), 1)
+    repeat = (
+        lax.broadcasted_iota(jnp.int32, (levels, planes), 1) // fields
+        == lax.broadcasted_iota(jnp.int32, (levels, planes), 0)
+    ).astype(jnp.float32)
+    for ref, start, at, half in (
+        (weight_east_ref, columns - LANES, LANES - 1, 0.5),
+        (weight_west_ref, 0, 0, -0.5),
+    ):
+        line = jnp.zeros((rows, levels), jnp.float32)
+        for r in range(rows):
+            pick = ((short_lane == at) & (row == r)).astype(jnp.float32)
+            line = line + lax.dot_general(
+                pick,
+                flow_ref[:, 0, r, start : start + LANES],
+                (((1,), (1,)), ((), ())),
+                precision=lax.Precision.HIGHEST,
+                preferred_element_type=jnp.float32,
+            )
+        line = jnp.dot(
+            line, repeat, precision=lax.Precision.HIGHEST, preferred_element_type=jnp.float32
+        )
+        ref[...] = diffusion_rate + half * line
 
     def level(k, state):
         lower, ratio_prev = state
@@ -177,23 +194,21 @@
         inverse = 1.0 / (1.0 + lower + upper + lower * ratio_prev)
         ratio = -upper * inverse
         mask_inv = mask * inverse
-        mask_inv_ref[k] = mask_inv
-        lower_inv_ref[k] = lower * inverse
-        ratio_ref[k] = ratio
+        coef_ref[0, k] = mask_inv
+        coef_ref[1, k] = lower * inverse
+        coef_ref[2, k] = ratio
         flow_along, flow_cross = flow_ref[k, 0], flow_ref[k, 1]
+        north_weight = diffusion_rate + 0.5 * flow_cross[rows - 1 : rows, :]
+        south_weight = diffusion_rate - 0.5 * flow_cross[0:1, :]
         centers, advects, alongs, crosses = [], [], [], []
         for f in range(fields):
+            weight_north_ref[pl.ds(k * fields + f, 1), :] = north_weight
+            weight_south_ref[pl.ds(k * fields + f, 1), :] = south_weight
             x = adj_ref[k, f]
-            at = k * fields + f
-            tall = pl.ds(pl.multiple_of(at * rows, rows), rows)
-            halo_east = jnp.concatenate([east_f[tall, :]] * (columns // LANES), axis=1)
-            halo_west = jnp.concatenate([west_f[tall, :]] * (columns // LANES), axis=1)
-            east = jnp.where(last_column, halo_east, pltpu.roll(x, columns - 1, 1))
-            west = jnp.where(first_column, halo_west, pltpu.roll(x, 1, 1))
-            halo_north = jnp.broadcast_to(north_f[pl.ds(at, 1), :], shape)
-            halo_south = jnp.broadcast_to(south_f[pl.ds(at, 1), :], shape)
-            north = jnp.where(last_row, halo_north, pltpu.roll(x, rows - 1, 0))
-            south = jnp.where(first_row, halo_south, pltpu.roll(x, 1, 0))
+            east = jnp.where(last_column, 0.0, pltpu.roll(x, columns - 1, 1))
+            west = jnp.where(first_column, 0.0, pltpu.roll(x, 1, 1))
+            north = jnp.where(last_row, 0.0, pltpu.roll(x, rows - 1, 0))
+            south = jnp.where(first_row, 0.0, pltpu.roll(x, 1, 0))
             along = 0.5 * (east - west)
             cross = 0.5 * (north - south)
             advect = (
@@ -219,35 +234,122 @@
     lax.fori_loop(0, levels, level, (zero, zero))
 
 
-def local_part(seam_code, adjoint, flow, land_mask, mixing, north, south, east, west):
+def local_part(adjoint, flow, land_mask, mixing):
     levels, fields, rows, columns = adjoint.shape
     planes = levels * fields
     vmem = pl.BlockSpec(memory_space=pltpu.VMEM)
-    plane = jax.ShapeDtypeStruct((levels, rows, columns), jnp.float32)
+    shape = lambda *dims: jax.ShapeDtypeStruct(dims, jnp.float32)
     return pl.pallas_call(
         local_kernel,
-        out_shape=(jax.ShapeDtypeStruct(adjoint.shape, jnp.float32), plane, plane, plane),
-        in_specs=[pl.BlockSpec(memory_space=pltpu.SMEM)] + [vmem] * 8,
-        out_specs=(vmem,) * 4,
-        scratch_shapes=[pltpu.VMEM((planes, columns), jnp.float32)] * 2
-        + [pltpu.VMEM((planes * rows, LANES), jnp.float32)] * 2,
+        out_shape=(
+            shape(*adjoint.shape),
+            shape(3, levels, rows, columns),
+            shape(planes, columns),
+            shape(planes, columns),
+            shape(rows, planes),
+            shape(rows, planes),
+        ),
+        in_specs=[vmem] * 4,
+        out_specs=(vmem,) * 6,
         compiler_params=pltpu.CompilerParams(vmem_limit_bytes=VMEM_BYTES),
         cost_estimate=pl.CostEstimate(flops=1000, bytes_accessed=100000, transcendentals=0),
         name="local_part",
-    )(seam_code, adjoint, flow, land_mask, mixing, north, south, east, west)
+    )(adjoint, flow, land_mask, mixing)
+
+
+def turned_edge(edge, code):
+    planes = edge.shape[1]
+    cosine = jnp.where(code == 0, 1.0, 0.0) - jnp.where(code == 2, 1.0, 0.0)
+    sine = jnp.where(code == 1, 1.0, 0.0) - jnp.where(code == 3, 1.0, 0.0)
+    field = lax.broadcasted_iota(jnp.int32, edge.shape, 1) & 3
+    zonal = cosine * edge - sine * pltpu.roll(edge, planes - 1, 1)
+    meridional = sine * pltpu.roll(edge, 1, 1) + cosine * edge
+    return jnp.where(field == 2, zonal, jnp.where(field == 3, meridional, edge))
+
+
+def edge_term(edge, weight, sign, axis, vector):
+    planes = edge.shape[axis]
+    field = lax.broadcasted_iota(jnp.int32, edge.shape, axis) & 3
+    ahead = lambda n: pltpu.roll(edge, planes - n, axis)
+    behind = lambda n: pltpu.roll(edge, n, axis)
+    thermal = sign * 0.5 * thermal_coef * couple_rate
+    haline = sign * 0.5 * haline_coef * couple_rate
+    other = thermal * behind(vector) - haline * behind(vector - 1)
+    mixed = jnp.where(field == 0, -thermal * ahead(vector), 0.0)
+    mixed = jnp.where(field == 1, haline * ahead(vector - 1), mixed)
+    mixed = jnp.where(field == vector, other, mixed)
+    return weight * edge + mixed
+
+
+def start_with_edges(
+    acc, own_code, next_code, north_ref, south_ref, east_ref, west_ref,
+    weight_north, weight_south, weight_east, weight_west,
+):
+    rows, planes, columns = acc.shape
+    east = turned_edge(east_ref[...].astype(jnp.float32), (4 - next_code) & 3)
+    west = turned_edge(west_ref[...].astype(jnp.float32), own_code)
+    fill = jnp.zeros((LANES - rows, planes), jnp.float32)
+    tall = lambda line: jnp.transpose(jnp.concatenate([line, fill], axis=0))
+    east = tall(edge_term(east, weight_east[...], 1.0, 1, 2))
+    west = tall(edge_term(west, weight_west[...], -1.0, 1, 2))
+    north = edge_term(north_ref[...].astype(jnp.float32), weight_north[...], 1.0, 0, 3)
+    south = edge_term(south_ref[...].astype(jnp.float32), weight_south[...], -1.0, 0, 3)
+    lane = lax.broadcasted_iota(jnp.int32, (planes, LANES), 1)
+    blank = jnp.zeros((planes, columns - 2 * LANES), jnp.float32)
+    for c in range(rows):
+        first = jnp.where(lane == 0, jnp.broadcast_to(west[:, c : c + 1], lane.shape), 0.0)
+        last = jnp.where(lane == LANES - 1, jnp.broadcast_to(east[:, c : c + 1], lane.shape), 0.0)
+        line = jnp.concatenate([first, blank, last], axis=1) if blank.shape[1] else (
+            jnp.concatenate([first, last], axis=1)
+        )
+        if c == 0:
+            line = line + south
+        if c == rows - 1:
+            line = line + north
+        acc[c] = line
 
 
 GROUP = 8
 
 
-def finish_kernel(got_ref, hor_ref, mask_inv_ref, lower_inv_ref, ratio_ref, out_ref, acc):
+def finish_kernel(
+    seam_ref, got_ref, north_ref, south_ref, east_ref, west_ref, hor_hbm, coef_hbm,
+    weight_north_hbm, weight_south_hbm, weight_east_hbm, weight_west_hbm,
+    out_hbm, acc, out_ref, hor_ref, coef_ref,
+    weight_north, weight_south, weight_east, weight_west, sems, out_sems,
+):
     tiles, block_rows, width = got_ref.shape
     capacity = block_rows - HEAD_ROWS
     levels, fields, rows, columns = out_ref.shape
     depth = GROUP * capacity
+    weight_copies = [
+        pltpu.make_async_copy(source, target, sems.at[i])
+        for i, (source, target) in enumerate(
+            (
+                (weight_north_hbm, weight_north),
+                (weight_south_hbm, weight_south),
+                (weight_east_hbm, weight_east),
+                (weight_west_hbm, weight_west),
+            )
+        )
+    ]
+    solve_copies = [
+        pltpu.make_async_copy(hor_hbm, hor_ref, sems.at[4]),
+        pltpu.make_async_copy(coef_hbm, coef_ref, sems.at[5]),
+    ]
+    for copy in weight_copies + solve_copies:
+        copy.start()
     column_id = lax.broadcasted_iota(jnp.int32, (columns, depth), 0).astype(jnp.float32)
     left = lax.broadcasted_iota(jnp.int32, (1, LANES), 1) < capacity
-    acc[...] = jnp.zeros_like(acc)
+    along_rank = lax.axis_index("along")
+    own_code = seam_ref[along_rank]
+    next_code = seam_ref[lax.rem(along_rank + 1, seam_ref.shape[0])]
+    for copy in weight_copies:
+        copy.wait()
+    start_with_edges(
+        acc, own_code, next_code, north_ref, south_ref, east_ref, west_ref,
+        weight_north, weight_south, weight_east, weight_west,
+    )
 
     def gather(g, carried):
         payload = got_ref[pl.ds(g * GROUP, GROUP), 0:capacity, :].reshape(depth, width)
@@ -274,12 +376,15 @@
 
     lax.fori_loop(0, tiles // GROUP, gather, 0)
 
+    for copy in solve_copies:
+        copy.wait()
+
     def forward(q, previous):
         forcing = jnp.swapaxes(acc[:, pl.ds(pl.multiple_of(q * 8, 8), 8), :], 0, 1)
         state = list(previous)
         for i in range(8 // fields):
             k = q * (8 // fields) + i
-            mask_inv, lower_inv = mask_inv_ref[k], lower_inv_ref[k]
+            mask_inv, lower_inv = coef_ref[0, k], coef_ref[1, k]
             for f in range(fields):
                 state[f] = (
                     hor_ref[k, f] + mask_inv * forcing[i * fields + f] + lower_inv * state[f]
@@ -292,28 +397,51 @@
 
     def backward(step, below):
         k = levels - 2 - step
-        ratio = ratio_ref[k]
+        ratio = coef_ref[2, k]
         here = []
         for f in range(fields):
             here.append(out_ref[k, f] - ratio * below[f])
             out_ref[k, f] = here[f]
         return tuple(here)
 
-    lax.fori_loop(0, levels - 1, backward, last)
-
-
-def finish(got, hor, mask_inv, lower_inv, ratio):
+    below = last
+    out_copies = []
+    part = levels // 4
+    done = 0
+    for i in range(4):
+        steps = part - 1 if i == 0 else part
+        below = lax.fori_loop(done, done + steps, backward, below)
+        done += steps
+        span = pl.ds(levels - (i + 1) * part, part)
+        copy = pltpu.make_async_copy(out_ref.at[span], out_hbm.at[span], out_sems.at[i])
+        copy.start()
+        out_copies.append(copy)
+    for copy in out_copies:
+        copy.wait()
+
+
+def finish(seam_code, got, halos, local):
+    hor, coef, weights = local[0], local[1], local[2:]
     levels, fields, rows, columns = hor.shape
+    planes = levels * fields
     vmem = pl.BlockSpec(memory_space=pltpu.VMEM)
+    hbm = pl.BlockSpec(memory_space=pltpu.HBM)
     return pl.pallas_call(
         finish_kernel,
         out_shape=jax.ShapeDtypeStruct(hor.shape, jnp.float32),
-        in_specs=[vmem] * 5,
-        out_specs=vmem,
-        scratch_shapes=[pltpu.VMEM((rows, levels * fields, columns), jnp.float32)],
-        compiler_params=pltpu.CompilerParams(vmem_limit_bytes=VMEM_BYTES),
+        in_specs=[pl.BlockSpec(memory_space=pltpu.SMEM)] + [vmem] * 5 + [hbm] * 6,
+        out_specs=hbm,
+        scratch_shapes=[
+            pltpu.VMEM((rows, planes, columns), jnp.float32),
+            pltpu.VMEM(hor.shape, jnp.float32),
+            pltpu.VMEM(hor.shape, jnp.float32),
+            pltpu.VMEM(coef.shape, jnp.float32),
+        ]
+        + [pltpu.VMEM(w.shape, jnp.float32) for w in weights]
+        + [pltpu.SemaphoreType.DMA((6,)), pltpu.SemaphoreType.DMA((4,))],
+        compiler_params=pltpu.CompilerParams(vmem_limit_bytes=WIDE_VMEM_BYTES),
         name="finish",
-    )(got, hor, mask_inv, lower_inv, ratio)
+    )(seam_code, got, *halos, hor, coef, *weights)
 
 
 def per_device(adjoint, flow, land_mask, mixing, seam_code, obs_misfit, obs_owner, obs_cell):
@@ -331,14 +459,12 @@
     line_up = [(i, i + 1) for i in range(cross_count - 1)]
     line_down = [(target, source) for source, target in line_up]
     first_row, last_row, first_column, last_column = edges(adjoint)
-    west = lax.ppermute(last_column.astype(jnp.bfloat16), "along", ring_up)
-    east = lax.ppermute(first_column.astype(jnp.bfloat16), "along", ring_down)
+    west = lax.ppermute(last_column, "along", ring_up)
+    east = lax.ppermute(first_column, "along", ring_down)
     south = lax.ppermute(last_row, "cross", line_up)
     north = lax.ppermute(first_row, "cross", line_down)
-    hor, mask_inv, lower_inv, ratio = local_part(
-        seam_code, adjoint, flow, land_mask, mixing, north, south, east, west
-    )
-    return finish(got, hor, mask_inv, lower_inv, ratio)
+    local = local_part(adjoint, flow, land_mask, mixing)
+    return finish(seam_code, got, (north, south, east, west), local)
 
 
 def solution(mesh):

time: 78.2 us -> 71.3 us (0.912)
  waiting for transfers between devices: 15.7 us -> 6.61 us
  Pallas kernels: 28.2 us -> 34.2 us
  local copies, waits for them, and re-layouts: 9.02 us -> 5.09 us
    ppermute x2, waiting for transfers between devices: 15.7 us -> 4.67 us  [the longest x1 4.67 us: per_device(): west = lax.ppermute(last_column, 'along', ring_up)]
    unnamed x24 -> x28, local copies, waits for them, and re-layouts: 9.02 us -> 5.09 us
    pallas_call x1, Pallas kernels: 14.6 us -> 17.8 us  [finish(): pl.pallas_call(finish_kernel, out_shape=jax.ShapeDtypeStruct(hor.shape, j...]
    pallas_call x2, Pallas kernels: 5.85 us -> 8.18 us  [the longest x1 5.95 us: local_part(): pl.pallas_call(local_kernel, out_shape=(shape(*adjoint.shape), shape(3, l...]
    all_to_all x1, waiting for transfers between devices: 0.01 us -> 1.93 us  [per_device(): lax.all_to_all(packed, ('along', 'cross'), split_axis=0, concat_axis=0, t...]
  transfers between devices with their start and end apart: 5 -> 5, of which waited for: 1 -> 2; matrix products, arithmetic and copies ran while one was open for 0% -> 0% of each run, Pallas kernels for 8% -> 12%
where the time goes in v2:
time: 71.3 us; the launch traced here: 71.1 us
  Pallas kernels  34.2 us (48%)
  starting transfers between devices  25 us (35%)
  waiting for transfers between devices  6.61 us (9%)
  local copies, waits for them, and re-layouts  5.09 us (7%)
    pallas_call x1, Pallas kernels, finish(): pl.pallas_call(finish_kernel, out_shape=jax.ShapeDtypeStruct(hor.shape, j...  17.8 us
    all_to_all x1, starting transfers between devices, per_device(): lax.all_to_all(packed, ('along', 'cross'), split_axis=0, concat_axis=0, t...  11.9 us
    pallas_call x1, Pallas kernels, pack_rows(): pl.pallas_call(pack_kernel, out_shape=jax.ShapeDtypeStruct((tiles, capaci...  8.19 us
    pallas_call x1, Pallas kernels, local_part(): pl.pallas_call(local_kernel, out_shape=(shape(*adjoint.shape), shape(3, l...  5.95 us
    ppermute x1, starting transfers between devices, per_device(): east = lax.ppermute(first_column, 'along', ring_down)  5.76 us
    unnamed x28, local copies, waits for them, and re-layouts  5.09 us
    ppermute x1, waiting for transfers between devices, per_device(): west = lax.ppermute(last_column, 'along', ring_up)  4.67 us
    ppermute x1, starting transfers between devices, per_device(): south = lax.ppermute(last_row, 'cross', line_up)  4.31 us
  transfers between devices with their start and end apart: 5, of which 2 were waited for; matrix products, arithmetic and copies ran while one was open for 0% of the time, Pallas kernels for 12%

profile of v2, /device:TPU:1, one launch (start us, length us, event | category | flops | bytes accessed | tf_op | source)
XLA Modules:
  0.0 71.1 jit_solution(5391358797378362696)
XLA Ops:
  0.0 8.2 %pack_rows.1 = bf16[128,72,128]{2,1,0:T(8,128)(2,1)} custom-call(s32[32,128]{1,0:T(8,128)} %bitcast.4, s32[32,128]{1,0:T(8,128)} %bitcast.5, bf16[4096,128]{1,0:T(8,128)(2,1)} %rows_hbm.1), custom_call_target="tpu_custom_call" | custom-call | tf_op jit(solution)/shard_map/pack_rows/pallas_call | solution.py:95
  8.2 0.0 copy-start
  8.2 11.9 %all-to-all-start = ((bf16[128,72,128]{2,1,0:T(8,128)(2,1)}), bf16[128,72,128]{2,1,0:T(8,128)(2,1)}, u32[]{:S(2)}, u32[]{:S(2)}) async-start(bf16[128,72,128]{2,1,0:T(8,128)(2,1)} %pack_rows.1), calls=%async_computation | async-start | bytes 4718592 | tf_op jit(solution)/shard_map/all_to_all | solution.py:455
  20.1 0.0 copy-start.3
  20.1 0.0 copy-start.4
  20.2 0.0 copy-start.5
  20.2 2.2 %edges.1 = (bf16[128,256]{1,0:T(8,128)(2,1)S(1)}, bf16[128,256]{1,0:T(8,128)(2,1)S(1)}, bf16[16,128]{1,0:T(8,128)(2,1)S(1)}, bf16[16,128]{1,0:T(8,128)(2,1)S(1)}) custom-call(f32[128,16,256]{2,1,0:T(8,128)S(1)} %bitcast.3), custom_call_target="tpu_custom_call" | custom-call | flops 1000 | bytes 100000 | tf_op jit(solution)/shard_map/edges/pallas_call | solution.py:139
  22.4 3.0 %collective-permute-start = (bf16[128,256]{1,0:T(8,128)(2,1)S(1)}, bf16[128,256]{1,0:T(8,128)(2,1)S(1)}, u32[]{:S(2)}, u32[]{:S(2)}) collective-permute-start(bf16[128,256]{1,0:T(8,128)(2,1)S(1)} %get-tuple-element.19), channel_id=1, source_target_pairs={{1,0},{2,1},{3,2},{5,4},{6,5},{7,6},{9,8},{10,9},{11,10},{13,12},{... | collective-permute-start | bytes 196616 | tf_op jit(solution)/shard_map/ppermute | solution.py:465
  25.4 4.3 %collective-permute-start.1 = (bf16[128,256]{1,0:T(8,128)(2,1)S(1)}, bf16[128,256]{1,0:T(8,128)(2,1)S(1)}, u32[]{:S(2)}, u32[]{:S(2)}) collective-permute-start(bf16[128,256]{1,0:T(8,128)(2,1)S(1)} %get-tuple-element.20), channel_id=1, source_target_pairs={{0,1},{1,2},{2,3},{4,5},{5,6},{6,7},{8,9},{9,10},{10,11},{12,13},{... | collective-permute-start | bytes 196616 | tf_op jit(solution)/shard_map/ppermute | solution.py:464
  29.8 5.8 %collective-permute-start.2 = (bf16[16,128]{1,0:T(8,128)(2,1)S(1)}, bf16[16,128]{1,0:T(8,128)(2,1)S(1)}, u32[]{:S(2)}, u32[]{:S(2)}) collective-permute-start(bf16[16,128]{1,0:T(8,128)(2,1)S(1)} %get-tuple-element.21), channel_id=1, source_target_pairs={{4,0},{8,4},{12,8},{16,12},{20,16},{24,20},{28,24},{32,28},{36,32}... | collective-permute-start | bytes 12296 | tf_op jit(solution)/shard_map/ppermute | solution.py:463
  35.5 0.0 collective-permute-start.3
  35.6 6.0 %local_part.1 = (f32[32,4,16,256]{3,2,1,0:T(8,128)S(1)}, f32[3,32,16,256]{3,2,1,0:T(8,128)S(1)}, f32[128,256]{1,0:T(8,128)S(1)}, f32[128,256]{1,0:T(8,128)S(1)},...) custom-call(f32[32,4,16,256]{3,2,1,0:T(8,128)S(1)} %copy-done, f32[32,2,16,256]{3,2,1,0:T(8,128)S(1)} %copy-done.3, ...), custom_call_target="tpu_custom_call" | custom-call | flops 1000 | bytes 100000 | tf_op jit(solution)/shard_map/local_part/pallas_call | solution.py:242
  41.5 1.3 %copy-done.1 = f32[32,4,16,256]{3,2,1,0:T(8,128)} copy-done((f32[32,4,16,256]{3,2,1,0:T(8,128)}, f32[32,4,16,256]{3,2,1,0:T(8,128)S(1)}, u32[]{:S(2)}) %copy-start.1) | copy-done | bytes 2097176
  42.9 1.2 %copy-done.2 = f32[3,32,16,256]{3,2,1,0:T(8,128)} copy-done((f32[3,32,16,256]{3,2,1,0:T(8,128)}, f32[3,32,16,256]{3,2,1,0:T(8,128)S(1)}, u32[]{:S(2)}) %copy-start.2) | copy-done | bytes 1572888
  44.1 0.7 copy-done.6
  44.7 0.6 copy-done.7
  45.4 0.6 copy-done.8
  46.0 0.6 copy-done.9
  46.6 0.0 collective-permute-done.2.east_ref
  46.6 4.7 %collective-permute-done.3.west_ref = bf16[16,128]{1,0:T(8,128)(2,1)S(1)} collective-permute-done((bf16[16,128]{1,0:T(8,128)(2,1)S(1)}, bf16[16,128]{1,0:T(8,128)(2,1)S(1)}, u32[]{:S(2)}, u32[]{:S(2)}) %collective-permute-start.3) | collective-permute-done | bytes 4128 | tf_op jit(solution)/shard_map/ppermute | solution.py:462
  51.3 0.0 collective-permute-done.north_ref
  51.3 0.0 collective-permute-done.1.south_ref
  51.3 1.9 %all-to-all-done.got_ref = bf16[128,72,128]{2,1,0:T(8,128)(2,1)} async-done(((bf16[128,72,128]{2,1,0:T(8,128)(2,1)}), bf16[128,72,128]{2,1,0:T(8,128)(2,1)}, u32[]{:S(2)}, u32[]{:S(2)}) %all-to-all-start) | async-done | bytes 2359328 | tf_op jit(solution)/shard_map/all_to_all | solution.py:455
  53.2 17.8 %finish.1 = f32[32,4,16,256]{3,2,1,0:T(8,128)} custom-call(s32[32]{0:T(128)} %seam_ref.1, bf16[128,72,128]{2,1,0:T(8,128)(2,1)} %all-to-all-done.got_ref, bf16[128,256]{1,0:T(8,128)(2,1)} %copy-done.10, bf16[128,256]{1,0:T(8,128)(2,1)} %copy-done.11, bf16[16,128]{1,0:T(8,128)(2,1)} %copy-done.12, bf16[16,128]{1,0:T(8,128)(2,1)} %copy-done.13, ...), custom_call_target="tpu_custom_call" | custom-call | tf_op jit(solution)/shard_map/finish/pallas_call | solution.py:429
  (18 shorter events, 0.0 us)
Async XLA Ops:
  8.2 12.0 %copy-start = (f32[32,4,16,256]{3,2,1,0:T(8,128)S(1)}, f32[32,4,16,256]{3,2,1,0:T(8,128)}, u32[]{:S(2)}) copy-start(f32[32,4,16,256]{3,2,1,0:T(8,128)} %adj_ref) | copy-start | bytes 6291460
  8.2 45.0 %all-to-all-start = ((bf16[128,72,128]{2,1,0:T(8,128)(2,1)}), bf16[128,72,128]{2,1,0:T(8,128)(2,1)}, u32[]{:S(2)}, u32[]{:S(2)}) async-start(bf16[128,72,128]{2,1,0:T(8,128)(2,1)} %pack_rows.1), calls=%async_computation | async-start | bytes 4718592 | tf_op jit(solution)/shard_map/all_to_all | solution.py:455
  20.1 15.4 %copy-start.3 = (f32[32,2,16,256]{3,2,1,0:T(8,128)S(1)}, f32[32,2,16,256]{3,2,1,0:T(8,128)}, u32[]{:S(2)}) copy-start(f32[32,2,16,256]{3,2,1,0:T(8,128)} %flow_ref.1) | copy-start | bytes 3145732
  20.1 15.4 %copy-start.4 = (s32[32,16,256]{2,1,0:T(8,128)S(1)}, s32[32,16,256]{2,1,0:T(8,128)}, u32[]{:S(2)}) copy-start(s32[32,16,256]{2,1,0:T(8,128)} %mask_ref.1) | copy-start | bytes 1572868
  20.2 15.4 %copy-start.5 = (f32[31,16,256]{2,1,0:T(8,128)S(1)}, f32[31,16,256]{2,1,0:T(8,128)}, u32[]{:S(2)}) copy-start(f32[31,16,256]{2,1,0:T(8,128)} %mix_ref.1) | copy-start | bytes 1523716
  22.4 28.9 %collective-permute-start = (bf16[128,256]{1,0:T(8,128)(2,1)S(1)}, bf16[128,256]{1,0:T(8,128)(2,1)S(1)}, u32[]{:S(2)}, u32[]{:S(2)}) collective-permute-start(bf16[128,256]{1,0:T(8,128)(2,1)S(1)} %get-tuple-element.19), channel_id=1, source_target_pairs={{1,0},{2,1},{3,2},{5,4},{6,5},{7,6},{9,8},{10,9},{11,10},{13,12},{... | collective-permute-start | bytes 196616 | tf_op jit(solution)/shard_map/ppermute | solution.py:465
  25.4 25.8 %collective-permute-start.1 = (bf16[128,256]{1,0:T(8,128)(2,1)S(1)}, bf16[128,256]{1,0:T(8,128)(2,1)S(1)}, u32[]{:S(2)}, u32[]{:S(2)}) collective-permute-start(bf16[128,256]{1,0:T(8,128)(2,1)S(1)} %get-tuple-element.20), channel_id=1, source_target_pairs={{0,1},{1,2},{2,3},{4,5},{5,6},{6,7},{8,9},{9,10},{10,11},{12,13},{... | collective-permute-start | bytes 196616 | tf_op jit(solution)/shard_map/ppermute | solution.py:464
  29.8 16.8 %collective-permute-start.2 = (bf16[16,128]{1,0:T(8,128)(2,1)S(1)}, bf16[16,128]{1,0:T(8,128)(2,1)S(1)}, u32[]{:S(2)}, u32[]{:S(2)}) collective-permute-start(bf16[16,128]{1,0:T(8,128)(2,1)S(1)} %get-tuple-element.21), channel_id=1, source_target_pairs={{4,0},{8,4},{12,8},{16,12},{20,16},{24,20},{28,24},{32,28},{36,32}... | collective-permute-start | bytes 12296 | tf_op jit(solution)/shard_map/ppermute | solution.py:463
  35.5 15.7 %collective-permute-start.3 = (bf16[16,128]{1,0:T(8,128)(2,1)S(1)}, bf16[16,128]{1,0:T(8,128)(2,1)S(1)}, u32[]{:S(2)}, u32[]{:S(2)}) collective-permute-start(bf16[16,128]{1,0:T(8,128)(2,1)S(1)} %get-tuple-element.22), channel_id=1, source_target_pairs={{0,4},{4,8},{8,12},{12,16},{16,20},{20,24},{24,28},{28,32},{32,36}... | collective-permute-start | bytes 12296 | tf_op jit(solution)/shard_map/ppermute | solution.py:462
  41.5 1.4 %copy-start.1 = (f32[32,4,16,256]{3,2,1,0:T(8,128)}, f32[32,4,16,256]{3,2,1,0:T(8,128)S(1)}, u32[]{:S(2)}) copy-start(f32[32,4,16,256]{3,2,1,0:T(8,128)S(1)} %get-tuple-element.23.hor_hbm) | copy-start | bytes 6291460
  42.9 1.2 %copy-start.2 = (f32[3,32,16,256]{3,2,1,0:T(8,128)}, f32[3,32,16,256]{3,2,1,0:T(8,128)S(1)}, u32[]{:S(2)}) copy-start(f32[3,32,16,256]{3,2,1,0:T(8,128)S(1)} %get-tuple-element.24.coef_hbm) | copy-start | bytes 4718596
  44.1 0.7 copy-start.6
  44.7 0.6 copy-start.7
  45.4 0.6 copy-start.8
  46.0 0.6 copy-start.9
  46.6 6.6 %copy-start.12 = (bf16[16,128]{1,0:T(8,128)(2,1)}, bf16[16,128]{1,0:T(8,128)(2,1)S(1)}, u32[]{:S(2)}) copy-start(bf16[16,128]{1,0:T(8,128)(2,1)S(1)} %collective-permute-done.2.east_ref) | copy-start | bytes 12292
  51.2 2.0 %copy-start.13 = (bf16[16,128]{1,0:T(8,128)(2,1)}, bf16[16,128]{1,0:T(8,128)(2,1)S(1)}, u32[]{:S(2)}) copy-start(bf16[16,128]{1,0:T(8,128)(2,1)S(1)} %collective-permute-done.3.west_ref) | copy-start | bytes 12292
  51.3 2.0 %copy-start.10 = (bf16[128,256]{1,0:T(8,128)(2,1)}, bf16[128,256]{1,0:T(8,128)(2,1)S(1)}, u32[]{:S(2)}) copy-start(bf16[128,256]{1,0:T(8,128)(2,1)S(1)} %collective-permute-done.north_ref) | copy-start | bytes 196612
  51.3 2.0 %copy-start.11 = (bf16[128,256]{1,0:T(8,128)(2,1)}, bf16[128,256]{1,0:T(8,128)(2,1)S(1)}, u32[]{:S(2)}) copy-start(bf16[128,256]{1,0:T(8,128)(2,1)S(1)} %collective-permute-done.1.south_ref) | copy-start | bytes 196612

commit v3 on v2

--- a/solution.py
+++ b/solution.py
@@ -1,3 +1,5 @@
+import functools
+
 import jax
 import jax.numpy as jnp
 from jax import lax
@@ -12,33 +14,39 @@
 haline_coef = 0.6
 
 LANES = 128
-HEAD_ROWS = 8
+HEAD_ROWS = 2
+PARTS = 4
 VMEM_BYTES = 20 * 1024 * 1024
 WIDE_VMEM_BYTES = 61 * 1024 * 1024
 
 
 def pack_kernel(
-    owner_hbm, cell_hbm, rows_hbm, out_ref,
-    owner_ref, cell_ref, rows_ref, stage, rows_f, meta, slot_v, slot_s, sems,
+    owner_hbm, cell_hbm, rows_hbm, out_hbm,
+    owner_ref, cell_ref, rows_ref, out_ref, stage, rows_f, slot_v, slot_s, sems, out_sems,
+    *, tiles,
 ):
-    tiles, block_rows, _ = out_ref.shape
+    block_rows = out_ref.shape[0] // tiles
     capacity = block_rows - HEAD_ROWS
     blocks = owner_ref.shape[0]
+    half = blocks // 2
     owner_copy = pltpu.make_async_copy(owner_hbm, owner_ref, sems.at[0])
     cell_copy = pltpu.make_async_copy(cell_hbm, cell_ref, sems.at[1])
     rows_copy = pltpu.make_async_copy(rows_hbm, rows_ref, sems.at[2])
     owner_copy.start()
     cell_copy.start()
     rows_copy.start()
-    owner_copy.wait()
-    cell_copy.wait()
     tile_id = lax.broadcasted_iota(jnp.int32, (tiles, LANES), 0)
     low = lax.broadcasted_iota(jnp.int32, (LANES, 2 * LANES), 0)
     high = lax.broadcasted_iota(jnp.int32, (LANES, 2 * LANES), 1)
     count_with = ((low <= high) | (high >= LANES)).astype(jnp.float32).astype(jnp.bfloat16)
-    place = (lax.broadcasted_iota(jnp.int32, (LANES, LANES), 0) % capacity).astype(jnp.float32)
+    device = lax.axis_index("along") * lax.axis_size("cross") + lax.axis_index("cross")
+    place = lax.broadcasted_iota(jnp.int32, (LANES, LANES), 0) - device * block_rows
+    place = (place & (LANES - 1)).astype(jnp.float32)
     carry = jnp.zeros((tiles, LANES), jnp.float32)
     total = jnp.zeros((tiles, 2 * LANES), jnp.float32)
+    owner_copy.wait()
+    cell_copy.wait()
+    slot_copies = []
     for b in range(blocks):
         owner = owner_ref[b : b + 1, :]
         cell = cell_ref[b : b + 1, :]
@@ -47,7 +55,7 @@
         counts = jnp.dot(hit_narrow, count_with, preferred_element_type=jnp.float32)
         rank = jnp.sum((counts[:, :LANES] + carry) * hit, axis=0, keepdims=True) - 1.0
         carry = carry + counts[:, LANES:]
-        slot_v[b : b + 1, :] = owner * capacity + rank.astype(jnp.int32)
+        slot_v[b : b + 1, :] = owner * block_rows + rank.astype(jnp.int32)
         row_part = ((cell >> 8) + 1).astype(jnp.float32)
         column_part = (cell & 255).astype(jnp.float32)
         here = place == rank
@@ -57,13 +65,17 @@
         total = total + lax.dot_general(
             hit_narrow, values, (((1,), (1,)), ((), ())), preferred_element_type=jnp.float32
         )
-    meta[0] = total[:, :LANES]
-    meta[1] = total[:, LANES:]
-    slot_copy = pltpu.make_async_copy(slot_v, slot_s, sems.at[3])
-    slot_copy.start()
+        if (b + 1) % half == 0:
+            span = pl.ds(b + 1 - half, half)
+            copy = pltpu.make_async_copy(
+                slot_v.at[span], slot_s.at[span], sems.at[3 + len(slot_copies)]
+            )
+            copy.start()
+            slot_copies.append(copy)
+    stage[pl.ds(capacity, tiles, stride=block_rows), :] = total[:, :LANES]
+    stage[pl.ds(capacity + 1, tiles, stride=block_rows), :] = total[:, LANES:]
     rows_copy.wait()
     rows_f[...] = rows_ref[...].astype(jnp.float32)
-    slot_copy.wait()
 
     def scatter(b, carried):
         base = pl.multiple_of(b * LANES, LANES)
@@ -71,42 +83,50 @@
             stage[pl.ds(slot_s[b, j], 1), :] = rows_f[pl.ds(base + j, 1), :]
         return carried
 
-    lax.fori_loop(0, blocks, scatter, 0)
-    first = lax.broadcasted_iota(jnp.int32, (HEAD_ROWS, LANES), 0) == 0
-
-    def narrow(d, carried):
-        base = pl.multiple_of(d * capacity, capacity)
-        out_ref[d, 0:capacity, :] = stage[pl.ds(base, capacity), :].astype(jnp.bfloat16)
-        head = jnp.where(
-            first,
-            jnp.broadcast_to(meta[0, pl.ds(d, 1), :], (HEAD_ROWS, LANES)),
-            jnp.broadcast_to(meta[1, pl.ds(d, 1), :], (HEAD_ROWS, LANES)),
-        )
-        out_ref[d, capacity:block_rows, :] = head.astype(jnp.bfloat16)
+    for i, copy in enumerate(slot_copies):
+        copy.wait()
+        lax.fori_loop(i * half, (i + 1) * half, scatter, 0)
+
+    step = out_ref.shape[0] // PARTS
+    piece = capacity
+
+    def narrow(i, carried):
+        span = pl.ds(pl.multiple_of(i * piece, piece), piece)
+        out_ref[span, :] = stage[span, :].astype(jnp.bfloat16)
         return carried
 
-    lax.fori_loop(0, tiles, narrow, 0, unroll=4)
+    out_copies = []
+    for i in range(PARTS):
+        lax.fori_loop(i * step // piece, (i + 1) * step // piece, narrow, 0, unroll=3)
+        span = pl.ds(i * step, step)
+        copy = pltpu.make_async_copy(out_ref.at[span], out_hbm.at[span], out_sems.at[i])
+        copy.start()
+        out_copies.append(copy)
+    for copy in out_copies:
+        copy.wait()
 
 
 def pack_rows(obs_owner, obs_cell, obs_misfit, tiles, capacity):
     obs_rows, width = obs_misfit.shape
     blocks = obs_rows // LANES
-    vmem = pl.BlockSpec(memory_space=pltpu.VMEM)
+    slots = tiles * (capacity + HEAD_ROWS)
+    hbm = pl.BlockSpec(memory_space=pltpu.HBM)
     return pl.pallas_call(
-        pack_kernel,
-        out_shape=jax.ShapeDtypeStruct((tiles, capacity + HEAD_ROWS, width), jnp.bfloat16),
-        in_specs=[pl.BlockSpec(memory_space=pltpu.HBM)] * 3,
-        out_specs=vmem,
+        functools.partial(pack_kernel, tiles=tiles),
+        out_shape=jax.ShapeDtypeStruct((slots, width), jnp.bfloat16),
+        in_specs=[hbm] * 3,
+        out_specs=hbm,
         scratch_shapes=[
             pltpu.VMEM((blocks, LANES), jnp.int32),
             pltpu.VMEM((blocks, LANES), jnp.int32),
             pltpu.VMEM((obs_rows, width), jnp.bfloat16),
-            pltpu.VMEM((tiles * capacity, width), jnp.float32),
+            pltpu.VMEM((slots, width), jnp.bfloat16),
+            pltpu.VMEM((slots, width), jnp.float32),
             pltpu.VMEM((obs_rows, width), jnp.float32),
-            pltpu.VMEM((2, tiles, LANES), jnp.float32),
             pltpu.VMEM((blocks, LANES), jnp.int32),
             pltpu.SMEM((blocks, LANES), jnp.int32),
-            pltpu.SemaphoreType.DMA((4,)),
+            pltpu.SemaphoreType.DMA((5,)),
+            pltpu.SemaphoreType.DMA((PARTS,)),
         ],
         compiler_params=pltpu.CompilerParams(vmem_limit_bytes=WIDE_VMEM_BYTES),
         name="pack_rows",
@@ -309,19 +329,45 @@
         acc[c] = line
 
 
-GROUP = 8
+GATHER_BLOCKS = 3
+
+
+def lane_order(head_f, line_ref, capacity):
+    tiles = head_f.shape[0]
+    pitch = capacity + HEAD_ROWS
+    lane = lax.broadcasted_iota(jnp.int32, (1, LANES), 1)
+    for t in range(tiles * pitch // LANES):
+        line = jnp.zeros((1, LANES), jnp.float32)
+        for source in range(tiles):
+            start = source * pitch - t * LANES
+            if start < LANES and start + capacity > 0:
+                inside = (lane >= start) & (lane < start + capacity)
+                line = jnp.where(inside, head_f[source : source + 1, :], line)
+        line_ref[:, t * LANES : (t + 1) * LANES] = line
 
 
 def finish_kernel(
-    seam_ref, got_ref, north_ref, south_ref, east_ref, west_ref, hor_hbm, coef_hbm,
+    seam_ref, got_hbm, heads_hbm, north_ref, south_ref, east_ref, west_ref, hor_hbm, coef_hbm,
     weight_north_hbm, weight_south_hbm, weight_east_hbm, weight_west_hbm,
     out_hbm, acc, out_ref, hor_ref, coef_ref,
-    weight_north, weight_south, weight_east, weight_west, sems, out_sems,
+    weight_north, weight_south, weight_east, weight_west,
+    got_ref, heads_ref, head_f, row_line, column_line, sems, got_sems, out_sems,
 ):
-    tiles, block_rows, width = got_ref.shape
-    capacity = block_rows - HEAD_ROWS
+    slots, width = got_ref.shape
+    tiles = heads_ref.shape[0]
+    capacity = slots // tiles - HEAD_ROWS
     levels, fields, rows, columns = out_ref.shape
-    depth = GROUP * capacity
+    depth = slots // GATHER_BLOCKS
+    heads_copy = pltpu.make_async_copy(
+        heads_hbm.at[:, capacity // HEAD_ROWS], heads_ref, sems.at[6]
+    )
+    heads_copy.start()
+    got_copies = []
+    for i in range(GATHER_BLOCKS):
+        span = pl.ds(i * depth, depth)
+        copy = pltpu.make_async_copy(got_hbm.at[span], got_ref.at[span], got_sems.at[i])
+        copy.start()
+        got_copies.append(copy)
     weight_copies = [
         pltpu.make_async_copy(source, target, sems.at[i])
         for i, (source, target) in enumerate(
@@ -339,8 +385,6 @@
     ]
     for copy in weight_copies + solve_copies:
         copy.start()
-    column_id = lax.broadcasted_iota(jnp.int32, (columns, depth), 0).astype(jnp.float32)
-    left = lax.broadcasted_iota(jnp.int32, (1, LANES), 1) < capacity
     along_rank = lax.axis_index("along")
     own_code = seam_ref[along_rank]
     next_code = seam_ref[lax.rem(along_rank + 1, seam_ref.shape[0])]
@@ -351,20 +395,20 @@
         weight_north, weight_south, weight_east, weight_west,
     )
 
-    def gather(g, carried):
-        payload = got_ref[pl.ds(g * GROUP, GROUP), 0:capacity, :].reshape(depth, width)
-        turned = jnp.transpose(payload)
-        row_of, column_of = [], []
-        for i in range(0, GROUP, 2):
-            one = got_ref[g * GROUP + i, capacity:block_rows, :].astype(jnp.float32)
-            two = got_ref[g * GROUP + i + 1, capacity:block_rows, :].astype(jnp.float32)
-            row_of.append(jnp.where(left, one[0:1], two[0:1]))
-            column_of.append(jnp.where(left, one[1:2], two[1:2]))
-        row_of = jnp.concatenate(row_of, axis=1)
-        column_of = jnp.concatenate(column_of, axis=1)
+    heads_copy.wait()
+    heads = heads_ref[...].astype(jnp.float32)
+    for i, line_ref in enumerate((row_line, column_line)):
+        head_f[i] = heads[:, i, :]
+        lane_order(head_f.at[i], line_ref, capacity)
+    column_id = lax.broadcasted_iota(jnp.int32, (columns, depth), 0).astype(jnp.float32)
+    zero = jnp.zeros((width, depth), jnp.bfloat16)
+    for i in range(GATHER_BLOCKS):
+        got_copies[i].wait()
+        turned = jnp.transpose(got_ref[i * depth : (i + 1) * depth, :])
+        row_of = row_line[:, i * depth : (i + 1) * depth]
+        column_of = column_line[:, i * depth : (i + 1) * depth]
         onehot = (column_id == column_of).astype(jnp.float32).astype(jnp.bfloat16)
         row_wide = jnp.broadcast_to(row_of, (width, depth)).astype(jnp.bfloat16)
-        zero = jnp.zeros((width, depth), jnp.bfloat16)
         masked = jnp.concatenate(
             [jnp.where(row_wide == (c + 1), turned, zero) for c in range(rows)], axis=0
         )
@@ -372,9 +416,6 @@
             masked, onehot, (((1,), (1,)), ((), ())), preferred_element_type=jnp.float32
         )
         acc[...] += part.reshape(rows, width, columns)
-        return carried
-
-    lax.fori_loop(0, tiles // GROUP, gather, 0)
 
     for copy in solve_copies:
         copy.wait()
@@ -406,9 +447,9 @@
 
     below = last
     out_copies = []
-    part = levels // 4
+    part = levels // PARTS
     done = 0
-    for i in range(4):
+    for i in range(PARTS):
         steps = part - 1 if i == 0 else part
         below = lax.fori_loop(done, done + steps, backward, below)
         done += steps
@@ -420,8 +461,10 @@
         copy.wait()
 
 
-def finish(seam_code, got, halos, local):
+def finish(seam_code, got, halos, local, tiles):
     hor, coef, weights = local[0], local[1], local[2:]
+    slots, width = got.shape
+    heads = got.reshape(tiles, slots // tiles // HEAD_ROWS, HEAD_ROWS, width)
     levels, fields, rows, columns = hor.shape
     planes = levels * fields
     vmem = pl.BlockSpec(memory_space=pltpu.VMEM)
@@ -429,7 +472,7 @@
     return pl.pallas_call(
         finish_kernel,
         out_shape=jax.ShapeDtypeStruct(hor.shape, jnp.float32),
-        in_specs=[pl.BlockSpec(memory_space=pltpu.SMEM)] + [vmem] * 5 + [hbm] * 6,
+        in_specs=[pl.BlockSpec(memory_space=pltpu.SMEM)] + [hbm] * 2 + [vmem] * 4 + [hbm] * 6,
         out_specs=hbm,
         scratch_shapes=[
             pltpu.VMEM((rows, planes, columns), jnp.float32),
@@ -438,10 +481,19 @@
             pltpu.VMEM(coef.shape, jnp.float32),
         ]
         + [pltpu.VMEM(w.shape, jnp.float32) for w in weights]
-        + [pltpu.SemaphoreType.DMA((6,)), pltpu.SemaphoreType.DMA((4,))],
+        + [
+            pltpu.VMEM((slots, width), jnp.bfloat16),
+            pltpu.VMEM((tiles, HEAD_ROWS, width), jnp.bfloat16),
+            pltpu.VMEM((2, tiles, LANES), jnp.float32),
+            pltpu.VMEM((1, slots), jnp.float32),
+            pltpu.VMEM((1, slots), jnp.float32),
+            pltpu.SemaphoreType.DMA((7,)),
+            pltpu.SemaphoreType.DMA((GATHER_BLOCKS,)),
+            pltpu.SemaphoreType.DMA((PARTS,)),
+        ],
         compiler_params=pltpu.CompilerParams(vmem_limit_bytes=WIDE_VMEM_BYTES),
         name="finish",
-    )(seam_code, got, *halos, hor, coef, *weights)
+    )(seam_code, got, heads, *halos, hor, coef, *weights)
 
 
 def per_device(adjoint, flow, land_mask, mixing, seam_code, obs_misfit, obs_owner, obs_cell):
@@ -452,7 +504,10 @@
     capacity = 2 * obs_misfit.shape[0] // devices
     packed = pack_rows(obs_owner, obs_cell, obs_misfit, devices, capacity)
     packed, adjoint = lax.optimization_barrier((packed, adjoint))
-    got = lax.all_to_all(packed, ("along", "cross"), split_axis=0, concat_axis=0, tiled=True)
+    slots, width = packed.shape
+    pairs = packed.reshape(slots // HEAD_ROWS, HEAD_ROWS, width)
+    got = lax.all_to_all(pairs, ("along", "cross"), split_axis=0, concat_axis=0, tiled=True)
+    got = got.reshape(slots, width)
 
     ring_up = [(i, (i + 1) % along_count) for i in range(along_count)]
     ring_down = [(target, source) for source, target in ring_up]
@@ -464,7 +519,7 @@
     south = lax.ppermute(last_row, "cross", line_up)
     north = lax.ppermute(first_row, "cross", line_down)
     local = local_part(adjoint, flow, land_mask, mixing)
-    return finish(seam_code, got, (north, south, east, west), local)
+    return finish(seam_code, got, (north, south, east, west), local, devices)
 
 
 def solution(mesh):

time: 71.3 us -> 71.8 us (level)
  Pallas kernels: 34.2 us -> 36.9 us
  waiting for transfers between devices: 6.61 us -> 4.33 us
    pallas_call x1, Pallas kernels: 17.8 us -> 21.1 us  [finish(): pl.pallas_call(finish_kernel, out_shape=jax.ShapeDtypeStruct(hor.shape, j...]
    ppermute x1, waiting for transfers between devices: 4.67 us -> 2.32 us  [per_device(): west = lax.ppermute(last_column, 'along', ring_up)]
    pallas_call x1, Pallas kernels: 8.19 us -> 7.36 us  [pack_rows(): pl.pallas_call(functools.partial(pack_kernel, tiles=tiles), out_shape=jax...]
where the time goes in v3:
time: 71.8 us; the launch traced here: 71.6 us
  Pallas kernels  36.9 us (51%)
  starting transfers between devices  25 us (35%)
  local copies, waits for them, and re-layouts  5.06 us (7%)
  waiting for transfers between devices  4.33 us (6%)
    pallas_call x1, Pallas kernels, finish(): pl.pallas_call(finish_kernel, out_shape=jax.ShapeDtypeStruct(hor.shape, j...  21.1 us
    all_to_all x1, starting transfers between devices, per_device(): lax.all_to_all(pairs, ('along', 'cross'), split_axis=0, concat_axis=0, ti...  11.9 us
    pallas_call x1, Pallas kernels, pack_rows(): pl.pallas_call(functools.partial(pack_kernel, tiles=tiles), out_shape=jax...  7.36 us
    pallas_call x1, Pallas kernels, local_part(): pl.pallas_call(local_kernel, out_shape=(shape(*adjoint.shape), shape(3, l...  6.17 us
    ppermute x1, starting transfers between devices, per_device(): east = lax.ppermute(first_column, 'along', ring_down)  5.76 us
    unnamed x28, local copies, waits for them, and re-layouts  5.06 us
    ppermute x1, starting transfers between devices, per_device(): south = lax.ppermute(last_row, 'cross', line_up)  4.31 us
    ppermute x1, starting transfers between devices, per_device(): north = lax.ppermute(first_row, 'cross', line_down)  3.04 us
  transfers between devices with their start and end apart: 5, of which 2 were waited for; matrix products, arithmetic and copies ran while one was open for 0% of the time, Pallas kernels for 12%

profile of v3, /device:TPU:1, one launch (start us, length us, event | category | flops | bytes accessed | tf_op | source)
XLA Modules:
  0.0 71.6 jit_solution(11396527307670618301)
XLA Ops:
  0.0 7.4 %pack_rows.1 = bf16[8448,128]{1,0:T(8,128)(2,1)} custom-call(s32[32,128]{1,0:T(8,128)} %bitcast.8, s32[32,128]{1,0:T(8,128)} %bitcast.9, bf16[4096,128]{1,0:T(8,128)(2,1)} %rows_hbm.1), custom_call_target="tpu_custom_call" | custom-call | tf_op jit(solution)/shard_map/pack_rows/pallas_call | solution.py:114
  7.4 0.0 copy-start
  7.4 11.9 %all-to-all-start = ((bf16[4224,2,128]{2,1,0:T(2,128)(2,1)}), bf16[4224,2,128]{2,1,0:T(2,128)(2,1)}, u32[]{:S(2)}, u32[]{:S(2)}) async-start(bf16[4224,2,128]{2,1,0:T(2,128)(2,1)} %bitcast.7), calls=%async_computation | async-start | bytes 4325376 | tf_op jit(solution)/shard_map/all_to_all | solution.py:509
  19.3 0.0 copy-start.3
  19.3 0.0 copy-start.4
  19.3 0.0 copy-start.5
  19.3 2.2 %edges.1 = (bf16[128,256]{1,0:T(8,128)(2,1)S(1)}, bf16[128,256]{1,0:T(8,128)(2,1)S(1)}, bf16[16,128]{1,0:T(8,128)(2,1)S(1)}, bf16[16,128]{1,0:T(8,128)(2,1)S(1)}) custom-call(f32[128,16,256]{2,1,0:T(8,128)S(1)} %bitcast.6), custom_call_target="tpu_custom_call" | custom-call | flops 1000 | bytes 100000 | tf_op jit(solution)/shard_map/edges/pallas_call | solution.py:159
  21.6 3.0 %collective-permute-start = (bf16[128,256]{1,0:T(8,128)(2,1)S(1)}, bf16[128,256]{1,0:T(8,128)(2,1)S(1)}, u32[]{:S(2)}, u32[]{:S(2)}) collective-permute-start(bf16[128,256]{1,0:T(8,128)(2,1)S(1)} %get-tuple-element.19), channel_id=1, source_target_pairs={{1,0},{2,1},{3,2},{5,4},{6,5},{7,6},{9,8},{10,9},{11,10},{13,12},{... | collective-permute-start | bytes 196616 | tf_op jit(solution)/shard_map/ppermute | solution.py:520
  24.6 4.3 %collective-permute-start.1 = (bf16[128,256]{1,0:T(8,128)(2,1)S(1)}, bf16[128,256]{1,0:T(8,128)(2,1)S(1)}, u32[]{:S(2)}, u32[]{:S(2)}) collective-permute-start(bf16[128,256]{1,0:T(8,128)(2,1)S(1)} %get-tuple-element.20), channel_id=1, source_target_pairs={{0,1},{1,2},{2,3},{4,5},{5,6},{6,7},{8,9},{9,10},{10,11},{12,13},{... | collective-permute-start | bytes 196616 | tf_op jit(solution)/shard_map/ppermute | solution.py:519
  28.9 5.8 %collective-permute-start.2 = (bf16[16,128]{1,0:T(8,128)(2,1)S(1)}, bf16[16,128]{1,0:T(8,128)(2,1)S(1)}, u32[]{:S(2)}, u32[]{:S(2)}) collective-permute-start(bf16[16,128]{1,0:T(8,128)(2,1)S(1)} %get-tuple-element.21), channel_id=1, source_target_pairs={{4,0},{8,4},{12,8},{16,12},{20,16},{24,20},{28,24},{32,28},{36,32}... | collective-permute-start | bytes 12296 | tf_op jit(solution)/shard_map/ppermute | solution.py:518
  34.7 0.0 collective-permute-start.3
  34.7 6.2 %local_part.1 = (f32[32,4,16,256]{3,2,1,0:T(8,128)S(1)}, f32[3,32,16,256]{3,2,1,0:T(8,128)S(1)}, f32[128,256]{1,0:T(8,128)S(1)}, f32[128,256]{1,0:T(8,128)S(1)},...) custom-call(f32[32,4,16,256]{3,2,1,0:T(8,128)S(1)} %copy-done, f32[32,2,16,256]{3,2,1,0:T(8,128)S(1)} %copy-done.3, ...), custom_call_target="tpu_custom_call" | custom-call | flops 1000 | bytes 100000 | tf_op jit(solution)/shard_map/local_part/pallas_call | solution.py:262
  40.9 1.4 %copy-done.1 = f32[32,4,16,256]{3,2,1,0:T(8,128)} copy-done((f32[32,4,16,256]{3,2,1,0:T(8,128)}, f32[32,4,16,256]{3,2,1,0:T(8,128)S(1)}, u32[]{:S(2)}) %copy-start.1) | copy-done | bytes 2097176
  42.3 1.2 %copy-done.2 = f32[3,32,16,256]{3,2,1,0:T(8,128)} copy-done((f32[3,32,16,256]{3,2,1,0:T(8,128)}, f32[3,32,16,256]{3,2,1,0:T(8,128)S(1)}, u32[]{:S(2)}) %copy-start.2) | copy-done | bytes 1572888
  43.4 0.7 copy-done.6
  44.1 0.6 copy-done.7
  44.7 0.6 copy-done.8
  45.3 0.6 copy-done.9
  45.9 0.0 collective-permute-done.2.east_ref
  45.9 2.3 %collective-permute-done.3.west_ref = bf16[16,128]{1,0:T(8,128)(2,1)S(1)} collective-permute-done((bf16[16,128]{1,0:T(8,128)(2,1)S(1)}, bf16[16,128]{1,0:T(8,128)(2,1)S(1)}, u32[]{:S(2)}, u32[]{:S(2)}) %collective-permute-start.3) | collective-permute-done | bytes 4128 | tf_op jit(solution)/shard_map/ppermute | solution.py:517
  48.3 0.0 collective-permute-done.north_ref
  48.3 0.0 collective-permute-done.1.south_ref
  48.3 2.0 %all-to-all-done = bf16[4224,2,128]{2,1,0:T(2,128)(2,1)} async-done(((bf16[4224,2,128]{2,1,0:T(2,128)(2,1)}), bf16[4224,2,128]{2,1,0:T(2,128)(2,1)}, u32[]{:S(2)}, u32[]{:S(2)}) %all-to-all-start) | async-done | bytes 2162720 | tf_op jit(solution)/shard_map/all_to_all | solution.py:509
  50.3 21.1 %finish.1 = f32[32,4,16,256]{3,2,1,0:T(8,128)} custom-call(s32[32]{0:T(128)} %seam_ref.1, bf16[8448,128]{1,0:T(8,128)(2,1)} %bitcast.3.got_hbm, bf16[128,33,2,128]{3,2,1,0:T(2,128)(2,1)} %bitcast.4.heads_hbm, bf16[128,256]{1,0:T(8,128)(2,1)} %copy-done.10, bf16[128,256]{1,0:T(8,128)(2,1)} %copy-done.11, bf16[16,128]{1,0:T(8,128)(2,1)} %copy-done.12, ...), custom_call_target="tpu_custom_call" | custom-call | tf_op jit(solution)/shard_map/finish/pallas_call | solution.py:472
  (18 shorter events, 0.0 us)
Async XLA Ops:
  7.4 12.0 %copy-start = (f32[32,4,16,256]{3,2,1,0:T(8,128)S(1)}, f32[32,4,16,256]{3,2,1,0:T(8,128)}, u32[]{:S(2)}) copy-start(f32[32,4,16,256]{3,2,1,0:T(8,128)} %adj_ref) | copy-start | bytes 6291460
  7.4 42.9 %all-to-all-start = ((bf16[4224,2,128]{2,1,0:T(2,128)(2,1)}), bf16[4224,2,128]{2,1,0:T(2,128)(2,1)}, u32[]{:S(2)}, u32[]{:S(2)}) async-start(bf16[4224,2,128]{2,1,0:T(2,128)(2,1)} %bitcast.7), calls=%async_computation | async-start | bytes 4325376 | tf_op jit(solution)/shard_map/all_to_all | solution.py:509
  19.3 15.4 %copy-start.3 = (f32[32,2,16,256]{3,2,1,0:T(8,128)S(1)}, f32[32,2,16,256]{3,2,1,0:T(8,128)}, u32[]{:S(2)}) copy-start(f32[32,2,16,256]{3,2,1,0:T(8,128)} %flow_ref.1) | copy-start | bytes 3145732
  19.3 15.4 %copy-start.4 = (s32[32,16,256]{2,1,0:T(8,128)S(1)}, s32[32,16,256]{2,1,0:T(8,128)}, u32[]{:S(2)}) copy-start(s32[32,16,256]{2,1,0:T(8,128)} %mask_ref.1) | copy-start | bytes 1572868
  19.3 15.4 %copy-start.5 = (f32[31,16,256]{2,1,0:T(8,128)S(1)}, f32[31,16,256]{2,1,0:T(8,128)}, u32[]{:S(2)}) copy-start(f32[31,16,256]{2,1,0:T(8,128)} %mix_ref.1) | copy-start | bytes 1523716
  21.6 26.7 %collective-permute-start = (bf16[128,256]{1,0:T(8,128)(2,1)S(1)}, bf16[128,256]{1,0:T(8,128)(2,1)S(1)}, u32[]{:S(2)}, u32[]{:S(2)}) collective-permute-start(bf16[128,256]{1,0:T(8,128)(2,1)S(1)} %get-tuple-element.19), channel_id=1, source_target_pairs={{1,0},{2,1},{3,2},{5,4},{6,5},{7,6},{9,8},{10,9},{11,10},{13,12},{... | collective-permute-start | bytes 196616 | tf_op jit(solution)/shard_map/ppermute | solution.py:520
  24.6 23.6 %collective-permute-start.1 = (bf16[128,256]{1,0:T(8,128)(2,1)S(1)}, bf16[128,256]{1,0:T(8,128)(2,1)S(1)}, u32[]{:S(2)}, u32[]{:S(2)}) collective-permute-start(bf16[128,256]{1,0:T(8,128)(2,1)S(1)} %get-tuple-element.20), channel_id=1, source_target_pairs={{0,1},{1,2},{2,3},{4,5},{5,6},{6,7},{8,9},{9,10},{10,11},{12,13},{... | collective-permute-start | bytes 196616 | tf_op jit(solution)/shard_map/ppermute | solution.py:519
  28.9 17.0 %collective-permute-start.2 = (bf16[16,128]{1,0:T(8,128)(2,1)S(1)}, bf16[16,128]{1,0:T(8,128)(2,1)S(1)}, u32[]{:S(2)}, u32[]{:S(2)}) collective-permute-start(bf16[16,128]{1,0:T(8,128)(2,1)S(1)} %get-tuple-element.21), channel_id=1, source_target_pairs={{4,0},{8,4},{12,8},{16,12},{20,16},{24,20},{28,24},{32,28},{36,32}... | collective-permute-start | bytes 12296 | tf_op jit(solution)/shard_map/ppermute | solution.py:518
  34.7 13.6 %collective-permute-start.3 = (bf16[16,128]{1,0:T(8,128)(2,1)S(1)}, bf16[16,128]{1,0:T(8,128)(2,1)S(1)}, u32[]{:S(2)}, u32[]{:S(2)}) collective-permute-start(bf16[16,128]{1,0:T(8,128)(2,1)S(1)} %get-tuple-element.22), channel_id=1, source_target_pairs={{0,4},{4,8},{8,12},{12,16},{16,20},{20,24},{24,28},{28,32},{32,36}... | collective-permute-start | bytes 12296 | tf_op jit(solution)/shard_map/ppermute | solution.py:517
  40.9 1.4 %copy-start.1 = (f32[32,4,16,256]{3,2,1,0:T(8,128)}, f32[32,4,16,256]{3,2,1,0:T(8,128)S(1)}, u32[]{:S(2)}) copy-start(f32[32,4,16,256]{3,2,1,0:T(8,128)S(1)} %get-tuple-element.23.hor_hbm) | copy-start | bytes 6291460
  42.3 1.2 %copy-start.2 = (f32[3,32,16,256]{3,2,1,0:T(8,128)}, f32[3,32,16,256]{3,2,1,0:T(8,128)S(1)}, u32[]{:S(2)}) copy-start(f32[3,32,16,256]{3,2,1,0:T(8,128)S(1)} %get-tuple-element.24.coef_hbm) | copy-start | bytes 4718596
  43.4 0.7 copy-start.6
  44.1 0.6 copy-start.7
  44.7 0.6 copy-start.8
  45.3 0.6 copy-start.9
  45.9 4.3 %copy-start.12 = (bf16[16,128]{1,0:T(8,128)(2,1)}, bf16[16,128]{1,0:T(8,128)(2,1)S(1)}, u32[]{:S(2)}) copy-start(bf16[16,128]{1,0:T(8,128)(2,1)S(1)} %collective-permute-done.2.east_ref) | copy-start | bytes 12292
  48.2 2.0 %copy-start.13 = (bf16[16,128]{1,0:T(8,128)(2,1)}, bf16[16,128]{1,0:T(8,128)(2,1)S(1)}, u32[]{:S(2)}) copy-start(bf16[16,128]{1,0:T(8,128)(2,1)S(1)} %collective-permute-done.3.west_ref) | copy-start | bytes 12292
  48.3 2.0 %copy-start.10 = (bf16[128,256]{1,0:T(8,128)(2,1)}, bf16[128,256]{1,0:T(8,128)(2,1)S(1)}, u32[]{:S(2)}) copy-start(bf16[128,256]{1,0:T(8,128)(2,1)S(1)} %collective-permute-done.north_ref) | copy-start | bytes 196612
  48.3 2.0 %copy-start.11 = (bf16[128,256]{1,0:T(8,128)(2,1)}, bf16[128,256]{1,0:T(8,128)(2,1)S(1)}, u32[]{:S(2)}) copy-start(bf16[128,256]{1,0:T(8,128)(2,1)S(1)} %collective-permute-done.1.south_ref) | copy-start | bytes 196612

commit v4 on v3

--- a/solution.py
+++ b/solution.py
@@ -362,12 +362,9 @@
         heads_hbm.at[:, capacity // HEAD_ROWS], heads_ref, sems.at[6]
     )
     heads_copy.start()
-    got_copies = []
     for i in range(GATHER_BLOCKS):
         span = pl.ds(i * depth, depth)
-        copy = pltpu.make_async_copy(got_hbm.at[span], got_ref.at[span], got_sems.at[i])
-        copy.start()
-        got_copies.append(copy)
+        pltpu.make_async_copy(got_hbm.at[span], got_ref.at[span], got_sems.at[i]).start()
     weight_copies = [
         pltpu.make_async_copy(source, target, sems.at[i])
         for i, (source, target) in enumerate(
@@ -402,13 +399,13 @@
         lane_order(head_f.at[i], line_ref, capacity)
     column_id = lax.broadcasted_iota(jnp.int32, (columns, depth), 0).astype(jnp.float32)
     zero = jnp.zeros((width, depth), jnp.bfloat16)
-    for i in range(GATHER_BLOCKS):
-        got_copies[i].wait()
-        turned = jnp.transpose(got_ref[i * depth : (i + 1) * depth, :])
-        row_of = row_line[:, i * depth : (i + 1) * depth]
-        column_of = column_line[:, i * depth : (i + 1) * depth]
-        onehot = (column_id == column_of).astype(jnp.float32).astype(jnp.bfloat16)
-        row_wide = jnp.broadcast_to(row_of, (width, depth)).astype(jnp.bfloat16)
+
+    def gather(i, carried):
+        span = pl.ds(pl.multiple_of(i * depth, depth), depth)
+        pltpu.make_async_copy(got_hbm.at[span], got_ref.at[span], got_sems.at[i]).wait()
+        turned = jnp.transpose(got_ref[span, :])
+        onehot = (column_id == column_line[:, span]).astype(jnp.float32).astype(jnp.bfloat16)
+        row_wide = jnp.broadcast_to(row_line[:, span], (width, depth)).astype(jnp.bfloat16)
         masked = jnp.concatenate(
             [jnp.where(row_wide == (c + 1), turned, zero) for c in range(rows)], axis=0
         )
@@ -416,6 +413,9 @@
             masked, onehot, (((1,), (1,)), ((), ())), preferred_element_type=jnp.float32
         )
         acc[...] += part.reshape(rows, width, columns)
+        return carried
+
+    lax.fori_loop(0, GATHER_BLOCKS, gather, 0)
 
     for copy in solve_copies:
         copy.wait()

time: 71.8 us -> 65.7 us (0.915)
  Pallas kernels: 36.9 us -> 30.7 us
    pallas_call x1, Pallas kernels: 21.1 us -> 15.1 us  [finish(): pl.pallas_call(finish_kernel, out_shape=jax.ShapeDtypeStruct(hor.shape, j...]
  transfers between devices with their start and end apart: 5 -> 5, of which waited for: 2 -> 2; matrix products, arithmetic and copies ran while one was open for 0% -> 0% of each run, Pallas kernels for 12% -> 13%
where the time goes in v4:
time: 65.7 us; the launch traced here: 65.4 us
  Pallas kernels  30.7 us (47%)
  starting transfers between devices  25 us (38%)
  local copies, waits for them, and re-layouts  5.06 us (8%)
  waiting for transfers between devices  4.51 us (7%)
    pallas_call x1, Pallas kernels, finish(): pl.pallas_call(finish_kernel, out_shape=jax.ShapeDtypeStruct(hor.shape, j...  15.1 us
    all_to_all x1, starting transfers between devices, per_device(): lax.all_to_all(pairs, ('along', 'cross'), split_axis=0, concat_axis=0, ti...  11.9 us
    pallas_call x1, Pallas kernels, pack_rows(): pl.pallas_call(functools.partial(pack_kernel, tiles=tiles), out_shape=jax...  7.36 us
    pallas_call x1, Pallas kernels, local_part(): pl.pallas_call(local_kernel, out_shape=(shape(*adjoint.shape), shape(3, l...  5.98 us
    ppermute x1, starting transfers between devices, per_device(): east = lax.ppermute(first_column, 'along', ring_down)  5.76 us
    unnamed x28, local copies, waits for them, and re-layouts  5.06 us
    ppermute x1, starting transfers between devices, per_device(): south = lax.ppermute(last_row, 'cross', line_up)  4.31 us
    ppermute x1, starting transfers between devices, per_device(): north = lax.ppermute(first_row, 'cross', line_down)  3.04 us
  transfers between devices with their start and end apart: 5, of which 2 were waited for; matrix products, arithmetic and copies ran while one was open for 0% of the time, Pallas kernels for 13%

profile of v4, /device:TPU:1, one launch (start us, length us, event | category | flops | bytes accessed | tf_op | source)
XLA Modules:
  0.0 65.4 jit_solution(3675256269287758716)
XLA Ops:
  0.0 7.4 %pack_rows.1 = bf16[8448,128]{1,0:T(8,128)(2,1)} custom-call(s32[32,128]{1,0:T(8,128)} %bitcast.8, s32[32,128]{1,0:T(8,128)} %bitcast.9, bf16[4096,128]{1,0:T(8,128)(2,1)} %rows_hbm.1), custom_call_target="tpu_custom_call" | custom-call | tf_op jit(solution)/shard_map/pack_rows/pallas_call | solution.py:114
  7.4 0.0 copy-start
  7.4 11.9 %all-to-all-start = ((bf16[4224,2,128]{2,1,0:T(2,128)(2,1)}), bf16[4224,2,128]{2,1,0:T(2,128)(2,1)}, u32[]{:S(2)}, u32[]{:S(2)}) async-start(bf16[4224,2,128]{2,1,0:T(2,128)(2,1)} %bitcast.7), calls=%async_computation | async-start | bytes 4325376 | tf_op jit(solution)/shard_map/all_to_all | solution.py:509
  19.3 0.0 copy-start.3
  19.3 0.0 copy-start.4
  19.3 0.0 copy-start.5
  19.3 2.2 %edges.1 = (bf16[128,256]{1,0:T(8,128)(2,1)S(1)}, bf16[128,256]{1,0:T(8,128)(2,1)S(1)}, bf16[16,128]{1,0:T(8,128)(2,1)S(1)}, bf16[16,128]{1,0:T(8,128)(2,1)S(1)}) custom-call(f32[128,16,256]{2,1,0:T(8,128)S(1)} %bitcast.6), custom_call_target="tpu_custom_call" | custom-call | flops 1000 | bytes 100000 | tf_op jit(solution)/shard_map/edges/pallas_call | solution.py:159
  21.6 3.0 %collective-permute-start = (bf16[128,256]{1,0:T(8,128)(2,1)S(1)}, bf16[128,256]{1,0:T(8,128)(2,1)S(1)}, u32[]{:S(2)}, u32[]{:S(2)}) collective-permute-start(bf16[128,256]{1,0:T(8,128)(2,1)S(1)} %get-tuple-element.19), channel_id=1, source_target_pairs={{1,0},{2,1},{3,2},{5,4},{6,5},{7,6},{9,8},{10,9},{11,10},{13,12},{... | collective-permute-start | bytes 196616 | tf_op jit(solution)/shard_map/ppermute | solution.py:520
  24.6 4.3 %collective-permute-start.1 = (bf16[128,256]{1,0:T(8,128)(2,1)S(1)}, bf16[128,256]{1,0:T(8,128)(2,1)S(1)}, u32[]{:S(2)}, u32[]{:S(2)}) collective-permute-start(bf16[128,256]{1,0:T(8,128)(2,1)S(1)} %get-tuple-element.20), channel_id=1, source_target_pairs={{0,1},{1,2},{2,3},{4,5},{5,6},{6,7},{8,9},{9,10},{10,11},{12,13},{... | collective-permute-start | bytes 196616 | tf_op jit(solution)/shard_map/ppermute | solution.py:519
  28.9 5.8 %collective-permute-start.2 = (bf16[16,128]{1,0:T(8,128)(2,1)S(1)}, bf16[16,128]{1,0:T(8,128)(2,1)S(1)}, u32[]{:S(2)}, u32[]{:S(2)}) collective-permute-start(bf16[16,128]{1,0:T(8,128)(2,1)S(1)} %get-tuple-element.21), channel_id=1, source_target_pairs={{4,0},{8,4},{12,8},{16,12},{20,16},{24,20},{28,24},{32,28},{36,32}... | collective-permute-start | bytes 12296 | tf_op jit(solution)/shard_map/ppermute | solution.py:518
  34.7 0.0 collective-permute-start.3
  34.7 6.0 %local_part.1 = (f32[32,4,16,256]{3,2,1,0:T(8,128)S(1)}, f32[3,32,16,256]{3,2,1,0:T(8,128)S(1)}, f32[128,256]{1,0:T(8,128)S(1)}, f32[128,256]{1,0:T(8,128)S(1)},...) custom-call(f32[32,4,16,256]{3,2,1,0:T(8,128)S(1)} %copy-done, f32[32,2,16,256]{3,2,1,0:T(8,128)S(1)} %copy-done.3, ...), custom_call_target="tpu_custom_call" | custom-call | flops 1000 | bytes 100000 | tf_op jit(solution)/shard_map/local_part/pallas_call | solution.py:262
  40.7 1.4 %copy-done.1 = f32[32,4,16,256]{3,2,1,0:T(8,128)} copy-done((f32[32,4,16,256]{3,2,1,0:T(8,128)}, f32[32,4,16,256]{3,2,1,0:T(8,128)S(1)}, u32[]{:S(2)}) %copy-start.1) | copy-done | bytes 2097176
  42.1 1.2 %copy-done.2 = f32[3,32,16,256]{3,2,1,0:T(8,128)} copy-done((f32[3,32,16,256]{3,2,1,0:T(8,128)}, f32[3,32,16,256]{3,2,1,0:T(8,128)S(1)}, u32[]{:S(2)}) %copy-start.2) | copy-done | bytes 1572888
  43.2 0.7 %copy-done.6 = f32[128,256]{1,0:T(8,128)} copy-done((f32[128,256]{1,0:T(8,128)}, f32[128,256]{1,0:T(8,128)S(1)}, u32[]{:S(2)}) %copy-start.6) | copy-done | bytes 131096
  43.9 0.6 copy-done.7
  44.5 0.6 copy-done.8
  45.1 0.6 copy-done.9
  45.7 0.0 collective-permute-done.2.east_ref
  45.7 2.5 %collective-permute-done.3.west_ref = bf16[16,128]{1,0:T(8,128)(2,1)S(1)} collective-permute-done((bf16[16,128]{1,0:T(8,128)(2,1)S(1)}, bf16[16,128]{1,0:T(8,128)(2,1)S(1)}, u32[]{:S(2)}, u32[]{:S(2)}) %collective-permute-start.3) | collective-permute-done | bytes 4128 | tf_op jit(solution)/shard_map/ppermute | solution.py:517
  48.2 0.0 collective-permute-done.north_ref
  48.3 0.0 collective-permute-done.1.south_ref
  48.3 2.0 %all-to-all-done = bf16[4224,2,128]{2,1,0:T(2,128)(2,1)} async-done(((bf16[4224,2,128]{2,1,0:T(2,128)(2,1)}), bf16[4224,2,128]{2,1,0:T(2,128)(2,1)}, u32[]{:S(2)}, u32[]{:S(2)}) %all-to-all-start) | async-done | bytes 2162720 | tf_op jit(solution)/shard_map/all_to_all | solution.py:509
  50.3 15.1 %finish.1 = f32[32,4,16,256]{3,2,1,0:T(8,128)} custom-call(s32[32]{0:T(128)} %seam_ref.1, bf16[8448,128]{1,0:T(8,128)(2,1)} %bitcast.3.got_hbm, bf16[128,33,2,128]{3,2,1,0:T(2,128)(2,1)} %bitcast.4.heads_hbm, bf16[128,256]{1,0:T(8,128)(2,1)} %copy-done.10, bf16[128,256]{1,0:T(8,128)(2,1)} %copy-done.11, bf16[16,128]{1,0:T(8,128)(2,1)} %copy-done.12, ...), custom_call_target="tpu_custom_call" | custom-call | tf_op jit(solution)/shard_map/finish/pallas_call | solution.py:472
  (18 shorter events, 0.0 us)
Async XLA Ops:
  7.4 12.0 %copy-start = (f32[32,4,16,256]{3,2,1,0:T(8,128)S(1)}, f32[32,4,16,256]{3,2,1,0:T(8,128)}, u32[]{:S(2)}) copy-start(f32[32,4,16,256]{3,2,1,0:T(8,128)} %adj_ref) | copy-start | bytes 6291460
  7.4 42.9 %all-to-all-start = ((bf16[4224,2,128]{2,1,0:T(2,128)(2,1)}), bf16[4224,2,128]{2,1,0:T(2,128)(2,1)}, u32[]{:S(2)}, u32[]{:S(2)}) async-start(bf16[4224,2,128]{2,1,0:T(2,128)(2,1)} %bitcast.7), calls=%async_computation | async-start | bytes 4325376 | tf_op jit(solution)/shard_map/all_to_all | solution.py:509
  19.3 15.4 %copy-start.3 = (f32[32,2,16,256]{3,2,1,0:T(8,128)S(1)}, f32[32,2,16,256]{3,2,1,0:T(8,128)}, u32[]{:S(2)}) copy-start(f32[32,2,16,256]{3,2,1,0:T(8,128)} %flow_ref.1) | copy-start | bytes 3145732
  19.3 15.4 %copy-start.4 = (s32[32,16,256]{2,1,0:T(8,128)S(1)}, s32[32,16,256]{2,1,0:T(8,128)}, u32[]{:S(2)}) copy-start(s32[32,16,256]{2,1,0:T(8,128)} %mask_ref.1) | copy-start | bytes 1572868
  19.3 15.4 %copy-start.5 = (f32[31,16,256]{2,1,0:T(8,128)S(1)}, f32[31,16,256]{2,1,0:T(8,128)}, u32[]{:S(2)}) copy-start(f32[31,16,256]{2,1,0:T(8,128)} %mix_ref.1) | copy-start | bytes 1523716
  21.6 26.7 %collective-permute-start = (bf16[128,256]{1,0:T(8,128)(2,1)S(1)}, bf16[128,256]{1,0:T(8,128)(2,1)S(1)}, u32[]{:S(2)}, u32[]{:S(2)}) collective-permute-start(bf16[128,256]{1,0:T(8,128)(2,1)S(1)} %get-tuple-element.19), channel_id=1, source_target_pairs={{1,0},{2,1},{3,2},{5,4},{6,5},{7,6},{9,8},{10,9},{11,10},{13,12},{... | collective-permute-start | bytes 196616 | tf_op jit(solution)/shard_map/ppermute | solution.py:520
  24.6 23.6 %collective-permute-start.1 = (bf16[128,256]{1,0:T(8,128)(2,1)S(1)}, bf16[128,256]{1,0:T(8,128)(2,1)S(1)}, u32[]{:S(2)}, u32[]{:S(2)}) collective-permute-start(bf16[128,256]{1,0:T(8,128)(2,1)S(1)} %get-tuple-element.20), channel_id=1, source_target_pairs={{0,1},{1,2},{2,3},{4,5},{5,6},{6,7},{8,9},{9,10},{10,11},{12,13},{... | collective-permute-start | bytes 196616 | tf_op jit(solution)/shard_map/ppermute | solution.py:519
  28.9 16.8 %collective-permute-start.2 = (bf16[16,128]{1,0:T(8,128)(2,1)S(1)}, bf16[16,128]{1,0:T(8,128)(2,1)S(1)}, u32[]{:S(2)}, u32[]{:S(2)}) collective-permute-start(bf16[16,128]{1,0:T(8,128)(2,1)S(1)} %get-tuple-element.21), channel_id=1, source_target_pairs={{4,0},{8,4},{12,8},{16,12},{20,16},{24,20},{28,24},{32,28},{36,32}... | collective-permute-start | bytes 12296 | tf_op jit(solution)/shard_map/ppermute | solution.py:518
  34.7 13.6 %collective-permute-start.3 = (bf16[16,128]{1,0:T(8,128)(2,1)S(1)}, bf16[16,128]{1,0:T(8,128)(2,1)S(1)}, u32[]{:S(2)}, u32[]{:S(2)}) collective-permute-start(bf16[16,128]{1,0:T(8,128)(2,1)S(1)} %get-tuple-element.22), channel_id=1, source_target_pairs={{0,4},{4,8},{8,12},{12,16},{16,20},{20,24},{24,28},{28,32},{32,36}... | collective-permute-start | bytes 12296 | tf_op jit(solution)/shard_map/ppermute | solution.py:517
  40.7 1.4 %copy-start.1 = (f32[32,4,16,256]{3,2,1,0:T(8,128)}, f32[32,4,16,256]{3,2,1,0:T(8,128)S(1)}, u32[]{:S(2)}) copy-start(f32[32,4,16,256]{3,2,1,0:T(8,128)S(1)} %get-tuple-element.23.hor_hbm) | copy-start | bytes 6291460
  42.1 1.2 %copy-start.2 = (f32[3,32,16,256]{3,2,1,0:T(8,128)}, f32[3,32,16,256]{3,2,1,0:T(8,128)S(1)}, u32[]{:S(2)}) copy-start(f32[3,32,16,256]{3,2,1,0:T(8,128)S(1)} %get-tuple-element.24.coef_hbm) | copy-start | bytes 4718596
  43.2 0.7 %copy-start.6 = (f32[128,256]{1,0:T(8,128)}, f32[128,256]{1,0:T(8,128)S(1)}, u32[]{:S(2)}) copy-start(f32[128,256]{1,0:T(8,128)S(1)} %get-tuple-element.25.weight_north_hbm) | copy-start | bytes 393220
  43.9 0.6 copy-start.7
  44.5 0.6 copy-start.8
  45.1 0.6 copy-start.9
  45.7 4.5 %copy-start.12 = (bf16[16,128]{1,0:T(8,128)(2,1)}, bf16[16,128]{1,0:T(8,128)(2,1)S(1)}, u32[]{:S(2)}) copy-start(bf16[16,128]{1,0:T(8,128)(2,1)S(1)} %collective-permute-done.2.east_ref) | copy-start | bytes 12292
  48.2 2.0 %copy-start.13 = (bf16[16,128]{1,0:T(8,128)(2,1)}, bf16[16,128]{1,0:T(8,128)(2,1)S(1)}, u32[]{:S(2)}) copy-start(bf16[16,128]{1,0:T(8,128)(2,1)S(1)} %collective-permute-done.3.west_ref) | copy-start | bytes 12292
  48.3 2.0 %copy-start.10 = (bf16[128,256]{1,0:T(8,128)(2,1)}, bf16[128,256]{1,0:T(8,128)(2,1)S(1)}, u32[]{:S(2)}) copy-start(bf16[128,256]{1,0:T(8,128)(2,1)S(1)} %collective-permute-done.north_ref) | copy-start | bytes 196612
  48.3 2.0 %copy-start.11 = (bf16[128,256]{1,0:T(8,128)(2,1)}, bf16[128,256]{1,0:T(8,128)(2,1)S(1)}, u32[]{:S(2)}) copy-start(bf16[128,256]{1,0:T(8,128)(2,1)S(1)} %collective-permute-done.1.south_ref) | copy-start | bytes 196612

commit v5 on v4

--- a/solution.py
+++ b/solution.py
@@ -16,7 +16,9 @@
 LANES = 128
 HEAD_ROWS = 2
 PARTS = 4
-VMEM_BYTES = 20 * 1024 * 1024
+CONVERT_AFTER = 16
+LAST_VMEM_BYTES = 44 * 1024 * 1024
+LOCAL_PLANES = 1536
 WIDE_VMEM_BYTES = 61 * 1024 * 1024
 
 
@@ -65,6 +67,12 @@
         total = total + lax.dot_general(
             hit_narrow, values, (((1,), (1,)), ((), ())), preferred_element_type=jnp.float32
         )
+        if b == CONVERT_AFTER:
+            rows_copy.wait()
+        if b >= CONVERT_AFTER:
+            share = rows_ref.shape[0] // (blocks - CONVERT_AFTER)
+            at = (b - CONVERT_AFTER) * share
+            rows_f[at : at + share, :] = rows_ref[at : at + share, :].astype(jnp.float32)
         if (b + 1) % half == 0:
             span = pl.ds(b + 1 - half, half)
             copy = pltpu.make_async_copy(
@@ -74,8 +82,6 @@
             slot_copies.append(copy)
     stage[pl.ds(capacity, tiles, stride=block_rows), :] = total[:, :LANES]
     stage[pl.ds(capacity + 1, tiles, stride=block_rows), :] = total[:, LANES:]
-    rows_copy.wait()
-    rows_f[...] = rows_ref[...].astype(jnp.float32)
 
     def scatter(b, carried):
         base = pl.multiple_of(b * LANES, LANES)
@@ -161,15 +167,14 @@
         out_shape=(row, row, side, side),
         in_specs=[vmem],
         out_specs=(vmem,) * 4,
-        compiler_params=pltpu.CompilerParams(vmem_limit_bytes=VMEM_BYTES),
+        compiler_params=pltpu.CompilerParams(vmem_limit_bytes=WIDE_VMEM_BYTES),
         cost_estimate=pl.CostEstimate(flops=1000, bytes_accessed=100000, transcendentals=0),
         name="edges",
     )(adjoint.reshape(planes, rows, columns))
 
 
 def local_kernel(
-    adj_ref, flow_ref, mask_ref, mix_ref,
-    hor_ref, coef_ref, weight_north_ref, weight_south_ref, weight_east_ref, weight_west_ref,
+    adj_ref, flow_ref, mask_ref, mix_ref, local_hbm, hor_ref, coef_ref, weight_ref, sems,
 ):
     levels, fields, rows, columns = adj_ref.shape
     planes = levels * fields
@@ -185,10 +190,8 @@
         lax.broadcasted_iota(jnp.int32, (levels, planes), 1) // fields
         == lax.broadcasted_iota(jnp.int32, (levels, planes), 0)
     ).astype(jnp.float32)
-    for ref, start, at, half in (
-        (weight_east_ref, columns - LANES, LANES - 1, 0.5),
-        (weight_west_ref, 0, 0, -0.5),
-    ):
+    row_planes = planes // rows
+    for place, start, at, half in ((0, columns - LANES, LANES - 1, 0.5), (planes, 0, 0, -0.5)):
         line = jnp.zeros((rows, levels), jnp.float32)
         for r in range(rows):
             pick = ((short_lane == at) & (row == r)).astype(jnp.float32)
@@ -202,7 +205,7 @@
         line = jnp.dot(
             line, repeat, precision=lax.Precision.HIGHEST, preferred_element_type=jnp.float32
         )
-        ref[...] = diffusion_rate + half * line
+        weight_ref[2 * row_planes, :, place : place + planes] = diffusion_rate + half * line
 
     def level(k, state):
         lower, ratio_prev = state
@@ -214,16 +217,17 @@
         inverse = 1.0 / (1.0 + lower + upper + lower * ratio_prev)
         ratio = -upper * inverse
         mask_inv = mask * inverse
-        coef_ref[0, k] = mask_inv
-        coef_ref[1, k] = lower * inverse
-        coef_ref[2, k] = ratio
+        coef_ref[k] = mask_inv
+        coef_ref[levels + k] = lower * inverse
+        coef_ref[2 * levels + k] = ratio
         flow_along, flow_cross = flow_ref[k, 0], flow_ref[k, 1]
         north_weight = diffusion_rate + 0.5 * flow_cross[rows - 1 : rows, :]
         south_weight = diffusion_rate - 0.5 * flow_cross[0:1, :]
         centers, advects, alongs, crosses = [], [], [], []
         for f in range(fields):
-            weight_north_ref[pl.ds(k * fields + f, 1), :] = north_weight
-            weight_south_ref[pl.ds(k * fields + f, 1), :] = south_weight
+            at = k * fields + f
+            weight_ref[at // rows, pl.ds(at % rows, 1), :] = north_weight
+            weight_ref[row_planes + at // rows, pl.ds(at % rows, 1), :] = south_weight
             x = adj_ref[k, f]
             east = jnp.where(last_column, 0.0, pltpu.roll(x, columns - 1, 1))
             west = jnp.where(first_column, 0.0, pltpu.roll(x, 1, 1))
@@ -244,34 +248,50 @@
         diverge = alongs[2] + crosses[3]
         buoy_along = thermal_coef * alongs[0] - haline_coef * alongs[1]
         buoy_cross = thermal_coef * crosses[0] - haline_coef * crosses[1]
-        hor_ref[k, 0] = mask_inv * (advects[0] - thermal_coef * couple_rate * diverge)
-        hor_ref[k, 1] = mask_inv * (advects[1] + haline_coef * couple_rate * diverge)
-        hor_ref[k, 2] = mask_inv * (advects[2] + coriolis * centers[3] + couple_rate * buoy_along)
-        hor_ref[k, 3] = mask_inv * (advects[3] - coriolis * centers[2] + couple_rate * buoy_cross)
+        hor_ref[k * fields + 0] = mask_inv * (advects[0] - thermal_coef * couple_rate * diverge)
+        hor_ref[k * fields + 1] = mask_inv * (advects[1] + haline_coef * couple_rate * diverge)
+        hor_ref[k * fields + 2] = mask_inv * (advects[2] + coriolis * centers[3] + couple_rate * buoy_along)
+        hor_ref[k * fields + 3] = mask_inv * (advects[3] - coriolis * centers[2] + couple_rate * buoy_cross)
         return upper, ratio
 
     zero = jnp.zeros(shape, jnp.float32)
     lax.fori_loop(0, levels, level, (zero, zero))
+    copies = local_copies(local_hbm, (hor_ref, coef_ref, weight_ref), sems, False)
+    for copy in copies:
+        copy.start()
+    for copy in copies:
+        copy.wait()
+
+
+def local_copies(local_hbm, refs, sems, inward):
+    copies, at = [], 0
+    for i, ref in enumerate(refs):
+        part = local_hbm.at[pl.ds(at, ref.shape[0])]
+        source, target = (part, ref) if inward else (ref, part)
+        copies.append(pltpu.make_async_copy(source, target, sems.at[i]))
+        at += ref.shape[0]
+    return copies
+
+
+def local_scratch(levels, fields, rows, columns):
+    planes = levels * fields
+    return [
+        pltpu.VMEM((planes, rows, columns), jnp.float32),
+        pltpu.VMEM((3 * levels, rows, columns), jnp.float32),
+        pltpu.VMEM((2 * planes // rows + 1, rows, columns), jnp.float32),
+    ]
 
 
 def local_part(adjoint, flow, land_mask, mixing):
     levels, fields, rows, columns = adjoint.shape
-    planes = levels * fields
     vmem = pl.BlockSpec(memory_space=pltpu.VMEM)
-    shape = lambda *dims: jax.ShapeDtypeStruct(dims, jnp.float32)
     return pl.pallas_call(
         local_kernel,
-        out_shape=(
-            shape(*adjoint.shape),
-            shape(3, levels, rows, columns),
-            shape(planes, columns),
-            shape(planes, columns),
-            shape(rows, planes),
-            shape(rows, planes),
-        ),
+        out_shape=jax.ShapeDtypeStruct((LOCAL_PLANES, rows, columns), jnp.float32),
         in_specs=[vmem] * 4,
-        out_specs=(vmem,) * 6,
-        compiler_params=pltpu.CompilerParams(vmem_limit_bytes=VMEM_BYTES),
+        out_specs=pl.BlockSpec(memory_space=pltpu.HBM),
+        scratch_shapes=local_scratch(*adjoint.shape) + [pltpu.SemaphoreType.DMA((3,))],
+        compiler_params=pltpu.CompilerParams(vmem_limit_bytes=WIDE_VMEM_BYTES),
         cost_estimate=pl.CostEstimate(flops=1000, bytes_accessed=100000, transcendentals=0),
         name="local_part",
     )(adjoint, flow, land_mask, mixing)
@@ -302,18 +322,22 @@
 
 
 def start_with_edges(
-    acc, own_code, next_code, north_ref, south_ref, east_ref, west_ref,
-    weight_north, weight_south, weight_east, weight_west,
+    acc, own_code, next_code, north_ref, south_ref, east_ref, west_ref, weight_ref
 ):
     rows, planes, columns = acc.shape
+    row_planes = planes // rows
+    weight_north = weight_ref[0:row_planes].reshape(planes, columns)
+    weight_south = weight_ref[row_planes : 2 * row_planes].reshape(planes, columns)
+    weight_east = weight_ref[2 * row_planes, :, 0:planes]
+    weight_west = weight_ref[2 * row_planes, :, planes : 2 * planes]
     east = turned_edge(east_ref[...].astype(jnp.float32), (4 - next_code) & 3)
     west = turned_edge(west_ref[...].astype(jnp.float32), own_code)
     fill = jnp.zeros((LANES - rows, planes), jnp.float32)
     tall = lambda line: jnp.transpose(jnp.concatenate([line, fill], axis=0))
-    east = tall(edge_term(east, weight_east[...], 1.0, 1, 2))
-    west = tall(edge_term(west, weight_west[...], -1.0, 1, 2))
-    north = edge_term(north_ref[...].astype(jnp.float32), weight_north[...], 1.0, 0, 3)
-    south = edge_term(south_ref[...].astype(jnp.float32), weight_south[...], -1.0, 0, 3)
+    east = tall(edge_term(east, weight_east, 1.0, 1, 2))
+    west = tall(edge_term(west, weight_west, -1.0, 1, 2))
+    north = edge_term(north_ref[...].astype(jnp.float32), weight_north, 1.0, 0, 3)
+    south = edge_term(south_ref[...].astype(jnp.float32), weight_south, -1.0, 0, 3)
     lane = lax.broadcasted_iota(jnp.int32, (planes, LANES), 1)
     blank = jnp.zeros((planes, columns - 2 * LANES), jnp.float32)
     for c in range(rows):
@@ -347,53 +371,27 @@
 
 
 def finish_kernel(
-    seam_ref, got_hbm, heads_hbm, north_ref, south_ref, east_ref, west_ref, hor_hbm, coef_hbm,
-    weight_north_hbm, weight_south_hbm, weight_east_hbm, weight_west_hbm,
-    out_hbm, acc, out_ref, hor_ref, coef_ref,
-    weight_north, weight_south, weight_east, weight_west,
-    got_ref, heads_ref, head_f, row_line, column_line, sems, got_sems, out_sems,
+    seam_ref, got_ref, heads_ref, north_ref, south_ref, east_ref, west_ref, local_hbm,
+    out_hbm, acc, out_ref, hor_ref, coef_ref, weight_ref,
+    head_f, row_line, column_line, sems, out_sems,
 ):
     slots, width = got_ref.shape
-    tiles = heads_ref.shape[0]
+    tiles, pairs = heads_ref.shape[0], heads_ref.shape[1]
     capacity = slots // tiles - HEAD_ROWS
     levels, fields, rows, columns = out_ref.shape
     depth = slots // GATHER_BLOCKS
-    heads_copy = pltpu.make_async_copy(
-        heads_hbm.at[:, capacity // HEAD_ROWS], heads_ref, sems.at[6]
-    )
-    heads_copy.start()
-    for i in range(GATHER_BLOCKS):
-        span = pl.ds(i * depth, depth)
-        pltpu.make_async_copy(got_hbm.at[span], got_ref.at[span], got_sems.at[i]).start()
-    weight_copies = [
-        pltpu.make_async_copy(source, target, sems.at[i])
-        for i, (source, target) in enumerate(
-            (
-                (weight_north_hbm, weight_north),
-                (weight_south_hbm, weight_south),
-                (weight_east_hbm, weight_east),
-                (weight_west_hbm, weight_west),
-            )
-        )
-    ]
-    solve_copies = [
-        pltpu.make_async_copy(hor_hbm, hor_ref, sems.at[4]),
-        pltpu.make_async_copy(coef_hbm, coef_ref, sems.at[5]),
-    ]
-    for copy in weight_copies + solve_copies:
+    copies = local_copies(local_hbm, (hor_ref, coef_ref, weight_ref), sems, True)
+    for copy in copies[::-1]:
         copy.start()
     along_rank = lax.axis_index("along")
     own_code = seam_ref[along_rank]
     next_code = seam_ref[lax.rem(along_rank + 1, seam_ref.shape[0])]
-    for copy in weight_copies:
-        copy.wait()
+    copies[2].wait()
     start_with_edges(
-        acc, own_code, next_code, north_ref, south_ref, east_ref, west_ref,
-        weight_north, weight_south, weight_east, weight_west,
+        acc, own_code, next_code, north_ref, south_ref, east_ref, west_ref, weight_ref
     )
 
-    heads_copy.wait()
-    heads = heads_ref[...].astype(jnp.float32)
+    heads = heads_ref[:, pairs - 1].astype(jnp.float32)
     for i, line_ref in enumerate((row_line, column_line)):
         head_f[i] = heads[:, i, :]
         lane_order(head_f.at[i], line_ref, capacity)
@@ -402,7 +400,6 @@
 
     def gather(i, carried):
         span = pl.ds(pl.multiple_of(i * depth, depth), depth)
-        pltpu.make_async_copy(got_hbm.at[span], got_ref.at[span], got_sems.at[i]).wait()
         turned = jnp.transpose(got_ref[span, :])
         onehot = (column_id == column_line[:, span]).astype(jnp.float32).astype(jnp.bfloat16)
         row_wide = jnp.broadcast_to(row_line[:, span], (width, depth)).astype(jnp.bfloat16)
@@ -417,18 +414,18 @@
 
     lax.fori_loop(0, GATHER_BLOCKS, gather, 0)
 
-    for copy in solve_copies:
-        copy.wait()
+    copies[0].wait()
+    copies[1].wait()
 
     def forward(q, previous):
         forcing = jnp.swapaxes(acc[:, pl.ds(pl.multiple_of(q * 8, 8), 8), :], 0, 1)
         state = list(previous)
         for i in range(8 // fields):
             k = q * (8 // fields) + i
-            mask_inv, lower_inv = coef_ref[0, k], coef_ref[1, k]
+            mask_inv, lower_inv = coef_ref[k], coef_ref[levels + k]
             for f in range(fields):
                 state[f] = (
-                    hor_ref[k, f] + mask_inv * forcing[i * fields + f] + lower_inv * state[f]
+                    hor_ref[k * fields + f] + mask_inv * forcing[i * fields + f] + lower_inv * state[f]
                 )
                 out_ref[k, f] = state[f]
         return tuple(state)
@@ -438,7 +435,7 @@
 
     def backward(step, below):
         k = levels - 2 - step
-        ratio = coef_ref[2, k]
+        ratio = coef_ref[2 * levels + k]
         here = []
         for f in range(fields):
             here.append(out_ref[k, f] - ratio * below[f])
@@ -461,39 +458,32 @@
         copy.wait()
 
 
-def finish(seam_code, got, halos, local, tiles):
-    hor, coef, weights = local[0], local[1], local[2:]
+def finish(seam_code, got, halos, local, tiles, shape):
     slots, width = got.shape
     heads = got.reshape(tiles, slots // tiles // HEAD_ROWS, HEAD_ROWS, width)
-    levels, fields, rows, columns = hor.shape
-    planes = levels * fields
+    levels, fields, rows, columns = shape
     vmem = pl.BlockSpec(memory_space=pltpu.VMEM)
     hbm = pl.BlockSpec(memory_space=pltpu.HBM)
     return pl.pallas_call(
         finish_kernel,
-        out_shape=jax.ShapeDtypeStruct(hor.shape, jnp.float32),
-        in_specs=[pl.BlockSpec(memory_space=pltpu.SMEM)] + [hbm] * 2 + [vmem] * 4 + [hbm] * 6,
+        out_shape=jax.ShapeDtypeStruct(shape, jnp.float32),
+        in_specs=[pl.BlockSpec(memory_space=pltpu.SMEM)] + [vmem] * 6 + [hbm],
         out_specs=hbm,
         scratch_shapes=[
-            pltpu.VMEM((rows, planes, columns), jnp.float32),
-            pltpu.VMEM(hor.shape, jnp.float32),
-            pltpu.VMEM(hor.shape, jnp.float32),
-            pltpu.VMEM(coef.shape, jnp.float32),
+            pltpu.VMEM((rows, levels * fields, columns), jnp.float32),
+            pltpu.VMEM(shape, jnp.float32),
         ]
-        + [pltpu.VMEM(w.shape, jnp.float32) for w in weights]
+        + local_scratch(*shape)
         + [
-            pltpu.VMEM((slots, width), jnp.bfloat16),
-            pltpu.VMEM((tiles, HEAD_ROWS, width), jnp.bfloat16),
             pltpu.VMEM((2, tiles, LANES), jnp.float32),
             pltpu.VMEM((1, slots), jnp.float32),
             pltpu.VMEM((1, slots), jnp.float32),
-            pltpu.SemaphoreType.DMA((7,)),
-            pltpu.SemaphoreType.DMA((GATHER_BLOCKS,)),
+            pltpu.SemaphoreType.DMA((3,)),
             pltpu.SemaphoreType.DMA((PARTS,)),
         ],
-        compiler_params=pltpu.CompilerParams(vmem_limit_bytes=WIDE_VMEM_BYTES),
+        compiler_params=pltpu.CompilerParams(vmem_limit_bytes=LAST_VMEM_BYTES),
         name="finish",
-    )(seam_code, got, heads, *halos, hor, coef, *weights)
+    )(seam_code, got, heads, *halos, local)
 
 
 def per_device(adjoint, flow, land_mask, mixing, seam_code, obs_misfit, obs_owner, obs_cell):
@@ -519,7 +509,7 @@
     south = lax.ppermute(last_row, "cross", line_up)
     north = lax.ppermute(first_row, "cross", line_down)
     local = local_part(adjoint, flow, land_mask, mixing)
-    return finish(seam_code, got, (north, south, east, west), local, devices)
+    return finish(seam_code, got, (north, south, east, west), local, devices, adjoint.shape)
 
 
 def solution(mesh):

time: 65.7 us -> 65.2 us (level)
  Pallas kernels: 30.7 us -> 36.4 us
  local copies, waits for them, and re-layouts: 5.06 us -> 0.01 us
    unnamed x28 -> x2, local copies, waits for them, and re-layouts: 5.06 us -> 0.01 us
    pallas_call x2, Pallas kernels: 21.1 us -> 24.5 us  [the longest x1 14.5 us: finish(): pl.pallas_call(finish_kernel, out_shape=jax.ShapeDtypeStruct(shape, jnp.f...]
    pallas_call x1, Pallas kernels: 2.23 us -> 4.25 us  [edges(): pl.pallas_call(edge_kernel, out_shape=(row, row, side, side), in_specs=[v...]
  transfers between devices with their start and end apart: 5 -> 5, of which waited for: 2 -> 2; matrix products, arithmetic and copies ran while one was open for 0% -> 0% of each run, Pallas kernels for 13% -> 22%
where the time goes in v5:
time: 65.2 us; the launch traced here: 64.9 us
  Pallas kernels  36.4 us (56%)
  starting transfers between devices  24.6 us (38%)
  waiting for transfers between devices  3.87 us (6%)
    pallas_call x1, Pallas kernels, finish(): pl.pallas_call(finish_kernel, out_shape=jax.ShapeDtypeStruct(shape, jnp.f...  14.5 us
    all_to_all x1, starting transfers between devices, per_device(): lax.all_to_all(pairs, ('along', 'cross'), split_axis=0, concat_axis=0, ti...  11.5 us
    pallas_call x1, Pallas kernels, local_part(): pl.pallas_call(local_kernel, out_shape=jax.ShapeDtypeStruct((LOCAL_PLANES...  10 us
    pallas_call x1, Pallas kernels, pack_rows(): pl.pallas_call(functools.partial(pack_kernel, tiles=tiles), out_shape=jax...  7.62 us
    ppermute x1, starting transfers between devices, per_device(): east = lax.ppermute(first_column, 'along', ring_down)  5.76 us
    ppermute x1, starting transfers between devices, per_device(): south = lax.ppermute(last_row, 'cross', line_up)  4.38 us
    pallas_call x1, Pallas kernels, edges(): pl.pallas_call(edge_kernel, out_shape=(row, row, side, side), in_specs=[v...  4.25 us
    ppermute x1, starting transfers between devices, per_device(): north = lax.ppermute(first_row, 'cross', line_down)  2.96 us
  transfers between devices with their start and end apart: 5, of which 2 were waited for; matrix products, arithmetic and copies ran while one was open for 0% of the time, Pallas kernels for 22%

profile of v5, /device:TPU:1, one launch (start us, length us, event | category | flops | bytes accessed | tf_op | source)
XLA Modules:
  0.0 64.9 jit_solution(16114421924643304070)
XLA Ops:
  0.0 7.6 %pack_rows.1 = bf16[8448,128]{1,0:T(8,128)(2,1)} custom-call(s32[32,128]{1,0:T(8,128)} %bitcast.10, s32[32,128]{1,0:T(8,128)} %bitcast.11, bf16[4096,128]{1,0:T(8,128)(2,1)} %rows_hbm.1), custom_call_target="tpu_custom_call" | custom-call | tf_op jit(solution)/shard_map/pack_rows/pallas_call | solution.py:120
  7.6 11.5 %all-to-all-start = ((bf16[4224,2,128]{2,1,0:T(2,128)(2,1)}), bf16[4224,2,128]{2,1,0:T(2,128)(2,1)S(1)}, u32[]{:S(2)}, u32[]{:S(2)}) async-start(bf16[4224,2,128]{2,1,0:T(2,128)(2,1)} %bitcast.8), calls=%async_computation | async-start | bytes 4325376 | tf_op jit(solution)/shard_map/all_to_all | solution.py:499
  19.1 4.2 %edges.1 = (bf16[128,256]{1,0:T(8,128)(2,1)}, bf16[128,256]{1,0:T(8,128)(2,1)}, bf16[16,128]{1,0:T(8,128)(2,1)}, bf16[16,128]{1,0:T(8,128)(2,1)}) custom-call(f32[128,16,256]{2,1,0:T(8,128)} %bitcast.9), custom_call_target="tpu_custom_call" | custom-call | flops 1000 | bytes 100000 | tf_op jit(solution)/shard_map/edges/pallas_call | solution.py:165
  23.4 3.0 %collective-permute-start = (bf16[128,256]{1,0:T(8,128)(2,1)}, bf16[128,256]{1,0:T(8,128)(2,1)S(1)}, u32[]{:S(2)}, u32[]{:S(2)}) collective-permute-start(bf16[128,256]{1,0:T(8,128)(2,1)} %get-tuple-element.13), channel_id=1, source_target_pairs={{1,0},{2,1},{3,2},{5,4},{6,5},{7,6},{9,8},{10,9},{11,10},{13,12},{... | collective-permute-start | bytes 196616 | tf_op jit(solution)/shard_map/ppermute | solution.py:510
  26.4 4.4 %collective-permute-start.1 = (bf16[128,256]{1,0:T(8,128)(2,1)}, bf16[128,256]{1,0:T(8,128)(2,1)S(1)}, u32[]{:S(2)}, u32[]{:S(2)}) collective-permute-start(bf16[128,256]{1,0:T(8,128)(2,1)} %get-tuple-element.14), channel_id=1, source_target_pairs={{0,1},{1,2},{2,3},{4,5},{5,6},{6,7},{8,9},{9,10},{10,11},{12,13},{... | collective-permute-start | bytes 196616 | tf_op jit(solution)/shard_map/ppermute | solution.py:509
  30.7 5.8 %collective-permute-start.2 = (bf16[16,128]{1,0:T(8,128)(2,1)}, bf16[16,128]{1,0:T(8,128)(2,1)S(1)}, u32[]{:S(2)}, u32[]{:S(2)}) collective-permute-start(bf16[16,128]{1,0:T(8,128)(2,1)} %get-tuple-element.15), channel_id=1, source_target_pairs={{4,0},{8,4},{12,8},{16,12},{20,16},{24,20},{28,24},{32,28},{36,32}... | collective-permute-start | bytes 12296 | tf_op jit(solution)/shard_map/ppermute | solution.py:508
  36.5 0.0 copy-start
  36.5 0.0 collective-permute-start.3
  36.5 10.0 %local_part.1.local_hbm = f32[1536,16,256]{2,1,0:T(8,128)} custom-call(f32[32,4,16,256]{3,2,1,0:T(8,128)} %adj_ref, f32[32,2,16,256]{3,2,1,0:T(8,128)} %flow_ref.1, s32[32,16,256]{2,1,0:T(8,128)} %mask_ref.1, f32[31,16,256]{2,1,0:T(8,128)} %mix_ref.1), custom_call_target="tpu_custom_call" | custom-call | flops 1000 | bytes 100000 | tf_op jit(solution)/shard_map/local_part/pallas_call | solution.py:288
  46.5 0.0 collective-permute-done.2.east_ref
  46.5 1.8 %collective-permute-done.3.west_ref = bf16[16,128]{1,0:T(8,128)(2,1)S(1)} collective-permute-done((bf16[16,128]{1,0:T(8,128)(2,1)}, bf16[16,128]{1,0:T(8,128)(2,1)S(1)}, u32[]{:S(2)}, u32[]{:S(2)}) %collective-permute-start.3) | collective-permute-done | bytes 4128 | tf_op jit(solution)/shard_map/ppermute | solution.py:507
  48.4 0.0 collective-permute-done.north_ref
  48.4 0.0 collective-permute-done.1.south_ref
  48.4 2.0 %all-to-all-done = bf16[4224,2,128]{2,1,0:T(2,128)(2,1)S(1)} async-done(((bf16[4224,2,128]{2,1,0:T(2,128)(2,1)}), bf16[4224,2,128]{2,1,0:T(2,128)(2,1)S(1)}, u32[]{:S(2)}, u32[]{:S(2)}) %all-to-all-start) | async-done | bytes 2162720 | tf_op jit(solution)/shard_map/all_to_all | solution.py:499
  50.4 0.0 copy-done
  50.4 14.5 %finish.1 = f32[32,4,16,256]{3,2,1,0:T(8,128)} custom-call(s32[32]{0:T(128)S(1)} %copy-done, bf16[8448,128]{1,0:T(8,128)(2,1)S(1)} %bitcast.6, bf16[128,33,2,128]{3,2,1,0:T(2,128)(2,1)S(1)} %bitcast.7, bf16[128,256]{1,0:T(8,128)(2,1)S(1)} %collective-permute-done.north_ref, bf16[128,256]{1,0:T(8,128)(2,1)S(1)} %collective-permute-done.1.south_ref, ...), custom_call_target="tpu_custom_call" | custom-call | tf_op jit(solution)/shard_map/finish/pallas_call | solution.py:467
Async XLA Ops:
  7.6 42.8 %all-to-all-start = ((bf16[4224,2,128]{2,1,0:T(2,128)(2,1)}), bf16[4224,2,128]{2,1,0:T(2,128)(2,1)S(1)}, u32[]{:S(2)}, u32[]{:S(2)}) async-start(bf16[4224,2,128]{2,1,0:T(2,128)(2,1)} %bitcast.8), calls=%async_computation | async-start | bytes 4325376 | tf_op jit(solution)/shard_map/all_to_all | solution.py:499
  23.4 25.0 %collective-permute-start = (bf16[128,256]{1,0:T(8,128)(2,1)}, bf16[128,256]{1,0:T(8,128)(2,1)S(1)}, u32[]{:S(2)}, u32[]{:S(2)}) collective-permute-start(bf16[128,256]{1,0:T(8,128)(2,1)} %get-tuple-element.13), channel_id=1, source_target_pairs={{1,0},{2,1},{3,2},{5,4},{6,5},{7,6},{9,8},{10,9},{11,10},{13,12},{... | collective-permute-start | bytes 196616 | tf_op jit(solution)/shard_map/ppermute | solution.py:510
  26.4 22.0 %collective-permute-start.1 = (bf16[128,256]{1,0:T(8,128)(2,1)}, bf16[128,256]{1,0:T(8,128)(2,1)S(1)}, u32[]{:S(2)}, u32[]{:S(2)}) collective-permute-start(bf16[128,256]{1,0:T(8,128)(2,1)} %get-tuple-element.14), channel_id=1, source_target_pairs={{0,1},{1,2},{2,3},{4,5},{5,6},{6,7},{8,9},{9,10},{10,11},{12,13},{... | collective-permute-start | bytes 196616 | tf_op jit(solution)/shard_map/ppermute | solution.py:509
  30.7 15.8 %collective-permute-start.2 = (bf16[16,128]{1,0:T(8,128)(2,1)}, bf16[16,128]{1,0:T(8,128)(2,1)S(1)}, u32[]{:S(2)}, u32[]{:S(2)}) collective-permute-start(bf16[16,128]{1,0:T(8,128)(2,1)} %get-tuple-element.15), channel_id=1, source_target_pairs={{4,0},{8,4},{12,8},{16,12},{20,16},{24,20},{28,24},{32,28},{36,32}... | collective-permute-start | bytes 12296 | tf_op jit(solution)/shard_map/ppermute | solution.py:508
  36.5 13.9 %copy-start = (s32[32]{0:T(128)S(1)}, s32[32]{0:T(128)}, u32[]{:S(2)}) copy-start(s32[32]{0:T(128)} %seam_ref.1) | copy-start | bytes 388
  36.5 11.9 %collective-permute-start.3 = (bf16[16,128]{1,0:T(8,128)(2,1)}, bf16[16,128]{1,0:T(8,128)(2,1)S(1)}, u32[]{:S(2)}, u32[]{:S(2)}) collective-permute-start(bf16[16,128]{1,0:T(8,128)(2,1)} %get-tuple-element.16), channel_id=1, source_target_pairs={{0,4},{4,8},{8,12},{12,16},{16,20},{20,24},{24,28},{28,32},{32,36}... | collective-permute-start | bytes 12296 | tf_op jit(solution)/shard_map/ppermute | solution.py:507

commit v6 on v5

--- a/solution.py
+++ b/solution.py
@@ -16,8 +16,8 @@
 LANES = 128
 HEAD_ROWS = 2
 PARTS = 4
-CONVERT_AFTER = 16
 LAST_VMEM_BYTES = 44 * 1024 * 1024
+LOCAL_VMEM_BYTES = 50 * 1024 * 1024
 LOCAL_PLANES = 1536
 WIDE_VMEM_BYTES = 61 * 1024 * 1024
 
@@ -67,12 +67,6 @@
         total = total + lax.dot_general(
             hit_narrow, values, (((1,), (1,)), ((), ())), preferred_element_type=jnp.float32
         )
-        if b == CONVERT_AFTER:
-            rows_copy.wait()
-        if b >= CONVERT_AFTER:
-            share = rows_ref.shape[0] // (blocks - CONVERT_AFTER)
-            at = (b - CONVERT_AFTER) * share
-            rows_f[at : at + share, :] = rows_ref[at : at + share, :].astype(jnp.float32)
         if (b + 1) % half == 0:
             span = pl.ds(b + 1 - half, half)
             copy = pltpu.make_async_copy(
@@ -82,6 +76,8 @@
             slot_copies.append(copy)
     stage[pl.ds(capacity, tiles, stride=block_rows), :] = total[:, :LANES]
     stage[pl.ds(capacity + 1, tiles, stride=block_rows), :] = total[:, LANES:]
+    rows_copy.wait()
+    rows_f[...] = rows_ref[...].astype(jnp.float32)
 
     def scatter(b, carried):
         base = pl.multiple_of(b * LANES, LANES)
@@ -174,7 +170,7 @@
 
 
 def local_kernel(
-    adj_ref, flow_ref, mask_ref, mix_ref, local_hbm, hor_ref, coef_ref, weight_ref, sems,
+    adj_ref, flow_ref, mask_ref, mix_ref, local_hbm, weight_ref, hor_ref, coef_ref, sems,
 ):
     levels, fields, rows, columns = adj_ref.shape
     planes = levels * fields
@@ -256,7 +252,7 @@
 
     zero = jnp.zeros(shape, jnp.float32)
     lax.fori_loop(0, levels, level, (zero, zero))
-    copies = local_copies(local_hbm, (hor_ref, coef_ref, weight_ref), sems, False)
+    copies = local_copies(local_hbm, (hor_ref, coef_ref), sems, False)
     for copy in copies:
         copy.start()
     for copy in copies:
@@ -278,7 +274,6 @@
     return [
         pltpu.VMEM((planes, rows, columns), jnp.float32),
         pltpu.VMEM((3 * levels, rows, columns), jnp.float32),
-        pltpu.VMEM((2 * planes // rows + 1, rows, columns), jnp.float32),
     ]
 
 
@@ -287,11 +282,14 @@
     vmem = pl.BlockSpec(memory_space=pltpu.VMEM)
     return pl.pallas_call(
         local_kernel,
-        out_shape=jax.ShapeDtypeStruct((LOCAL_PLANES, rows, columns), jnp.float32),
+        out_shape=(
+            jax.ShapeDtypeStruct((LOCAL_PLANES, rows, columns), jnp.float32),
+            jax.ShapeDtypeStruct((2 * levels * fields // rows + 1, rows, columns), jnp.float32),
+        ),
         in_specs=[vmem] * 4,
-        out_specs=pl.BlockSpec(memory_space=pltpu.HBM),
-        scratch_shapes=local_scratch(*adjoint.shape) + [pltpu.SemaphoreType.DMA((3,))],
-        compiler_params=pltpu.CompilerParams(vmem_limit_bytes=WIDE_VMEM_BYTES),
+        out_specs=(pl.BlockSpec(memory_space=pltpu.HBM), vmem),
+        scratch_shapes=local_scratch(*adjoint.shape) + [pltpu.SemaphoreType.DMA((2,))],
+        compiler_params=pltpu.CompilerParams(vmem_limit_bytes=LOCAL_VMEM_BYTES),
         cost_estimate=pl.CostEstimate(flops=1000, bytes_accessed=100000, transcendentals=0),
         name="local_part",
     )(adjoint, flow, land_mask, mixing)
@@ -353,7 +351,7 @@
         acc[c] = line
 
 
-GATHER_BLOCKS = 3
+GATHER_BLOCKS = 1
 
 
 def lane_order(head_f, line_ref, capacity):
@@ -371,8 +369,8 @@
 
 
 def finish_kernel(
-    seam_ref, got_ref, heads_ref, north_ref, south_ref, east_ref, west_ref, local_hbm,
-    out_hbm, acc, out_ref, hor_ref, coef_ref, weight_ref,
+    seam_ref, got_ref, heads_ref, north_ref, south_ref, east_ref, west_ref, weight_ref, local_hbm,
+    out_hbm, acc, out_ref, hor_ref, coef_ref,
     head_f, row_line, column_line, sems, out_sems,
 ):
     slots, width = got_ref.shape
@@ -380,13 +378,12 @@
     capacity = slots // tiles - HEAD_ROWS
     levels, fields, rows, columns = out_ref.shape
     depth = slots // GATHER_BLOCKS
-    copies = local_copies(local_hbm, (hor_ref, coef_ref, weight_ref), sems, True)
-    for copy in copies[::-1]:
+    copies = local_copies(local_hbm, (hor_ref, coef_ref), sems, True)
+    for copy in copies:
         copy.start()
     along_rank = lax.axis_index("along")
     own_code = seam_ref[along_rank]
     next_code = seam_ref[lax.rem(along_rank + 1, seam_ref.shape[0])]
-    copies[2].wait()
     start_with_edges(
         acc, own_code, next_code, north_ref, south_ref, east_ref, west_ref, weight_ref
     )
@@ -458,7 +455,7 @@
         copy.wait()
 
 
-def finish(seam_code, got, halos, local, tiles, shape):
+def finish(seam_code, got, halos, weight, local, tiles, shape):
     slots, width = got.shape
     heads = got.reshape(tiles, slots // tiles // HEAD_ROWS, HEAD_ROWS, width)
     levels, fields, rows, columns = shape
@@ -467,7 +464,7 @@
     return pl.pallas_call(
         finish_kernel,
         out_shape=jax.ShapeDtypeStruct(shape, jnp.float32),
-        in_specs=[pl.BlockSpec(memory_space=pltpu.SMEM)] + [vmem] * 6 + [hbm],
+        in_specs=[pl.BlockSpec(memory_space=pltpu.SMEM)] + [vmem] * 7 + [hbm],
         out_specs=hbm,
         scratch_shapes=[
             pltpu.VMEM((rows, levels * fields, columns), jnp.float32),
@@ -478,12 +475,12 @@
             pltpu.VMEM((2, tiles, LANES), jnp.float32),
             pltpu.VMEM((1, slots), jnp.float32),
             pltpu.VMEM((1, slots), jnp.float32),
-            pltpu.SemaphoreType.DMA((3,)),
+            pltpu.SemaphoreType.DMA((2,)),
             pltpu.SemaphoreType.DMA((PARTS,)),
         ],
         compiler_params=pltpu.CompilerParams(vmem_limit_bytes=LAST_VMEM_BYTES),
         name="finish",
-    )(seam_code, got, heads, *halos, local)
+    )(seam_code, got, heads, *halos, weight, local)
 
 
 def per_device(adjoint, flow, land_mask, mixing, seam_code, obs_misfit, obs_owner, obs_cell):
@@ -508,8 +505,9 @@
     east = lax.ppermute(first_column, "along", ring_down)
     south = lax.ppermute(last_row, "cross", line_up)
     north = lax.ppermute(first_row, "cross", line_down)
-    local = local_part(adjoint, flow, land_mask, mixing)
-    return finish(seam_code, got, (north, south, east, west), local, devices, adjoint.shape)
+    local, weight = local_part(adjoint, flow, land_mask, mixing)
+    halos = (north, south, east, west)
+    return finish(seam_code, got, halos, weight, local, devices, adjoint.shape)
 
 
 def solution(mesh):

time: 65.2 us -> 63.6 us (0.975)
  Pallas kernels: 36.4 us -> 33.9 us
  local copies, waits for them, and re-layouts: 0.01 us -> 2.27 us
  waiting for transfers between devices: 3.87 us -> 2.09 us
    unnamed x2 -> x8, local copies, waits for them, and re-layouts: 0.01 us -> 2.27 us
    ppermute x1, waiting for transfers between devices: 1.85 us -> 0.07 us  [per_device(): west = lax.ppermute(last_column, 'along', ring_up)]
    pallas_call x1, Pallas kernels: 14.5 us -> 12.8 us  [finish(): pl.pallas_call(finish_kernel, out_shape=jax.ShapeDtypeStruct(shape, jnp.f...]
where the time goes in v6:
time: 63.6 us; the launch traced here: 63.2 us
  Pallas kernels  33.9 us (53%)
  starting transfers between devices  24.7 us (39%)
  local copies, waits for them, and re-layouts  2.27 us (4%)
  waiting for transfers between devices  2.09 us (3%)
    pallas_call x1, Pallas kernels, finish(): pl.pallas_call(finish_kernel, out_shape=jax.ShapeDtypeStruct(shape, jnp.f...  12.8 us
    all_to_all x1, starting transfers between devices, per_device(): lax.all_to_all(pairs, ('along', 'cross'), split_axis=0, concat_axis=0, ti...  11.5 us
    pallas_call x1, Pallas kernels, local_part(): pl.pallas_call(local_kernel, out_shape=(jax.ShapeDtypeStruct((LOCAL_PLANE...  9.39 us
    pallas_call x1, Pallas kernels, pack_rows(): pl.pallas_call(functools.partial(pack_kernel, tiles=tiles), out_shape=jax...  7.43 us
    ppermute x1, starting transfers between devices, per_device(): east = lax.ppermute(first_column, 'along', ring_down)  5.76 us
    ppermute x1, starting transfers between devices, per_device(): south = lax.ppermute(last_row, 'cross', line_up)  4.38 us
    pallas_call x1, Pallas kernels, edges(): pl.pallas_call(edge_kernel, out_shape=(row, row, side, side), in_specs=[v...  4.25 us
    ppermute x1, starting transfers between devices, per_device(): north = lax.ppermute(first_row, 'cross', line_down)  3.1 us
  transfers between devices with their start and end apart: 5, of which 2 were waited for; matrix products, arithmetic and copies ran while one was open for 0% of the time, Pallas kernels for 22%

profile of v6, /device:TPU:1, one launch (start us, length us, event | category | flops | bytes accessed | tf_op | source)
XLA Modules:
  0.0 63.2 jit_solution(15720637238078687895)
XLA Ops:
  0.0 7.4 %pack_rows.1 = bf16[8448,128]{1,0:T(8,128)(2,1)} custom-call(s32[32,128]{1,0:T(8,128)} %bitcast.10, s32[32,128]{1,0:T(8,128)} %bitcast.11, bf16[4096,128]{1,0:T(8,128)(2,1)} %rows_hbm.1), custom_call_target="tpu_custom_call" | custom-call | tf_op jit(solution)/shard_map/pack_rows/pallas_call | solution.py:116
  7.4 0.0 copy-start.1
  7.4 11.5 %all-to-all-start = ((bf16[4224,2,128]{2,1,0:T(2,128)(2,1)}), bf16[4224,2,128]{2,1,0:T(2,128)(2,1)S(1)}, u32[]{:S(2)}, u32[]{:S(2)}) async-start(bf16[4224,2,128]{2,1,0:T(2,128)(2,1)} %bitcast.8), calls=%async_computation | async-start | bytes 4325376 | tf_op jit(solution)/shard_map/all_to_all | solution.py:496
  19.0 4.2 %edges.1 = (bf16[128,256]{1,0:T(8,128)(2,1)}, bf16[128,256]{1,0:T(8,128)(2,1)}, bf16[16,128]{1,0:T(8,128)(2,1)}, bf16[16,128]{1,0:T(8,128)(2,1)}) custom-call(f32[128,16,256]{2,1,0:T(8,128)} %bitcast.9), custom_call_target="tpu_custom_call" | custom-call | flops 1000 | bytes 100000 | tf_op jit(solution)/shard_map/edges/pallas_call | solution.py:161
  23.2 0.0 copy-start.3
  23.2 3.1 %collective-permute-start = (bf16[128,256]{1,0:T(8,128)(2,1)}, bf16[128,256]{1,0:T(8,128)(2,1)S(1)}, u32[]{:S(2)}, u32[]{:S(2)}) collective-permute-start(bf16[128,256]{1,0:T(8,128)(2,1)} %get-tuple-element.15), channel_id=1, source_target_pairs={{1,0},{2,1},{3,2},{5,4},{6,5},{7,6},{9,8},{10,9},{11,10},{13,12},{... | collective-permute-start | bytes 196616 | tf_op jit(solution)/shard_map/ppermute | solution.py:507
  26.3 4.4 %collective-permute-start.1 = (bf16[128,256]{1,0:T(8,128)(2,1)}, bf16[128,256]{1,0:T(8,128)(2,1)S(1)}, u32[]{:S(2)}, u32[]{:S(2)}) collective-permute-start(bf16[128,256]{1,0:T(8,128)(2,1)} %get-tuple-element.16), channel_id=1, source_target_pairs={{0,1},{1,2},{2,3},{4,5},{5,6},{6,7},{8,9},{9,10},{10,11},{12,13},{... | collective-permute-start | bytes 196616 | tf_op jit(solution)/shard_map/ppermute | solution.py:506
  30.7 5.8 %collective-permute-start.2 = (bf16[16,128]{1,0:T(8,128)(2,1)}, bf16[16,128]{1,0:T(8,128)(2,1)S(1)}, u32[]{:S(2)}, u32[]{:S(2)}) collective-permute-start(bf16[16,128]{1,0:T(8,128)(2,1)} %get-tuple-element.17), channel_id=1, source_target_pairs={{4,0},{8,4},{12,8},{16,12},{20,16},{24,20},{28,24},{32,28},{36,32}... | collective-permute-start | bytes 12296 | tf_op jit(solution)/shard_map/ppermute | solution.py:505
  36.5 0.0 collective-permute-start.3
  36.5 0.0 copy-done.1
  36.5 0.0 copy-start
  36.5 1.2 %copy-done = f32[32,2,16,256]{3,2,1,0:T(8,128)S(1)} copy-done((f32[32,2,16,256]{3,2,1,0:T(8,128)S(1)}, f32[32,2,16,256]{3,2,1,0:T(8,128)}, u32[]{:S(2)}) %copy-start) | copy-done | bytes 1048600
  37.7 0.0 copy-start.2
  37.7 1.0 %copy-done.2 = f32[31,16,256]{2,1,0:T(8,128)S(1)} copy-done((f32[31,16,256]{2,1,0:T(8,128)S(1)}, f32[31,16,256]{2,1,0:T(8,128)}, u32[]{:S(2)}) %copy-start.2) | copy-done | bytes 507928
  38.7 9.4 %local_part.1 = (f32[1536,16,256]{2,1,0:T(8,128)}, f32[17,16,256]{2,1,0:T(8,128)S(1)}) custom-call(f32[32,4,16,256]{3,2,1,0:T(8,128)} %adj_ref, f32[32,2,16,256]{3,2,1,0:T(8,128)S(1)} %copy-done, s32[32,16,256]{2,1,0:T(8,128)S(1)} %copy-done.1, f32[31,16,256]{2,1,0:T(8,128)S(1)} %copy-done.2), custom_call_target="tpu_custom_call" | custom-call | flops 1000 | bytes 100000 | tf_op jit(solution)/shard_map/local_part/pallas_call | solution.py:283
  48.1 0.0 collective-permute-done.2.east_ref
  48.1 0.1 collective-permute-done.3.west_ref
  48.2 0.0 collective-permute-done.north_ref
  48.2 0.0 collective-permute-done.1.south_ref
  48.2 2.0 %all-to-all-done = bf16[4224,2,128]{2,1,0:T(2,128)(2,1)S(1)} async-done(((bf16[4224,2,128]{2,1,0:T(2,128)(2,1)}), bf16[4224,2,128]{2,1,0:T(2,128)(2,1)S(1)}, u32[]{:S(2)}, u32[]{:S(2)}) %all-to-all-start) | async-done | bytes 2162720 | tf_op jit(solution)/shard_map/all_to_all | solution.py:496
  50.2 0.0 copy-done.3
  50.2 12.8 %finish.1 = f32[32,4,16,256]{3,2,1,0:T(8,128)} custom-call(s32[32]{0:T(128)S(1)} %copy-done.3, bf16[8448,128]{1,0:T(8,128)(2,1)S(1)} %bitcast.6, bf16[128,33,2,128]{3,2,1,0:T(2,128)(2,1)S(1)} %bitcast.7, bf16[128,256]{1,0:T(8,128)(2,1)S(1)} %collective-permute-done.north_ref, bf16[128,256]{1,0:T(8,128)(2,1)S(1)} %collective-permute-done.1.south_ref, ...), custom_call_target="tpu_custom_call" | custom-call | tf_op jit(solution)/shard_map/finish/pallas_call | solution.py:464
Async XLA Ops:
  7.4 29.0 %copy-start.1 = (s32[32,16,256]{2,1,0:T(8,128)S(1)}, s32[32,16,256]{2,1,0:T(8,128)}, u32[]{:S(2)}) copy-start(s32[32,16,256]{2,1,0:T(8,128)} %mask_ref.1) | copy-start | bytes 1572868
  7.4 42.8 %all-to-all-start = ((bf16[4224,2,128]{2,1,0:T(2,128)(2,1)}), bf16[4224,2,128]{2,1,0:T(2,128)(2,1)S(1)}, u32[]{:S(2)}, u32[]{:S(2)}) async-start(bf16[4224,2,128]{2,1,0:T(2,128)(2,1)} %bitcast.8), calls=%async_computation | async-start | bytes 4325376 | tf_op jit(solution)/shard_map/all_to_all | solution.py:496
  23.2 27.0 %copy-start.3 = (s32[32]{0:T(128)S(1)}, s32[32]{0:T(128)}, u32[]{:S(2)}) copy-start(s32[32]{0:T(128)} %seam_ref.1) | copy-start | bytes 388
  23.2 25.0 %collective-permute-start = (bf16[128,256]{1,0:T(8,128)(2,1)}, bf16[128,256]{1,0:T(8,128)(2,1)S(1)}, u32[]{:S(2)}, u32[]{:S(2)}) collective-permute-start(bf16[128,256]{1,0:T(8,128)(2,1)} %get-tuple-element.15), channel_id=1, source_target_pairs={{1,0},{2,1},{3,2},{5,4},{6,5},{7,6},{9,8},{10,9},{11,10},{13,12},{... | collective-permute-start | bytes 196616 | tf_op jit(solution)/shard_map/ppermute | solution.py:507
  26.3 21.9 %collective-permute-start.1 = (bf16[128,256]{1,0:T(8,128)(2,1)}, bf16[128,256]{1,0:T(8,128)(2,1)S(1)}, u32[]{:S(2)}, u32[]{:S(2)}) collective-permute-start(bf16[128,256]{1,0:T(8,128)(2,1)} %get-tuple-element.16), channel_id=1, source_target_pairs={{0,1},{1,2},{2,3},{4,5},{5,6},{6,7},{8,9},{9,10},{10,11},{12,13},{... | collective-permute-start | bytes 196616 | tf_op jit(solution)/shard_map/ppermute | solution.py:506
  30.7 17.4 %collective-permute-start.2 = (bf16[16,128]{1,0:T(8,128)(2,1)}, bf16[16,128]{1,0:T(8,128)(2,1)S(1)}, u32[]{:S(2)}, u32[]{:S(2)}) collective-permute-start(bf16[16,128]{1,0:T(8,128)(2,1)} %get-tuple-element.17), channel_id=1, source_target_pairs={{4,0},{8,4},{12,8},{16,12},{20,16},{24,20},{28,24},{32,28},{36,32}... | collective-permute-start | bytes 12296 | tf_op jit(solution)/shard_map/ppermute | solution.py:505
  36.5 11.7 %collective-permute-start.3 = (bf16[16,128]{1,0:T(8,128)(2,1)}, bf16[16,128]{1,0:T(8,128)(2,1)S(1)}, u32[]{:S(2)}, u32[]{:S(2)}) collective-permute-start(bf16[16,128]{1,0:T(8,128)(2,1)} %get-tuple-element.18), channel_id=1, source_target_pairs={{0,4},{4,8},{8,12},{12,16},{16,20},{20,24},{24,28},{28,32},{32,36}... | collective-permute-start | bytes 12296 | tf_op jit(solution)/shard_map/ppermute | solution.py:504
  36.5 1.2 %copy-start = (f32[32,2,16,256]{3,2,1,0:T(8,128)S(1)}, f32[32,2,16,256]{3,2,1,0:T(8,128)}, u32[]{:S(2)}) copy-start(f32[32,2,16,256]{3,2,1,0:T(8,128)} %flow_ref.1) | copy-start | bytes 3145732
  37.7 1.0 %copy-start.2 = (f32[31,16,256]{2,1,0:T(8,128)S(1)}, f32[31,16,256]{2,1,0:T(8,128)}, u32[]{:S(2)}) copy-start(f32[31,16,256]{2,1,0:T(8,128)} %mix_ref.1) | copy-start | bytes 1523716

commit v7 on v6

--- a/solution.py
+++ b/solution.py
@@ -352,6 +352,7 @@
 
 
 GATHER_BLOCKS = 1
+ROW_PARTS = 2
 
 
 def lane_order(head_f, line_ref, capacity):
@@ -393,20 +394,26 @@
         head_f[i] = heads[:, i, :]
         lane_order(head_f.at[i], line_ref, capacity)
     column_id = lax.broadcasted_iota(jnp.int32, (columns, depth), 0).astype(jnp.float32)
+    column_id = column_id.astype(jnp.bfloat16)
     zero = jnp.zeros((width, depth), jnp.bfloat16)
 
     def gather(i, carried):
         span = pl.ds(pl.multiple_of(i * depth, depth), depth)
         turned = jnp.transpose(got_ref[span, :])
-        onehot = (column_id == column_line[:, span]).astype(jnp.float32).astype(jnp.bfloat16)
+        column_wide = jnp.broadcast_to(column_line[:, span], (columns, depth)).astype(jnp.bfloat16)
+        onehot = jnp.where(
+            column_id == column_wide, jnp.ones((), jnp.bfloat16), jnp.zeros((), jnp.bfloat16)
+        )
         row_wide = jnp.broadcast_to(row_line[:, span], (width, depth)).astype(jnp.bfloat16)
-        masked = jnp.concatenate(
-            [jnp.where(row_wide == (c + 1), turned, zero) for c in range(rows)], axis=0
-        )
-        part = lax.dot_general(
-            masked, onehot, (((1,), (1,)), ((), ())), preferred_element_type=jnp.float32
-        )
-        acc[...] += part.reshape(rows, width, columns)
+        for start in range(0, rows, rows // ROW_PARTS):
+            some = range(start, start + rows // ROW_PARTS)
+            masked = jnp.concatenate(
+                [jnp.where(row_wide == (c + 1), turned, zero) for c in some], axis=0
+            )
+            part = lax.dot_general(
+                masked, onehot, (((1,), (1,)), ((), ())), preferred_element_type=jnp.float32
+            )
+            acc[start : start + rows // ROW_PARTS] += part.reshape(rows // ROW_PARTS, width, columns)
         return carried
 
     lax.fori_loop(0, GATHER_BLOCKS, gather, 0)

time: 63.6 us -> 62.9 us (0.989)
  Pallas kernels: 33.9 us -> 33.2 us
    pallas_call x1, Pallas kernels: 12.8 us -> 12.1 us  [finish(): pl.pallas_call(finish_kernel, out_shape=jax.ShapeDtypeStruct(shape, jnp.f...]
where the time goes in v7:
time: 62.9 us; the launch traced here: 62.5 us
  Pallas kernels  33.2 us (53%)
  starting transfers between devices  24.7 us (39%)
  local copies, waits for them, and re-layouts  2.27 us (4%)
  waiting for transfers between devices  2.09 us (3%)
    pallas_call x1, Pallas kernels, finish(): pl.pallas_call(finish_kernel, out_shape=jax.ShapeDtypeStruct(shape, jnp.f...  12.1 us
    all_to_all x1, starting transfers between devices, per_device(): lax.all_to_all(pairs, ('along', 'cross'), split_axis=0, concat_axis=0, ti...  11.5 us
    pallas_call x1, Pallas kernels, local_part(): pl.pallas_call(local_kernel, out_shape=(jax.ShapeDtypeStruct((LOCAL_PLANE...  9.39 us
    pallas_call x1, Pallas kernels, pack_rows(): pl.pallas_call(functools.partial(pack_kernel, tiles=tiles), out_shape=jax...  7.43 us
    ppermute x1, starting transfers between devices, per_device(): east = lax.ppermute(first_column, 'along', ring_down)  5.76 us
    ppermute x1, starting transfers between devices, per_device(): south = lax.ppermute(last_row, 'cross', line_up)  4.38 us
    pallas_call x1, Pallas kernels, edges(): pl.pallas_call(edge_kernel, out_shape=(row, row, side, side), in_specs=[v...  4.25 us
    ppermute x1, starting transfers between devices, per_device(): north = lax.ppermute(first_row, 'cross', line_down)  3.1 us
  transfers between devices with their start and end apart: 5, of which 2 were waited for; matrix products, arithmetic and copies ran while one was open for 0% of the time, Pallas kernels for 22%

profile of v7, /device:TPU:1, one launch (start us, length us, event | category | flops | bytes accessed | tf_op | source)
XLA Modules:
  0.0 62.5 jit_solution(3639294891214034757)
XLA Ops:
  0.0 7.4 %pack_rows.1 = bf16[8448,128]{1,0:T(8,128)(2,1)} custom-call(s32[32,128]{1,0:T(8,128)} %bitcast.10, s32[32,128]{1,0:T(8,128)} %bitcast.11, bf16[4096,128]{1,0:T(8,128)(2,1)} %rows_hbm.1), custom_call_target="tpu_custom_call" | custom-call | tf_op jit(solution)/shard_map/pack_rows/pallas_call | solution.py:116
  7.4 0.0 copy-start.1
  7.4 11.5 %all-to-all-start = ((bf16[4224,2,128]{2,1,0:T(2,128)(2,1)}), bf16[4224,2,128]{2,1,0:T(2,128)(2,1)S(1)}, u32[]{:S(2)}, u32[]{:S(2)}) async-start(bf16[4224,2,128]{2,1,0:T(2,128)(2,1)} %bitcast.8), calls=%async_computation | async-start | bytes 4325376 | tf_op jit(solution)/shard_map/all_to_all | solution.py:503
  19.0 4.2 %edges.1 = (bf16[128,256]{1,0:T(8,128)(2,1)}, bf16[128,256]{1,0:T(8,128)(2,1)}, bf16[16,128]{1,0:T(8,128)(2,1)}, bf16[16,128]{1,0:T(8,128)(2,1)}) custom-call(f32[128,16,256]{2,1,0:T(8,128)} %bitcast.9), custom_call_target="tpu_custom_call" | custom-call | flops 1000 | bytes 100000 | tf_op jit(solution)/shard_map/edges/pallas_call | solution.py:161
  23.2 0.0 copy-start.3
  23.2 3.1 %collective-permute-start = (bf16[128,256]{1,0:T(8,128)(2,1)}, bf16[128,256]{1,0:T(8,128)(2,1)S(1)}, u32[]{:S(2)}, u32[]{:S(2)}) collective-permute-start(bf16[128,256]{1,0:T(8,128)(2,1)} %get-tuple-element.15), channel_id=1, source_target_pairs={{1,0},{2,1},{3,2},{5,4},{6,5},{7,6},{9,8},{10,9},{11,10},{13,12},{... | collective-permute-start | bytes 196616 | tf_op jit(solution)/shard_map/ppermute | solution.py:514
  26.3 4.4 %collective-permute-start.1 = (bf16[128,256]{1,0:T(8,128)(2,1)}, bf16[128,256]{1,0:T(8,128)(2,1)S(1)}, u32[]{:S(2)}, u32[]{:S(2)}) collective-permute-start(bf16[128,256]{1,0:T(8,128)(2,1)} %get-tuple-element.16), channel_id=1, source_target_pairs={{0,1},{1,2},{2,3},{4,5},{5,6},{6,7},{8,9},{9,10},{10,11},{12,13},{... | collective-permute-start | bytes 196616 | tf_op jit(solution)/shard_map/ppermute | solution.py:513
  30.7 5.8 %collective-permute-start.2 = (bf16[16,128]{1,0:T(8,128)(2,1)}, bf16[16,128]{1,0:T(8,128)(2,1)S(1)}, u32[]{:S(2)}, u32[]{:S(2)}) collective-permute-start(bf16[16,128]{1,0:T(8,128)(2,1)} %get-tuple-element.17), channel_id=1, source_target_pairs={{4,0},{8,4},{12,8},{16,12},{20,16},{24,20},{28,24},{32,28},{36,32}... | collective-permute-start | bytes 12296 | tf_op jit(solution)/shard_map/ppermute | solution.py:512
  36.5 0.0 collective-permute-start.3
  36.5 0.0 copy-done.1
  36.5 0.0 copy-start
  36.5 1.2 %copy-done = f32[32,2,16,256]{3,2,1,0:T(8,128)S(1)} copy-done((f32[32,2,16,256]{3,2,1,0:T(8,128)S(1)}, f32[32,2,16,256]{3,2,1,0:T(8,128)}, u32[]{:S(2)}) %copy-start) | copy-done | bytes 1048600
  37.7 0.0 copy-start.2
  37.7 1.0 %copy-done.2 = f32[31,16,256]{2,1,0:T(8,128)S(1)} copy-done((f32[31,16,256]{2,1,0:T(8,128)S(1)}, f32[31,16,256]{2,1,0:T(8,128)}, u32[]{:S(2)}) %copy-start.2) | copy-done | bytes 507928
  38.7 9.4 %local_part.1 = (f32[1536,16,256]{2,1,0:T(8,128)}, f32[17,16,256]{2,1,0:T(8,128)S(1)}) custom-call(f32[32,4,16,256]{3,2,1,0:T(8,128)} %adj_ref, f32[32,2,16,256]{3,2,1,0:T(8,128)S(1)} %copy-done, s32[32,16,256]{2,1,0:T(8,128)S(1)} %copy-done.1, f32[31,16,256]{2,1,0:T(8,128)S(1)} %copy-done.2), custom_call_target="tpu_custom_call" | custom-call | flops 1000 | bytes 100000 | tf_op jit(solution)/shard_map/local_part/pallas_call | solution.py:283
  48.1 0.0 collective-permute-done.2.east_ref
  48.1 0.1 collective-permute-done.3.west_ref
  48.2 0.0 collective-permute-done.north_ref
  48.2 0.0 collective-permute-done.1.south_ref
  48.2 2.0 %all-to-all-done = bf16[4224,2,128]{2,1,0:T(2,128)(2,1)S(1)} async-done(((bf16[4224,2,128]{2,1,0:T(2,128)(2,1)}), bf16[4224,2,128]{2,1,0:T(2,128)(2,1)S(1)}, u32[]{:S(2)}, u32[]{:S(2)}) %all-to-all-start) | async-done | bytes 2162720 | tf_op jit(solution)/shard_map/all_to_all | solution.py:503
  50.2 0.0 copy-done.3
  50.2 12.1 %finish.1 = f32[32,4,16,256]{3,2,1,0:T(8,128)} custom-call(s32[32]{0:T(128)S(1)} %copy-done.3, bf16[8448,128]{1,0:T(8,128)(2,1)S(1)} %bitcast.6, bf16[128,33,2,128]{3,2,1,0:T(2,128)(2,1)S(1)} %bitcast.7, bf16[128,256]{1,0:T(8,128)(2,1)S(1)} %collective-permute-done.north_ref, bf16[128,256]{1,0:T(8,128)(2,1)S(1)} %collective-permute-done.1.south_ref, ...), custom_call_target="tpu_custom_call" | custom-call | tf_op jit(solution)/shard_map/finish/pallas_call | solution.py:471
Async XLA Ops:
  7.4 29.0 %copy-start.1 = (s32[32,16,256]{2,1,0:T(8,128)S(1)}, s32[32,16,256]{2,1,0:T(8,128)}, u32[]{:S(2)}) copy-start(s32[32,16,256]{2,1,0:T(8,128)} %mask_ref.1) | copy-start | bytes 1572868
  7.4 42.8 %all-to-all-start = ((bf16[4224,2,128]{2,1,0:T(2,128)(2,1)}), bf16[4224,2,128]{2,1,0:T(2,128)(2,1)S(1)}, u32[]{:S(2)}, u32[]{:S(2)}) async-start(bf16[4224,2,128]{2,1,0:T(2,128)(2,1)} %bitcast.8), calls=%async_computation | async-start | bytes 4325376 | tf_op jit(solution)/shard_map/all_to_all | solution.py:503
  23.2 27.0 %copy-start.3 = (s32[32]{0:T(128)S(1)}, s32[32]{0:T(128)}, u32[]{:S(2)}) copy-start(s32[32]{0:T(128)} %seam_ref.1) | copy-start | bytes 388
  23.2 25.0 %collective-permute-start = (bf16[128,256]{1,0:T(8,128)(2,1)}, bf16[128,256]{1,0:T(8,128)(2,1)S(1)}, u32[]{:S(2)}, u32[]{:S(2)}) collective-permute-start(bf16[128,256]{1,0:T(8,128)(2,1)} %get-tuple-element.15), channel_id=1, source_target_pairs={{1,0},{2,1},{3,2},{5,4},{6,5},{7,6},{9,8},{10,9},{11,10},{13,12},{... | collective-permute-start | bytes 196616 | tf_op jit(solution)/shard_map/ppermute | solution.py:514
  26.3 21.9 %collective-permute-start.1 = (bf16[128,256]{1,0:T(8,128)(2,1)}, bf16[128,256]{1,0:T(8,128)(2,1)S(1)}, u32[]{:S(2)}, u32[]{:S(2)}) collective-permute-start(bf16[128,256]{1,0:T(8,128)(2,1)} %get-tuple-element.16), channel_id=1, source_target_pairs={{0,1},{1,2},{2,3},{4,5},{5,6},{6,7},{8,9},{9,10},{10,11},{12,13},{... | collective-permute-start | bytes 196616 | tf_op jit(solution)/shard_map/ppermute | solution.py:513
  30.7 17.4 %collective-permute-start.2 = (bf16[16,128]{1,0:T(8,128)(2,1)}, bf16[16,128]{1,0:T(8,128)(2,1)S(1)}, u32[]{:S(2)}, u32[]{:S(2)}) collective-permute-start(bf16[16,128]{1,0:T(8,128)(2,1)} %get-tuple-element.17), channel_id=1, source_target_pairs={{4,0},{8,4},{12,8},{16,12},{20,16},{24,20},{28,24},{32,28},{36,32}... | collective-permute-start | bytes 12296 | tf_op jit(solution)/shard_map/ppermute | solution.py:512
  36.5 11.7 %collective-permute-start.3 = (bf16[16,128]{1,0:T(8,128)(2,1)}, bf16[16,128]{1,0:T(8,128)(2,1)S(1)}, u32[]{:S(2)}, u32[]{:S(2)}) collective-permute-start(bf16[16,128]{1,0:T(8,128)(2,1)} %get-tuple-element.18), channel_id=1, source_target_pairs={{0,4},{4,8},{8,12},{12,16},{16,20},{20,24},{24,28},{28,32},{32,36}... | collective-permute-start | bytes 12296 | tf_op jit(solution)/shard_map/ppermute | solution.py:511
  36.5 1.2 %copy-start = (f32[32,2,16,256]{3,2,1,0:T(8,128)S(1)}, f32[32,2,16,256]{3,2,1,0:T(8,128)}, u32[]{:S(2)}) copy-start(f32[32,2,16,256]{3,2,1,0:T(8,128)} %flow_ref.1) | copy-start | bytes 3145732
  37.7 1.0 %copy-start.2 = (f32[31,16,256]{2,1,0:T(8,128)S(1)}, f32[31,16,256]{2,1,0:T(8,128)}, u32[]{:S(2)}) copy-start(f32[31,16,256]{2,1,0:T(8,128)} %mix_ref.1) | copy-start | bytes 1523716

commit v8 on v7

--- a/solution.py
+++ b/solution.py
@@ -170,7 +170,7 @@
 
 
 def local_kernel(
-    adj_ref, flow_ref, mask_ref, mix_ref, local_hbm, weight_ref, hor_ref, coef_ref, sems,
+    seam_ref, adj_ref, flow_ref, mask_ref, mix_ref, local_hbm, weight_ref, hor_ref, coef_ref, sems,
 ):
     levels, fields, rows, columns = adj_ref.shape
     planes = levels * fields
@@ -187,6 +187,13 @@
         == lax.broadcasted_iota(jnp.int32, (levels, planes), 0)
     ).astype(jnp.float32)
     row_planes = planes // rows
+    along_rank = lax.axis_index("along")
+    own_code = seam_ref[along_rank]
+    next_code = seam_ref[lax.rem(along_rank + 1, seam_ref.shape[0])]
+    for place, code in ((0, (4 - next_code) & 3), (planes, own_code)):
+        weight_ref[2 * row_planes + 1, :, place : place + planes] = jnp.full(
+            (rows, planes), code.astype(jnp.float32)
+        )
     for place, start, at, half in ((0, columns - LANES, LANES - 1, 0.5), (planes, 0, 0, -0.5)):
         line = jnp.zeros((rows, levels), jnp.float32)
         for r in range(rows):
@@ -277,22 +284,22 @@
     ]
 
 
-def local_part(adjoint, flow, land_mask, mixing):
+def local_part(seam_code, adjoint, flow, land_mask, mixing):
     levels, fields, rows, columns = adjoint.shape
     vmem = pl.BlockSpec(memory_space=pltpu.VMEM)
     return pl.pallas_call(
         local_kernel,
         out_shape=(
             jax.ShapeDtypeStruct((LOCAL_PLANES, rows, columns), jnp.float32),
-            jax.ShapeDtypeStruct((2 * levels * fields // rows + 1, rows, columns), jnp.float32),
+            jax.ShapeDtypeStruct((2 * levels * fields // rows + 2, rows, columns), jnp.float32),
         ),
-        in_specs=[vmem] * 4,
+        in_specs=[pl.BlockSpec(memory_space=pltpu.SMEM)] + [vmem] * 4,
         out_specs=(pl.BlockSpec(memory_space=pltpu.HBM), vmem),
         scratch_shapes=local_scratch(*adjoint.shape) + [pltpu.SemaphoreType.DMA((2,))],
         compiler_params=pltpu.CompilerParams(vmem_limit_bytes=LOCAL_VMEM_BYTES),
         cost_estimate=pl.CostEstimate(flops=1000, bytes_accessed=100000, transcendentals=0),
         name="local_part",
-    )(adjoint, flow, land_mask, mixing)
+    )(seam_code, adjoint, flow, land_mask, mixing)
 
 
 def turned_edge(edge, code):
@@ -320,7 +327,7 @@
 
 
 def start_with_edges(
-    acc, own_code, next_code, north_ref, south_ref, east_ref, west_ref, weight_ref
+    acc, north_ref, south_ref, east_ref, west_ref, weight_ref
 ):
     rows, planes, columns = acc.shape
     row_planes = planes // rows
@@ -328,8 +335,10 @@
     weight_south = weight_ref[row_planes : 2 * row_planes].reshape(planes, columns)
     weight_east = weight_ref[2 * row_planes, :, 0:planes]
     weight_west = weight_ref[2 * row_planes, :, planes : 2 * planes]
-    east = turned_edge(east_ref[...].astype(jnp.float32), (4 - next_code) & 3)
-    west = turned_edge(west_ref[...].astype(jnp.float32), own_code)
+    east = turned_edge(east_ref[...].astype(jnp.float32), weight_ref[2 * row_planes + 1, :, 0:planes])
+    west = turned_edge(
+        west_ref[...].astype(jnp.float32), weight_ref[2 * row_planes + 1, :, planes : 2 * planes]
+    )
     fill = jnp.zeros((LANES - rows, planes), jnp.float32)
     tall = lambda line: jnp.transpose(jnp.concatenate([line, fill], axis=0))
     east = tall(edge_term(east, weight_east, 1.0, 1, 2))
@@ -370,7 +379,7 @@
 
 
 def finish_kernel(
-    seam_ref, got_ref, heads_ref, north_ref, south_ref, east_ref, west_ref, weight_ref, local_hbm,
+    got_ref, heads_ref, north_ref, south_ref, east_ref, west_ref, weight_ref, local_hbm,
     out_hbm, acc, out_ref, hor_ref, coef_ref,
     head_f, row_line, column_line, sems, out_sems,
 ):
@@ -382,11 +391,8 @@
     copies = local_copies(local_hbm, (hor_ref, coef_ref), sems, True)
     for copy in copies:
         copy.start()
-    along_rank = lax.axis_index("along")
-    own_code = seam_ref[along_rank]
-    next_code = seam_ref[lax.rem(along_rank + 1, seam_ref.shape[0])]
     start_with_edges(
-        acc, own_code, next_code, north_ref, south_ref, east_ref, west_ref, weight_ref
+        acc, north_ref, south_ref, east_ref, west_ref, weight_ref
     )
 
     heads = heads_ref[:, pairs - 1].astype(jnp.float32)
@@ -462,7 +468,7 @@
         copy.wait()
 
 
-def finish(seam_code, got, halos, weight, local, tiles, shape):
+def finish(got, halos, weight, local, tiles, shape):
     slots, width = got.shape
     heads = got.reshape(tiles, slots // tiles // HEAD_ROWS, HEAD_ROWS, width)
     levels, fields, rows, columns = shape
@@ -471,7 +477,7 @@
     return pl.pallas_call(
         finish_kernel,
         out_shape=jax.ShapeDtypeStruct(shape, jnp.float32),
-        in_specs=[pl.BlockSpec(memory_space=pltpu.SMEM)] + [vmem] * 7 + [hbm],
+        in_specs=[vmem] * 7 + [hbm],
         out_specs=hbm,
         scratch_shapes=[
             pltpu.VMEM((rows, levels * fields, columns), jnp.float32),
@@ -487,7 +493,7 @@
         ],
         compiler_params=pltpu.CompilerParams(vmem_limit_bytes=LAST_VMEM_BYTES),
         name="finish",
-    )(seam_code, got, heads, *halos, weight, local)
+    )(got, heads, *halos, weight, local)
 
 
 def per_device(adjoint, flow, land_mask, mixing, seam_code, obs_misfit, obs_owner, obs_cell):
@@ -512,9 +518,9 @@
     east = lax.ppermute(first_column, "along", ring_down)
     south = lax.ppermute(last_row, "cross", line_up)
     north = lax.ppermute(first_row, "cross", line_down)
-    local, weight = local_part(adjoint, flow, land_mask, mixing)
+    local, weight = local_part(seam_code, adjoint, flow, land_mask, mixing)
     halos = (north, south, east, west)
-    return finish(seam_code, got, halos, weight, local, devices, adjoint.shape)
+    return finish(got, halos, weight, local, devices, adjoint.shape)
 
 
 def solution(mesh):

time: 62.9 us -> 63.2 us (level)
  no operation moved by 1% of the time
where the time goes in v8:
time: 63.2 us; the launch traced here: 62.8 us
  Pallas kernels  33.5 us (53%)
  starting transfers between devices  24.6 us (39%)
  local copies, waits for them, and re-layouts  2.27 us (4%)
  waiting for transfers between devices  2.26 us (4%)
    pallas_call x1, Pallas kernels, finish(): pl.pallas_call(finish_kernel, out_shape=jax.ShapeDtypeStruct(shape, jnp.f...  12.4 us
    all_to_all x1, starting transfers between devices, per_device(): lax.all_to_all(pairs, ('along', 'cross'), split_axis=0, concat_axis=0, ti...  11.5 us
    pallas_call x1, Pallas kernels, local_part(): pl.pallas_call(local_kernel, out_shape=(jax.ShapeDtypeStruct((LOCAL_PLANE...  9.35 us
    pallas_call x1, Pallas kernels, pack_rows(): pl.pallas_call(functools.partial(pack_kernel, tiles=tiles), out_shape=jax...  7.43 us
    ppermute x1, starting transfers between devices, per_device(): east = lax.ppermute(first_column, 'along', ring_down)  5.76 us
    ppermute x1, starting transfers between devices, per_device(): south = lax.ppermute(last_row, 'cross', line_up)  4.38 us
    pallas_call x1, Pallas kernels, edges(): pl.pallas_call(edge_kernel, out_shape=(row, row, side, side), in_specs=[v...  4.25 us
    ppermute x1, starting transfers between devices, per_device(): north = lax.ppermute(first_row, 'cross', line_down)  2.96 us
  transfers between devices with their start and end apart: 5, of which 2 were waited for; matrix products, arithmetic and copies ran while one was open for 0% of the time, Pallas kernels for 22%

profile of v8, /device:TPU:1, one launch (start us, length us, event | category | flops | bytes accessed | tf_op | source)
XLA Modules:
  0.0 62.8 jit_solution(14985411769936750216)
XLA Ops:
  0.0 7.4 %pack_rows.1 = bf16[8448,128]{1,0:T(8,128)(2,1)} custom-call(s32[32,128]{1,0:T(8,128)} %bitcast.10, s32[32,128]{1,0:T(8,128)} %bitcast.11, bf16[4096,128]{1,0:T(8,128)(2,1)} %rows_hbm.1), custom_call_target="tpu_custom_call" | custom-call | tf_op jit(solution)/shard_map/pack_rows/pallas_call | solution.py:116
  7.4 0.0 copy-start.1
  7.4 0.0 copy-start.3
  7.5 11.5 %all-to-all-start = ((bf16[4224,2,128]{2,1,0:T(2,128)(2,1)}), bf16[4224,2,128]{2,1,0:T(2,128)(2,1)S(1)}, u32[]{:S(2)}, u32[]{:S(2)}) async-start(bf16[4224,2,128]{2,1,0:T(2,128)(2,1)} %bitcast.8), calls=%async_computation | async-start | bytes 4325376 | tf_op jit(solution)/shard_map/all_to_all | solution.py:509
  19.0 4.2 %edges.1 = (bf16[128,256]{1,0:T(8,128)(2,1)}, bf16[128,256]{1,0:T(8,128)(2,1)}, bf16[16,128]{1,0:T(8,128)(2,1)}, bf16[16,128]{1,0:T(8,128)(2,1)}) custom-call(f32[128,16,256]{2,1,0:T(8,128)} %bitcast.9), custom_call_target="tpu_custom_call" | custom-call | flops 1000 | bytes 100000 | tf_op jit(solution)/shard_map/edges/pallas_call | solution.py:161
  23.2 3.0 %collective-permute-start = (bf16[128,256]{1,0:T(8,128)(2,1)}, bf16[128,256]{1,0:T(8,128)(2,1)S(1)}, u32[]{:S(2)}, u32[]{:S(2)}) collective-permute-start(bf16[128,256]{1,0:T(8,128)(2,1)} %get-tuple-element.15), channel_id=1, source_target_pairs={{1,0},{2,1},{3,2},{5,4},{6,5},{7,6},{9,8},{10,9},{11,10},{13,12},{... | collective-permute-start | bytes 196616 | tf_op jit(solution)/shard_map/ppermute | solution.py:520
  26.2 4.4 %collective-permute-start.1 = (bf16[128,256]{1,0:T(8,128)(2,1)}, bf16[128,256]{1,0:T(8,128)(2,1)S(1)}, u32[]{:S(2)}, u32[]{:S(2)}) collective-permute-start(bf16[128,256]{1,0:T(8,128)(2,1)} %get-tuple-element.16), channel_id=1, source_target_pairs={{0,1},{1,2},{2,3},{4,5},{5,6},{6,7},{8,9},{9,10},{10,11},{12,13},{... | collective-permute-start | bytes 196616 | tf_op jit(solution)/shard_map/ppermute | solution.py:519
  30.6 5.8 %collective-permute-start.2 = (bf16[16,128]{1,0:T(8,128)(2,1)}, bf16[16,128]{1,0:T(8,128)(2,1)S(1)}, u32[]{:S(2)}, u32[]{:S(2)}) collective-permute-start(bf16[16,128]{1,0:T(8,128)(2,1)} %get-tuple-element.17), channel_id=1, source_target_pairs={{4,0},{8,4},{12,8},{16,12},{20,16},{24,20},{28,24},{32,28},{36,32}... | collective-permute-start | bytes 12296 | tf_op jit(solution)/shard_map/ppermute | solution.py:518
  36.3 0.0 collective-permute-start.3
  36.3 0.0 copy-done.1
  36.3 0.0 copy-done.3
  36.4 0.0 copy-start
  36.4 1.2 %copy-done = f32[32,2,16,256]{3,2,1,0:T(8,128)S(1)} copy-done((f32[32,2,16,256]{3,2,1,0:T(8,128)S(1)}, f32[32,2,16,256]{3,2,1,0:T(8,128)}, u32[]{:S(2)}) %copy-start) | copy-done | bytes 1048600
  37.6 0.0 copy-start.2
  37.6 1.0 %copy-done.2 = f32[31,16,256]{2,1,0:T(8,128)S(1)} copy-done((f32[31,16,256]{2,1,0:T(8,128)S(1)}, f32[31,16,256]{2,1,0:T(8,128)}, u32[]{:S(2)}) %copy-start.2) | copy-done | bytes 507928
  38.6 9.3 %local_part.1 = (f32[1536,16,256]{2,1,0:T(8,128)}, f32[18,16,256]{2,1,0:T(8,128)S(1)}) custom-call(s32[32]{0:T(128)S(1)} %copy-done.3, f32[32,4,16,256]{3,2,1,0:T(8,128)} %adj_ref, f32[32,2,16,256]{3,2,1,0:T(8,128)S(1)} %copy-done, s32[32,16,256]{2,1,0:T(8,128)S(1)} %copy-done.1, f32[31,16,256]{2,1,0:T(8,128)S(1)} %copy-done.2), custom_call_target="tpu_custom_call" | custom-call | flops 1000 | bytes 100000 | tf_op jit(solution)/shard_map/local_part/pallas_call | solution.py:290
  48.0 0.0 collective-permute-done.2.east_ref
  48.0 0.2 collective-permute-done.3.west_ref
  48.2 0.0 collective-permute-done.north_ref
  48.2 0.0 collective-permute-done.1.south_ref
  48.2 2.0 %all-to-all-done = bf16[4224,2,128]{2,1,0:T(2,128)(2,1)S(1)} async-done(((bf16[4224,2,128]{2,1,0:T(2,128)(2,1)}), bf16[4224,2,128]{2,1,0:T(2,128)(2,1)S(1)}, u32[]{:S(2)}, u32[]{:S(2)}) %all-to-all-start) | async-done | bytes 2162720 | tf_op jit(solution)/shard_map/all_to_all | solution.py:509
  50.2 12.4 %finish.1 = f32[32,4,16,256]{3,2,1,0:T(8,128)} custom-call(bf16[8448,128]{1,0:T(8,128)(2,1)S(1)} %bitcast.6, bf16[128,33,2,128]{3,2,1,0:T(2,128)(2,1)S(1)} %bitcast.7, bf16[128,256]{1,0:T(8,128)(2,1)S(1)} %collective-permute-done.north_ref, bf16[128,256]{1,0:T(8,128)(2,1)S(1)} %collective-permute-done.1.south_ref, ...), custom_call_target="tpu_custom_call" | custom-call | tf_op jit(solution)/shard_map/finish/pallas_call | solution.py:477
Async XLA Ops:
  7.4 28.9 %copy-start.1 = (s32[32,16,256]{2,1,0:T(8,128)S(1)}, s32[32,16,256]{2,1,0:T(8,128)}, u32[]{:S(2)}) copy-start(s32[32,16,256]{2,1,0:T(8,128)} %mask_ref.1) | copy-start | bytes 1572868
  7.4 28.9 %copy-start.3 = (s32[32]{0:T(128)S(1)}, s32[32]{0:T(128)}, u32[]{:S(2)}) copy-start(s32[32]{0:T(128)} %seam_ref.1) | copy-start | bytes 388
  7.5 42.8 %all-to-all-start = ((bf16[4224,2,128]{2,1,0:T(2,128)(2,1)}), bf16[4224,2,128]{2,1,0:T(2,128)(2,1)S(1)}, u32[]{:S(2)}, u32[]{:S(2)}) async-start(bf16[4224,2,128]{2,1,0:T(2,128)(2,1)} %bitcast.8), calls=%async_computation | async-start | bytes 4325376 | tf_op jit(solution)/shard_map/all_to_all | solution.py:509
  23.2 25.0 %collective-permute-start = (bf16[128,256]{1,0:T(8,128)(2,1)}, bf16[128,256]{1,0:T(8,128)(2,1)S(1)}, u32[]{:S(2)}, u32[]{:S(2)}) collective-permute-start(bf16[128,256]{1,0:T(8,128)(2,1)} %get-tuple-element.15), channel_id=1, source_target_pairs={{1,0},{2,1},{3,2},{5,4},{6,5},{7,6},{9,8},{10,9},{11,10},{13,12},{... | collective-permute-start | bytes 196616 | tf_op jit(solution)/shard_map/ppermute | solution.py:520
  26.2 22.0 %collective-permute-start.1 = (bf16[128,256]{1,0:T(8,128)(2,1)}, bf16[128,256]{1,0:T(8,128)(2,1)S(1)}, u32[]{:S(2)}, u32[]{:S(2)}) collective-permute-start(bf16[128,256]{1,0:T(8,128)(2,1)} %get-tuple-element.16), channel_id=1, source_target_pairs={{0,1},{1,2},{2,3},{4,5},{5,6},{6,7},{8,9},{9,10},{10,11},{12,13},{... | collective-permute-start | bytes 196616 | tf_op jit(solution)/shard_map/ppermute | solution.py:519
  30.6 17.4 %collective-permute-start.2 = (bf16[16,128]{1,0:T(8,128)(2,1)}, bf16[16,128]{1,0:T(8,128)(2,1)S(1)}, u32[]{:S(2)}, u32[]{:S(2)}) collective-permute-start(bf16[16,128]{1,0:T(8,128)(2,1)} %get-tuple-element.17), channel_id=1, source_target_pairs={{4,0},{8,4},{12,8},{16,12},{20,16},{24,20},{28,24},{32,28},{36,32}... | collective-permute-start | bytes 12296 | tf_op jit(solution)/shard_map/ppermute | solution.py:518
  36.3 11.9 %collective-permute-start.3 = (bf16[16,128]{1,0:T(8,128)(2,1)}, bf16[16,128]{1,0:T(8,128)(2,1)S(1)}, u32[]{:S(2)}, u32[]{:S(2)}) collective-permute-start(bf16[16,128]{1,0:T(8,128)(2,1)} %get-tuple-element.18), channel_id=1, source_target_pairs={{0,4},{4,8},{8,12},{12,16},{16,20},{20,24},{24,28},{28,32},{32,36}... | collective-permute-start | bytes 12296 | tf_op jit(solution)/shard_map/ppermute | solution.py:517
  36.4 1.2 %copy-start = (f32[32,2,16,256]{3,2,1,0:T(8,128)S(1)}, f32[32,2,16,256]{3,2,1,0:T(8,128)}, u32[]{:S(2)}) copy-start(f32[32,2,16,256]{3,2,1,0:T(8,128)} %flow_ref.1) | copy-start | bytes 3145732
  37.6 1.0 %copy-start.2 = (f32[31,16,256]{2,1,0:T(8,128)S(1)}, f32[31,16,256]{2,1,0:T(8,128)}, u32[]{:S(2)}) copy-start(f32[31,16,256]{2,1,0:T(8,128)} %mix_ref.1) | copy-start | bytes 1523716

commit v9 on v7

--- a/solution.py
+++ b/solution.py
@@ -352,7 +352,7 @@
 
 
 GATHER_BLOCKS = 1
-ROW_PARTS = 2
+ROW_PARTS = 4
 
 
 def lane_order(head_f, line_ref, capacity):

time: 62.9 us -> 62.9 us (level)
  no operation moved by 1% of the time
where the time goes in v9:
time: 62.9 us; the launch traced here: 62.5 us
  Pallas kernels  33.2 us (53%)
  starting transfers between devices  24.7 us (39%)
  local copies, waits for them, and re-layouts  2.27 us (4%)
  waiting for transfers between devices  2.09 us (3%)
    pallas_call x1, Pallas kernels, finish(): pl.pallas_call(finish_kernel, out_shape=jax.ShapeDtypeStruct(shape, jnp.f...  12.1 us
    all_to_all x1, starting transfers between devices, per_device(): lax.all_to_all(pairs, ('along', 'cross'), split_axis=0, concat_axis=0, ti...  11.5 us
    pallas_call x1, Pallas kernels, local_part(): pl.pallas_call(local_kernel, out_shape=(jax.ShapeDtypeStruct((LOCAL_PLANE...  9.39 us
    pallas_call x1, Pallas kernels, pack_rows(): pl.pallas_call(functools.partial(pack_kernel, tiles=tiles), out_shape=jax...  7.43 us
    ppermute x1, starting transfers between devices, per_device(): east = lax.ppermute(first_column, 'along', ring_down)  5.76 us
    ppermute x1, starting transfers between devices, per_device(): south = lax.ppermute(last_row, 'cross', line_up)  4.38 us
    pallas_call x1, Pallas kernels, edges(): pl.pallas_call(edge_kernel, out_shape=(row, row, side, side), in_specs=[v...  4.25 us
    ppermute x1, starting transfers between devices, per_device(): north = lax.ppermute(first_row, 'cross', line_down)  3.1 us
  transfers between devices with their start and end apart: 5, of which 2 were waited for; matrix products, arithmetic and copies ran while one was open for 0% of the time, Pallas kernels for 22%

profile of v9, /device:TPU:1, one launch (start us, length us, event | category | flops | bytes accessed | tf_op | source)
XLA Modules:
  0.0 62.5 jit_solution(3614242866777277404)
XLA Ops:
  0.0 7.4 %pack_rows.1 = bf16[8448,128]{1,0:T(8,128)(2,1)} custom-call(s32[32,128]{1,0:T(8,128)} %bitcast.10, s32[32,128]{1,0:T(8,128)} %bitcast.11, bf16[4096,128]{1,0:T(8,128)(2,1)} %rows_hbm.1), custom_call_target="tpu_custom_call" | custom-call | tf_op jit(solution)/shard_map/pack_rows/pallas_call | solution.py:116
  7.4 0.0 copy-start.1
  7.4 11.5 %all-to-all-start = ((bf16[4224,2,128]{2,1,0:T(2,128)(2,1)}), bf16[4224,2,128]{2,1,0:T(2,128)(2,1)S(1)}, u32[]{:S(2)}, u32[]{:S(2)}) async-start(bf16[4224,2,128]{2,1,0:T(2,128)(2,1)} %bitcast.8), calls=%async_computation | async-start | bytes 4325376 | tf_op jit(solution)/shard_map/all_to_all | solution.py:503
  19.0 4.2 %edges.1 = (bf16[128,256]{1,0:T(8,128)(2,1)}, bf16[128,256]{1,0:T(8,128)(2,1)}, bf16[16,128]{1,0:T(8,128)(2,1)}, bf16[16,128]{1,0:T(8,128)(2,1)}) custom-call(f32[128,16,256]{2,1,0:T(8,128)} %bitcast.9), custom_call_target="tpu_custom_call" | custom-call | flops 1000 | bytes 100000 | tf_op jit(solution)/shard_map/edges/pallas_call | solution.py:161
  23.2 0.0 copy-start.3
  23.2 3.1 %collective-permute-start = (bf16[128,256]{1,0:T(8,128)(2,1)}, bf16[128,256]{1,0:T(8,128)(2,1)S(1)}, u32[]{:S(2)}, u32[]{:S(2)}) collective-permute-start(bf16[128,256]{1,0:T(8,128)(2,1)} %get-tuple-element.15), channel_id=1, source_target_pairs={{1,0},{2,1},{3,2},{5,4},{6,5},{7,6},{9,8},{10,9},{11,10},{13,12},{... | collective-permute-start | bytes 196616 | tf_op jit(solution)/shard_map/ppermute | solution.py:514
  26.3 4.4 %collective-permute-start.1 = (bf16[128,256]{1,0:T(8,128)(2,1)}, bf16[128,256]{1,0:T(8,128)(2,1)S(1)}, u32[]{:S(2)}, u32[]{:S(2)}) collective-permute-start(bf16[128,256]{1,0:T(8,128)(2,1)} %get-tuple-element.16), channel_id=1, source_target_pairs={{0,1},{1,2},{2,3},{4,5},{5,6},{6,7},{8,9},{9,10},{10,11},{12,13},{... | collective-permute-start | bytes 196616 | tf_op jit(solution)/shard_map/ppermute | solution.py:513
  30.7 5.8 %collective-permute-start.2 = (bf16[16,128]{1,0:T(8,128)(2,1)}, bf16[16,128]{1,0:T(8,128)(2,1)S(1)}, u32[]{:S(2)}, u32[]{:S(2)}) collective-permute-start(bf16[16,128]{1,0:T(8,128)(2,1)} %get-tuple-element.17), channel_id=1, source_target_pairs={{4,0},{8,4},{12,8},{16,12},{20,16},{24,20},{28,24},{32,28},{36,32}... | collective-permute-start | bytes 12296 | tf_op jit(solution)/shard_map/ppermute | solution.py:512
  36.5 0.0 collective-permute-start.3
  36.5 0.0 copy-done.1
  36.5 0.0 copy-start
  36.5 1.2 %copy-done = f32[32,2,16,256]{3,2,1,0:T(8,128)S(1)} copy-done((f32[32,2,16,256]{3,2,1,0:T(8,128)S(1)}, f32[32,2,16,256]{3,2,1,0:T(8,128)}, u32[]{:S(2)}) %copy-start) | copy-done | bytes 1048600
  37.7 0.0 copy-start.2
  37.7 1.0 %copy-done.2 = f32[31,16,256]{2,1,0:T(8,128)S(1)} copy-done((f32[31,16,256]{2,1,0:T(8,128)S(1)}, f32[31,16,256]{2,1,0:T(8,128)}, u32[]{:S(2)}) %copy-start.2) | copy-done | bytes 507928
  38.7 9.4 %local_part.1 = (f32[1536,16,256]{2,1,0:T(8,128)}, f32[17,16,256]{2,1,0:T(8,128)S(1)}) custom-call(f32[32,4,16,256]{3,2,1,0:T(8,128)} %adj_ref, f32[32,2,16,256]{3,2,1,0:T(8,128)S(1)} %copy-done, s32[32,16,256]{2,1,0:T(8,128)S(1)} %copy-done.1, f32[31,16,256]{2,1,0:T(8,128)S(1)} %copy-done.2), custom_call_target="tpu_custom_call" | custom-call | flops 1000 | bytes 100000 | tf_op jit(solution)/shard_map/local_part/pallas_call | solution.py:283
  48.1 0.0 collective-permute-done.2.east_ref
  48.1 0.1 collective-permute-done.3.west_ref
  48.2 0.0 collective-permute-done.north_ref
  48.2 0.0 collective-permute-done.1.south_ref
  48.2 2.0 %all-to-all-done = bf16[4224,2,128]{2,1,0:T(2,128)(2,1)S(1)} async-done(((bf16[4224,2,128]{2,1,0:T(2,128)(2,1)}), bf16[4224,2,128]{2,1,0:T(2,128)(2,1)S(1)}, u32[]{:S(2)}, u32[]{:S(2)}) %all-to-all-start) | async-done | bytes 2162720 | tf_op jit(solution)/shard_map/all_to_all | solution.py:503
  50.2 0.0 copy-done.3
  50.2 12.1 %finish.1 = f32[32,4,16,256]{3,2,1,0:T(8,128)} custom-call(s32[32]{0:T(128)S(1)} %copy-done.3, bf16[8448,128]{1,0:T(8,128)(2,1)S(1)} %bitcast.6, bf16[128,33,2,128]{3,2,1,0:T(2,128)(2,1)S(1)} %bitcast.7, bf16[128,256]{1,0:T(8,128)(2,1)S(1)} %collective-permute-done.north_ref, bf16[128,256]{1,0:T(8,128)(2,1)S(1)} %collective-permute-done.1.south_ref, ...), custom_call_target="tpu_custom_call" | custom-call | tf_op jit(solution)/shard_map/finish/pallas_call | solution.py:471
Async XLA Ops:
  7.4 29.0 %copy-start.1 = (s32[32,16,256]{2,1,0:T(8,128)S(1)}, s32[32,16,256]{2,1,0:T(8,128)}, u32[]{:S(2)}) copy-start(s32[32,16,256]{2,1,0:T(8,128)} %mask_ref.1) | copy-start | bytes 1572868
  7.4 42.8 %all-to-all-start = ((bf16[4224,2,128]{2,1,0:T(2,128)(2,1)}), bf16[4224,2,128]{2,1,0:T(2,128)(2,1)S(1)}, u32[]{:S(2)}, u32[]{:S(2)}) async-start(bf16[4224,2,128]{2,1,0:T(2,128)(2,1)} %bitcast.8), calls=%async_computation | async-start | bytes 4325376 | tf_op jit(solution)/shard_map/all_to_all | solution.py:503
  23.2 27.0 %copy-start.3 = (s32[32]{0:T(128)S(1)}, s32[32]{0:T(128)}, u32[]{:S(2)}) copy-start(s32[32]{0:T(128)} %seam_ref.1) | copy-start | bytes 388
  23.2 25.0 %collective-permute-start = (bf16[128,256]{1,0:T(8,128)(2,1)}, bf16[128,256]{1,0:T(8,128)(2,1)S(1)}, u32[]{:S(2)}, u32[]{:S(2)}) collective-permute-start(bf16[128,256]{1,0:T(8,128)(2,1)} %get-tuple-element.15), channel_id=1, source_target_pairs={{1,0},{2,1},{3,2},{5,4},{6,5},{7,6},{9,8},{10,9},{11,10},{13,12},{... | collective-permute-start | bytes 196616 | tf_op jit(solution)/shard_map/ppermute | solution.py:514
  26.3 21.9 %collective-permute-start.1 = (bf16[128,256]{1,0:T(8,128)(2,1)}, bf16[128,256]{1,0:T(8,128)(2,1)S(1)}, u32[]{:S(2)}, u32[]{:S(2)}) collective-permute-start(bf16[128,256]{1,0:T(8,128)(2,1)} %get-tuple-element.16), channel_id=1, source_target_pairs={{0,1},{1,2},{2,3},{4,5},{5,6},{6,7},{8,9},{9,10},{10,11},{12,13},{... | collective-permute-start | bytes 196616 | tf_op jit(solution)/shard_map/ppermute | solution.py:513
  30.7 17.4 %collective-permute-start.2 = (bf16[16,128]{1,0:T(8,128)(2,1)}, bf16[16,128]{1,0:T(8,128)(2,1)S(1)}, u32[]{:S(2)}, u32[]{:S(2)}) collective-permute-start(bf16[16,128]{1,0:T(8,128)(2,1)} %get-tuple-element.17), channel_id=1, source_target_pairs={{4,0},{8,4},{12,8},{16,12},{20,16},{24,20},{28,24},{32,28},{36,32}... | collective-permute-start | bytes 12296 | tf_op jit(solution)/shard_map/ppermute | solution.py:512
  36.5 11.7 %collective-permute-start.3 = (bf16[16,128]{1,0:T(8,128)(2,1)}, bf16[16,128]{1,0:T(8,128)(2,1)S(1)}, u32[]{:S(2)}, u32[]{:S(2)}) collective-permute-start(bf16[16,128]{1,0:T(8,128)(2,1)} %get-tuple-element.18), channel_id=1, source_target_pairs={{0,4},{4,8},{8,12},{12,16},{16,20},{20,24},{24,28},{28,32},{32,36}... | collective-permute-start | bytes 12296 | tf_op jit(solution)/shard_map/ppermute | solution.py:511
  36.5 1.2 %copy-start = (f32[32,2,16,256]{3,2,1,0:T(8,128)S(1)}, f32[32,2,16,256]{3,2,1,0:T(8,128)}, u32[]{:S(2)}) copy-start(f32[32,2,16,256]{3,2,1,0:T(8,128)} %flow_ref.1) | copy-start | bytes 3145732
  37.7 1.0 %copy-start.2 = (f32[31,16,256]{2,1,0:T(8,128)S(1)}, f32[31,16,256]{2,1,0:T(8,128)}, u32[]{:S(2)}) copy-start(f32[31,16,256]{2,1,0:T(8,128)} %mix_ref.1) | copy-start | bytes 1523716

commit v10 on v9

--- a/solution.py
+++ b/solution.py
@@ -352,7 +352,7 @@
 
 
 GATHER_BLOCKS = 1
-ROW_PARTS = 4
+ROW_PARTS = 8
 
 
 def lane_order(head_f, line_ref, capacity):

time: 62.9 us -> 62.9 us (level)
  no operation moved by 1% of the time
where the time goes in v10:
time: 62.9 us; the launch traced here: 62.5 us
  Pallas kernels  33.2 us (53%)
  starting transfers between devices  24.7 us (39%)
  local copies, waits for them, and re-layouts  2.27 us (4%)
  waiting for transfers between devices  2.09 us (3%)
    pallas_call x1, Pallas kernels, finish(): pl.pallas_call(finish_kernel, out_shape=jax.ShapeDtypeStruct(shape, jnp.f...  12.1 us
    all_to_all x1, starting transfers between devices, per_device(): lax.all_to_all(pairs, ('along', 'cross'), split_axis=0, concat_axis=0, ti...  11.5 us
    pallas_call x1, Pallas kernels, local_part(): pl.pallas_call(local_kernel, out_shape=(jax.ShapeDtypeStruct((LOCAL_PLANE...  9.39 us
    pallas_call x1, Pallas kernels, pack_rows(): pl.pallas_call(functools.partial(pack_kernel, tiles=tiles), out_shape=jax...  7.43 us
    ppermute x1, starting transfers between devices, per_device(): east = lax.ppermute(first_column, 'along', ring_down)  5.76 us
    ppermute x1, starting transfers between devices, per_device(): south = lax.ppermute(last_row, 'cross', line_up)  4.38 us
    pallas_call x1, Pallas kernels, edges(): pl.pallas_call(edge_kernel, out_shape=(row, row, side, side), in_specs=[v...  4.25 us
    ppermute x1, starting transfers between devices, per_device(): north = lax.ppermute(first_row, 'cross', line_down)  3.1 us
  transfers between devices with their start and end apart: 5, of which 2 were waited for; matrix products, arithmetic and copies ran while one was open for 0% of the time, Pallas kernels for 22%

profile of v10, /device:TPU:1, one launch (start us, length us, event | category | flops | bytes accessed | tf_op | source)
XLA Modules:
  0.0 62.5 jit_solution(8226143652456628377)
XLA Ops:
  0.0 7.4 %pack_rows.1 = bf16[8448,128]{1,0:T(8,128)(2,1)} custom-call(s32[32,128]{1,0:T(8,128)} %bitcast.10, s32[32,128]{1,0:T(8,128)} %bitcast.11, bf16[4096,128]{1,0:T(8,128)(2,1)} %rows_hbm.1), custom_call_target="tpu_custom_call" | custom-call | tf_op jit(solution)/shard_map/pack_rows/pallas_call | solution.py:116
  7.4 0.0 copy-start.1
  7.4 11.5 %all-to-all-start = ((bf16[4224,2,128]{2,1,0:T(2,128)(2,1)}), bf16[4224,2,128]{2,1,0:T(2,128)(2,1)S(1)}, u32[]{:S(2)}, u32[]{:S(2)}) async-start(bf16[4224,2,128]{2,1,0:T(2,128)(2,1)} %bitcast.8), calls=%async_computation | async-start | bytes 4325376 | tf_op jit(solution)/shard_map/all_to_all | solution.py:503
  19.0 4.2 %edges.1 = (bf16[128,256]{1,0:T(8,128)(2,1)}, bf16[128,256]{1,0:T(8,128)(2,1)}, bf16[16,128]{1,0:T(8,128)(2,1)}, bf16[16,128]{1,0:T(8,128)(2,1)}) custom-call(f32[128,16,256]{2,1,0:T(8,128)} %bitcast.9), custom_call_target="tpu_custom_call" | custom-call | flops 1000 | bytes 100000 | tf_op jit(solution)/shard_map/edges/pallas_call | solution.py:161
  23.2 0.0 copy-start.3
  23.2 3.1 %collective-permute-start = (bf16[128,256]{1,0:T(8,128)(2,1)}, bf16[128,256]{1,0:T(8,128)(2,1)S(1)}, u32[]{:S(2)}, u32[]{:S(2)}) collective-permute-start(bf16[128,256]{1,0:T(8,128)(2,1)} %get-tuple-element.15), channel_id=1, source_target_pairs={{1,0},{2,1},{3,2},{5,4},{6,5},{7,6},{9,8},{10,9},{11,10},{13,12},{... | collective-permute-start | bytes 196616 | tf_op jit(solution)/shard_map/ppermute | solution.py:514
  26.3 4.4 %collective-permute-start.1 = (bf16[128,256]{1,0:T(8,128)(2,1)}, bf16[128,256]{1,0:T(8,128)(2,1)S(1)}, u32[]{:S(2)}, u32[]{:S(2)}) collective-permute-start(bf16[128,256]{1,0:T(8,128)(2,1)} %get-tuple-element.16), channel_id=1, source_target_pairs={{0,1},{1,2},{2,3},{4,5},{5,6},{6,7},{8,9},{9,10},{10,11},{12,13},{... | collective-permute-start | bytes 196616 | tf_op jit(solution)/shard_map/ppermute | solution.py:513
  30.7 5.8 %collective-permute-start.2 = (bf16[16,128]{1,0:T(8,128)(2,1)}, bf16[16,128]{1,0:T(8,128)(2,1)S(1)}, u32[]{:S(2)}, u32[]{:S(2)}) collective-permute-start(bf16[16,128]{1,0:T(8,128)(2,1)} %get-tuple-element.17), channel_id=1, source_target_pairs={{4,0},{8,4},{12,8},{16,12},{20,16},{24,20},{28,24},{32,28},{36,32}... | collective-permute-start | bytes 12296 | tf_op jit(solution)/shard_map/ppermute | solution.py:512
  36.5 0.0 collective-permute-start.3
  36.5 0.0 copy-done.1
  36.5 0.0 copy-start
  36.5 1.2 %copy-done = f32[32,2,16,256]{3,2,1,0:T(8,128)S(1)} copy-done((f32[32,2,16,256]{3,2,1,0:T(8,128)S(1)}, f32[32,2,16,256]{3,2,1,0:T(8,128)}, u32[]{:S(2)}) %copy-start) | copy-done | bytes 1048600
  37.7 0.0 copy-start.2
  37.7 1.0 %copy-done.2 = f32[31,16,256]{2,1,0:T(8,128)S(1)} copy-done((f32[31,16,256]{2,1,0:T(8,128)S(1)}, f32[31,16,256]{2,1,0:T(8,128)}, u32[]{:S(2)}) %copy-start.2) | copy-done | bytes 507928
  38.7 9.4 %local_part.1 = (f32[1536,16,256]{2,1,0:T(8,128)}, f32[17,16,256]{2,1,0:T(8,128)S(1)}) custom-call(f32[32,4,16,256]{3,2,1,0:T(8,128)} %adj_ref, f32[32,2,16,256]{3,2,1,0:T(8,128)S(1)} %copy-done, s32[32,16,256]{2,1,0:T(8,128)S(1)} %copy-done.1, f32[31,16,256]{2,1,0:T(8,128)S(1)} %copy-done.2), custom_call_target="tpu_custom_call" | custom-call | flops 1000 | bytes 100000 | tf_op jit(solution)/shard_map/local_part/pallas_call | solution.py:283
  48.1 0.0 collective-permute-done.2.east_ref
  48.1 0.1 collective-permute-done.3.west_ref
  48.2 0.0 collective-permute-done.north_ref
  48.2 0.0 collective-permute-done.1.south_ref
  48.2 2.0 %all-to-all-done = bf16[4224,2,128]{2,1,0:T(2,128)(2,1)S(1)} async-done(((bf16[4224,2,128]{2,1,0:T(2,128)(2,1)}), bf16[4224,2,128]{2,1,0:T(2,128)(2,1)S(1)}, u32[]{:S(2)}, u32[]{:S(2)}) %all-to-all-start) | async-done | bytes 2162720 | tf_op jit(solution)/shard_map/all_to_all | solution.py:503
  50.2 0.0 copy-done.3
  50.2 12.1 %finish.1 = f32[32,4,16,256]{3,2,1,0:T(8,128)} custom-call(s32[32]{0:T(128)S(1)} %copy-done.3, bf16[8448,128]{1,0:T(8,128)(2,1)S(1)} %bitcast.6, bf16[128,33,2,128]{3,2,1,0:T(2,128)(2,1)S(1)} %bitcast.7, bf16[128,256]{1,0:T(8,128)(2,1)S(1)} %collective-permute-done.north_ref, bf16[128,256]{1,0:T(8,128)(2,1)S(1)} %collective-permute-done.1.south_ref, ...), custom_call_target="tpu_custom_call" | custom-call | tf_op jit(solution)/shard_map/finish/pallas_call | solution.py:471
Async XLA Ops:
  7.4 29.0 %copy-start.1 = (s32[32,16,256]{2,1,0:T(8,128)S(1)}, s32[32,16,256]{2,1,0:T(8,128)}, u32[]{:S(2)}) copy-start(s32[32,16,256]{2,1,0:T(8,128)} %mask_ref.1) | copy-start | bytes 1572868
  7.4 42.8 %all-to-all-start = ((bf16[4224,2,128]{2,1,0:T(2,128)(2,1)}), bf16[4224,2,128]{2,1,0:T(2,128)(2,1)S(1)}, u32[]{:S(2)}, u32[]{:S(2)}) async-start(bf16[4224,2,128]{2,1,0:T(2,128)(2,1)} %bitcast.8), calls=%async_computation | async-start | bytes 4325376 | tf_op jit(solution)/shard_map/all_to_all | solution.py:503
  23.2 27.0 %copy-start.3 = (s32[32]{0:T(128)S(1)}, s32[32]{0:T(128)}, u32[]{:S(2)}) copy-start(s32[32]{0:T(128)} %seam_ref.1) | copy-start | bytes 388
  23.2 25.0 %collective-permute-start = (bf16[128,256]{1,0:T(8,128)(2,1)}, bf16[128,256]{1,0:T(8,128)(2,1)S(1)}, u32[]{:S(2)}, u32[]{:S(2)}) collective-permute-start(bf16[128,256]{1,0:T(8,128)(2,1)} %get-tuple-element.15), channel_id=1, source_target_pairs={{1,0},{2,1},{3,2},{5,4},{6,5},{7,6},{9,8},{10,9},{11,10},{13,12},{... | collective-permute-start | bytes 196616 | tf_op jit(solution)/shard_map/ppermute | solution.py:514
  26.3 21.9 %collective-permute-start.1 = (bf16[128,256]{1,0:T(8,128)(2,1)}, bf16[128,256]{1,0:T(8,128)(2,1)S(1)}, u32[]{:S(2)}, u32[]{:S(2)}) collective-permute-start(bf16[128,256]{1,0:T(8,128)(2,1)} %get-tuple-element.16), channel_id=1, source_target_pairs={{0,1},{1,2},{2,3},{4,5},{5,6},{6,7},{8,9},{9,10},{10,11},{12,13},{... | collective-permute-start | bytes 196616 | tf_op jit(solution)/shard_map/ppermute | solution.py:513
  30.7 17.4 %collective-permute-start.2 = (bf16[16,128]{1,0:T(8,128)(2,1)}, bf16[16,128]{1,0:T(8,128)(2,1)S(1)}, u32[]{:S(2)}, u32[]{:S(2)}) collective-permute-start(bf16[16,128]{1,0:T(8,128)(2,1)} %get-tuple-element.17), channel_id=1, source_target_pairs={{4,0},{8,4},{12,8},{16,12},{20,16},{24,20},{28,24},{32,28},{36,32}... | collective-permute-start | bytes 12296 | tf_op jit(solution)/shard_map/ppermute | solution.py:512
  36.5 11.7 %collective-permute-start.3 = (bf16[16,128]{1,0:T(8,128)(2,1)}, bf16[16,128]{1,0:T(8,128)(2,1)S(1)}, u32[]{:S(2)}, u32[]{:S(2)}) collective-permute-start(bf16[16,128]{1,0:T(8,128)(2,1)} %get-tuple-element.18), channel_id=1, source_target_pairs={{0,4},{4,8},{8,12},{12,16},{16,20},{20,24},{24,28},{28,32},{32,36}... | collective-permute-start | bytes 12296 | tf_op jit(solution)/shard_map/ppermute | solution.py:511
  36.5 1.2 %copy-start = (f32[32,2,16,256]{3,2,1,0:T(8,128)S(1)}, f32[32,2,16,256]{3,2,1,0:T(8,128)}, u32[]{:S(2)}) copy-start(f32[32,2,16,256]{3,2,1,0:T(8,128)} %flow_ref.1) | copy-start | bytes 3145732
  37.7 1.0 %copy-start.2 = (f32[31,16,256]{2,1,0:T(8,128)S(1)}, f32[31,16,256]{2,1,0:T(8,128)}, u32[]{:S(2)}) copy-start(f32[31,16,256]{2,1,0:T(8,128)} %mix_ref.1) | copy-start | bytes 1523716
